TPU v7x, 128 devices: a whole 4x4x4 slice. The times are simulated.
128 devices in a mesh: slide: 32 (over y, x, core), row: 4 (over z).
Axes of the slice: x: 4, y: 4, z: 4, core: 2. Of those that a mesh axis runs over, the one named last changes fastest.
Arguments:
- tiles: bfloat16 [32, 4, 64, 16, 768], P('slide', None, 'row'), may hold values from -6 to 6
- cotangent: bfloat16 [32, 4, 64, 16, 768], P('slide', None, 'row'), may hold values from -6 to 6
- tile_counts: int32 [32], P('slide'), may hold values from 1 to 3, as said below
- dw_kernel: float32 [7, 7, 768], replicated, may hold values from -0.875 to 0.875
- ln_gain: float32 [768], replicated, may hold values from 0.5 to 1.5
- fc1_weight: bfloat16 [3072, 768], replicated, may hold values from -0.21875 to 0.21875
- fc2_weight: bfloat16 [768, 3072], replicated, may hold values from -0.109375 to 0.109375
- layer_scale: float32 [768], replicated, may hold values from 0.3 to 1.5
Outputs:
- block_out: bfloat16 [32, 4, 64, 16, 768], P('slide', None, 'row')
- grad_input: float32 [32, 4, 64, 16, 768], P('slide', None, 'row')
- grad_fc1: float32 [3072, 768], P(('slide', 'row'))
- grad_fc2: float32 [768, 3072], P(('slide', 'row'))
- grad_kernel: float32 [7, 7, 768], replicated
- grad_gain: float32 [768], replicated
- grad_scale: float32 [768], replicated
Inputs may be any that keep to these rules, and one draw needn't show every extreme that they name: For s < 16, tile_counts[s] + tile_counts[s + 16] = 4.
All inputs are finite; a program needn't handle non-finite values.
Results may differ from a plain program's by a relative error of at most 0.0062.
Values may be sent and summed in bfloat16 or wider, within the bound.
No kernel may reach another device: no remote copies, remote signals or barrier semaphores. Data moves between devices by JAX's collectives and lax.ppermute only.
A program may use at most 192 MiB of HBM per device.

v0:
```python
import math

import jax
import jax.numpy as jnp
from jax import lax
from jax.sharding import PartitionSpec as P

epsilon = 1e-06
root_half = 1.0 / math.sqrt(2.0)
density = 1.0 / math.sqrt(2.0 * math.pi)


def with_halo(cells, sides, width):
    for axis, dim in sides:
        count = lax.axis_size(axis)
        ends = count - 1
        head = lax.slice_in_dim(cells, 0, width, axis=dim)
        tail = lax.slice_in_dim(cells, cells.shape[dim] - width, cells.shape[dim], axis=dim)
        cells = jnp.concatenate(
            [
                lax.ppermute(tail, axis, [(i, (i + 1) % count) for i in range(ends)]),
                cells,
                lax.ppermute(head, axis, [((i + 1) % count, i) for i in range(ends)]),
            ],
            axis=dim,
        )
    return cells


def shifted(value, axis, by):
    peers = lax.axis_size(axis)
    pairs = [(i, i + by) for i in range(peers) if 0 <= i + by < peers]
    return lax.ppermute(value, axis, pairs)


def gelu_exact(values):
    return 0.5 * values * (1.0 + jax.scipy.special.erf(values * root_half))


def gelu_slope(values):
    return (
        0.5 * (1.0 + jax.scipy.special.erf(values * root_half))
        + values * jnp.exp(-0.5 * values * values) * density
    )


def block_pass(tiles_in, cotan, alive, kernel, gain, first, second, scale):
    slots, rows, cols, chans = tiles_in.shape
    extended = with_halo(tiles_in, (("row", 1),), 3)
    padded = jnp.pad(extended.astype(jnp.float32), ((0, 0), (0, 0), (3, 3), (0, 0)))
    filtered = jnp.zeros((slots, rows, cols, chans), jnp.float32)
    for tap_row in range(7):
        for tap_col in range(7):
            filtered = (
                filtered
                + kernel[tap_row, tap_col]
                * padded[:, tap_row : tap_row + rows, tap_col : tap_col + cols]
            )
    center = filtered - jnp.mean(filtered, axis=-1, keepdims=True)
    inv_std = lax.rsqrt(jnp.mean(center * center, axis=-1, keepdims=True) + epsilon)
    unit = center * inv_std
    normed = (unit * gain).astype(jnp.bfloat16).reshape(-1, chans)
    pre = lax.dot_general(
        normed, first, (((1,), (1,)), ((), ())), preferred_element_type=jnp.float32
    )
    act = gelu_exact(pre).astype(jnp.bfloat16)
    branch = lax.dot_general(
        act, second, (((1,), (1,)), ((), ())), preferred_element_type=jnp.float32
    )
    branch = branch.reshape(slots, rows, cols, chans)
    weight = alive.astype(jnp.float32)[:, None, None, None]
    out = ((tiles_in.astype(jnp.float32) + scale * branch) * weight).astype(jnp.bfloat16)
    held = cotan.astype(jnp.float32) * weight
    scale_grad = jnp.sum(held * branch, axis=(0, 1, 2))
    d_branch = (scale * held).astype(jnp.bfloat16).reshape(-1, chans)
    second_grad = lax.dot_general(
        d_branch, act, (((0,), (0,)), ((), ())), preferred_element_type=jnp.float32
    )
    d_act = jnp.dot(d_branch, second, preferred_element_type=jnp.float32)
    d_pre = (d_act * gelu_slope(pre)).astype(jnp.bfloat16)
    first_grad = lax.dot_general(
        d_pre, normed, (((0,), (0,)), ((), ())), preferred_element_type=jnp.float32
    )
    d_normed = jnp.dot(d_pre, first, preferred_element_type=jnp.float32).reshape(
        slots, rows, cols, chans
    )
    gain_grad = jnp.sum(d_normed * unit, axis=(0, 1, 2))
    scaled = d_normed * gain
    d_filt = inv_std * (
        scaled
        - jnp.mean(scaled, axis=-1, keepdims=True)
        - unit * jnp.mean(scaled * unit, axis=-1, keepdims=True)
    )
    kernel_grad = jnp.stack(
        [
            jnp.stack(
                [
                    jnp.sum(
                        padded[:, tap_row : tap_row + rows, tap_col : tap_col + cols] * d_filt,
                        axis=(0, 1, 2),
                    )
                    for tap_col in range(7)
                ]
            )
            for tap_row in range(7)
        ]
    )
    local = jnp.pad(d_filt, ((0, 0), (6, 6), (3, 3), (0, 0)))
    spread = jnp.zeros((slots, rows + 6, cols, chans), jnp.float32)
    for tap_row in range(7):
        for tap_col in range(7):
            spread = (
                spread
                + kernel[tap_row, tap_col]
                * local[:, 6 - tap_row : 12 - tap_row + rows, 6 - tap_col : 6 - tap_col + cols]
            )
    from_below = shifted(spread[:, :3].astype(jnp.bfloat16), "row", -1).astype(jnp.float32)
    from_above = shifted(spread[:, rows + 3 :].astype(jnp.bfloat16), "row", 1).astype(jnp.float32)
    back = spread[:, 3 : rows + 3]
    back = back.at[:, :3].add(from_above)
    back = back.at[:, rows - 3 :].add(from_below)
    input_grad = held + back
    return (out, input_grad, first_grad, second_grad, kernel_grad, gain_grad, scale_grad)


def body(tiles, cotangent, tile_counts, dw_kernel, ln_gain, fc1_weight, fc2_weight, layer_scale):
    tiles_in = tiles[0]
    cotan_in = cotangent[0]
    slots = tiles_in.shape[0]
    count = tile_counts[0]
    slot_ids = jnp.arange(slots, dtype=jnp.int32)
    results = block_pass(
        tiles_in,
        cotan_in,
        slot_ids < count,
        dw_kernel,
        ln_gain,
        fc1_weight,
        fc2_weight,
        layer_scale,
    )
    block_out = results[0]
    grad_input = results[1]
    first_term = results[2]
    second_term = results[3]
    grad_fc1, grad_fc2 = (
        lax.psum_scatter(first_term, ("slide", "row"), scatter_dimension=0, tiled=True),
        lax.psum_scatter(second_term, ("slide", "row"), scatter_dimension=0, tiled=True),
    )
    grad_kernel, grad_gain, grad_scale = lax.psum(
        (results[4], results[5], results[6]), ("slide", "row")
    )
    return (
        block_out[None],
        grad_input[None],
        grad_fc1,
        grad_fc2,
        grad_kernel,
        grad_gain,
        grad_scale,
    )


def solution(mesh):
    in_specs = (
        P("slide", None, "row", None, None),
        P("slide", None, "row", None, None),
        P("slide"),
        P(),
        P(),
        P(),
        P(),
        P(),
    )
    out_specs = (
        P("slide", None, "row", None, None),
        P("slide", None, "row", None, None),
        P(("slide", "row"), None),
        P(("slide", "row"), None),
        P(),
        P(),
        P(),
    )
    return jax.shard_map(body, mesh=mesh, in_specs=in_specs, out_specs=out_specs, check_vma=False)
```

profile of v0, /device:TPU:1, one launch (start us, length us, event | category | flops | bytes accessed | tf_op | source)
XLA Modules:
  0.0 853.6 jit_solution(16403976032581528221)
XLA Ops:
  9.6 5.0 collective-permute-start
  20.9 3.7 maximum_convert_fusion
  25.0 79.6 %fusion.110 = (f32[4,16,16]{2,1,0:T(8,128)S(1)}, f32[4,16,16,768]{3,2,1,0:T(8,128)S(1)}) fusion(f32[768]{0:T(1024)S(1)} %get-tuple-element.129, f32[768]{0:T(1024)S(1)} %get-tuple-element.130, f32[768]{0:T(1024)S(1)} %get-tuple-element.83, f32[4,22,16,768]{3,2,1,0:T(8,128)} %maximum_convert_fusion, f32[768]{0:T(1024)S(1)} %get-tuple-element.84, ...), kind=kLoop, calls=%fused_computation.329 | loop fusion | flops 77069312 | bytes 29651968 | tf_op jit(solution)/shard_map/reduce_sum | solution.py:59
  105.7 10.7 %multiply_convert_fusion = (bf16[1024,3072]{1,0:T(8,128)(2,1)S(1)}, f32[1024,3072]{1,0:T(8,128)}) fusion(bf16[1024,768]{1,0:T(8,128)(2,1)S(1)} %bitcast.55, bf16[3072,768]{1,0:T(8,128)(2,1)} %param.17), kind=kOutput, calls=%fused_computation.98 | convolution fusion | flops 4847566848 | bytes 25165824 | tf_op jit(solution)/shard_map/dot_general | solution.py:63
  116.5 7.4 multiply_reduce_fusion
  123.9 11.5 %fusion.6 = bf16[1024,3072]{1,0:T(8,128)(2,1)S(1)} fusion(f32[1024,3072]{1,0:T(8,128)} %get-tuple-element.145, bf16[1024,768]{1,0:T(8,128)(2,1)S(1)} %get-tuple-element.141, bf16[768,3072]{1,0:T(8,128)(2,1)S(1)} %bitcast.58), kind=kOutput, calls=%fused_computation.97 | convolution fusion | flops 4863295488 | bytes 25165824 | tf_op jit(solution)/shard_map/dot_general | solution.py:79
  135.5 5.2 multiply_reduce_fusion.52
  144.2 31.3 %multiply_reduce_fusion.2 = (f32[768]{0:T(1024)S(1)}, f32[768]{0:T(1024)S(1)}, f32[768]{0:T(1024)S(1)}, f32[768]{0:T(1024)S(1)}, f32[768]{0:T(1024)S(1)}, /*inde...) fusion(f32[4,22,16,768]{3,2,1,0:T(8,128)} %maximum_convert_fusi, ...), kind=kLoop, calls=%fused_computation.203 | loop fusion | flops 33802752 | bytes 23274496 | tf_op jit(solution)/shard_map/reduce_sum | solution.py:98
  175.6 5.0 multiply_reduce_fusion.38
  180.6 7.8 multiply_reduce_fusion.20
  190.2 10.3 %fusion.113 = f32[3072,768]{1,0:T(8,128)} fusion(bf16[1024,3072]{1,0:T(8,128)(2,1)} %copy-done.82, bf16[1024,768]{1,0:T(8,128)(2,1)S(1)} %bitcast.56), kind=kOutput, calls=%fused_computation.332 | convolution fusion | flops 4831838208 | bytes 17301504 | tf_op jit(solution)/shard_map/dot_general | solution.py:81
  201.9 10.4 %fusion.114 = f32[768,3072]{1,0:T(8,128)} fusion(bf16[1024,768]{1,0:T(8,128)(2,1)S(1)} %copy-done.81, bf16[1024,3072]{1,0:T(8,128)(2,1)} %copy-done.79), kind=kOutput, calls=%fused_computation.333 | convolution fusion | flops 4831838208 | bytes 17301504 | tf_op jit(solution)/shard_map/dot_general | solution.py:76
  212.3 363.4 %fusion = f32[8,3072]{1,0:T(8,128)S(1)} fusion(f32[768,3072]{1,0:T(8,128)} %fusion.114), kind=kCustom, calls=%all-reduce-scatter | all-reduce-scatter fusion | flops 3145729 | bytes 9535488
  579.6 14.9 %collective-permute-start.32 = (f32[8,3072]{1,0:T(8,128)S(1)}, f32[8,3072]{1,0:T(8,128)S(1)}, u32[]{:S(2)}, u32[]{:S(2)}) collective-permute-start(f32[8,3072]{1,0:T(8,128)S(1)} %fusion), channel_id=1, source_target_pairs={{0,29},{1,30},{2,31},{3,32},{4,33},{5,34},{6,35},{7,36},{8,37},{9,... | collective-permute-start | bytes 294920
  602.5 9.6 %collective-permute-start.25 = (f32[8,3072]{1,0:T(8,128)S(1)}, f32[8,3072]{1,0:T(8,128)S(1)}, u32[]{:S(2)}, u32[]{:S(2)}) collective-permute-start(f32[8,3072]{1,0:T(8,128)S(1)} %fusion), channel_id=1, source_target_pairs={{0,22},{1,23},{2,24},{3,25},{4,26},{5,27},{6,28},{7,29},{8,30},{9,... | collective-permute-start | bytes 294920
  612.1 4.0 collective-permute-start.24
  623.2 6.2 collective-permute-start.20
  636.3 6.6 collective-permute-start.16
  647.7 32.0 %fusion.108 = (bf16[4,22,16,768]{3,2,1,0:T(8,128)(2,1)}, f32[4,22,16,768]{3,2,1,0:T(8,128)S(1)}) fusion(f32[768]{0:T(1024)} %copy-done.39, f32[768]{0:T(1024)} %copy-done.40, f32[768]{0:T(1024)} %copy-done.42, f32[768]{0:T(1024)} %copy-done.43, f32[768]{0:T(1024)} %copy-done.44, f32[768]{0:T(1024)} %copy-done.45, f32[768]{0:T(1024)} %copy-done.46, ...), kind=kLoop, calls=%fused_computation.328 | loop fusion | flops 105971712 | bytes 9784320 | tf_op jit(solution)/shard_map/convert.3
  686.9 3.7 collective-permute-start.10
  693.4 3.8 multiply_convert_fusion.2
  705.2 3.8 collective-permute-start.5
  713.5 64.8 %all-reduce.4 = (f32[768]{0:T(1024)}, f32[768]{0:T(1024)}) all-reduce(f32[768]{0:T(1024)S(1)} %copy-done.74, f32[768]{0:T(1024)S(1)} %copy-done.77), channel_id=1, replica_groups=mesh['slide'=32,'row'=4] {'slide','row'}, use_global_device_ids=true, to_apply=%region_57.58 | all-reduce | flops 1536 | bytes 12288 | tf_op jit(solution)/shard_map/psum | solution.py:150
  782.6 56.0 %concatenate.8 = f32[262,3072]{1,0:T(8,128)} concatenate(f32[6,3072]{1,0:T(8,128)} %copy-done.11, f32[8,3072]{1,0:T(8,128)} %copy-done.10, f32[8,3072]{1,0:T(8,128)} %copy-done.12, f32[8,3072]{1,0:T(8,128)} %copy-done.13, f32[8,3072]{1,0:T(8,128)} %copy-done.14, f32[8,3072]{1,0:T(8,128)} %copy-done.15, f32[8,3072]{1,0:T(8,128)} %copy-done.16, f32[8,3072]{1,0:T(8,128)} %copy-done.17, ...), dimensions={0} | concatenate | bytes 6438912
  (337 shorter events, 79.7 us)
Async XLA Ops:
  7.2 837.8 %all-reduce.7.cloned.1.call-start = ((), (), s32[]{:S(2)}) async-start(), calls=%async_computation.2 | async-start | bytes 344064 | tf_op jit(solution)/shard_map/psum | solution.py:150
  190.2 654.8 %reduce-scatter.4.cloned.1.call-start = ((), (), s32[]{:S(2)}) async-start(), calls=%async_computation.1 | async-start | bytes 9510912 | tf_op jit(solution)/shard_map/reduce_scatter | solution.py:147
  575.7 21.5 %collective-permute-start.34 = (f32[8,3072]{1,0:T(8,128)S(1)}, f32[8,3072]{1,0:T(8,128)S(1)}, u32[]{:S(2)}, u32[]{:S(2)}) collective-permute-start(f32[8,3072]{1,0:T(8,128)S(1)} %fusion), channel_id=1, source_target_pairs={{0,31},{1,32},{2,33},{3,34},{4,35},{5,36},{6,37},{7,38},{8,39},{9,... | collective-permute-start | bytes 294920
  577.0 18.8 %collective-permute-start.35 = (f32[6,3072]{1,0:T(8,128)S(1)}, f32[6,3072]{1,0:T(8,128)S(1)}, u32[]{:S(2)}, u32[]{:S(2)}) collective-permute-start(f32[6,3072]{1,0:T(8,128)S(1)} %slice.790), channel_id=1, source_target_pairs={{0,32},{1,33},{2,34},{3,35},{4,36},{5,37},{6,38},{7,39},{8,40},{9,... | collective-permute-start | bytes 221192
  578.3 20.2 %collective-permute-start.33 = (f32[8,3072]{1,0:T(8,128)S(1)}, f32[8,3072]{1,0:T(8,128)S(1)}, u32[]{:S(2)}, u32[]{:S(2)}) collective-permute-start(f32[8,3072]{1,0:T(8,128)S(1)} %fusion), channel_id=1, source_target_pairs={{0,30},{1,31},{2,32},{3,33},{4,34},{5,35},{6,36},{7,37},{8,38},{9,... | collective-permute-start | bytes 294920
  579.6 20.2 %collective-permute-start.32 = (f32[8,3072]{1,0:T(8,128)S(1)}, f32[8,3072]{1,0:T(8,128)S(1)}, u32[]{:S(2)}, u32[]{:S(2)}) collective-permute-start(f32[8,3072]{1,0:T(8,128)S(1)} %fusion), channel_id=1, source_target_pairs={{0,29},{1,30},{2,31},{3,32},{4,33},{5,34},{6,35},{7,36},{8,37},{9,... | collective-permute-start | bytes 294920
  599.8 18.9 %collective-permute-start.27 = (f32[8,3072]{1,0:T(8,128)S(1)}, f32[8,3072]{1,0:T(8,128)S(1)}, u32[]{:S(2)}, u32[]{:S(2)}) collective-permute-start(f32[8,3072]{1,0:T(8,128)S(1)} %fusion), channel_id=1, source_target_pairs={{0,24},{1,25},{2,26},{3,27},{4,28},{5,29},{6,30},{7,31},{8,32},{9,... | collective-permute-start | bytes 294920
  601.2 20.1 %collective-permute-start.26 = (f32[8,3072]{1,0:T(8,128)S(1)}, f32[8,3072]{1,0:T(8,128)S(1)}, u32[]{:S(2)}, u32[]{:S(2)}) collective-permute-start(f32[8,3072]{1,0:T(8,128)S(1)} %fusion), channel_id=1, source_target_pairs={{0,23},{1,24},{2,25},{3,26},{4,27},{5,28},{6,29},{7,30},{8,31},{9,... | collective-permute-start | bytes 294920
  602.5 20.7 %collective-permute-start.25 = (f32[8,3072]{1,0:T(8,128)S(1)}, f32[8,3072]{1,0:T(8,128)S(1)}, u32[]{:S(2)}, u32[]{:S(2)}) collective-permute-start(f32[8,3072]{1,0:T(8,128)S(1)} %fusion), channel_id=1, source_target_pairs={{0,22},{1,23},{2,24},{3,25},{4,26},{5,27},{6,28},{7,29},{8,30},{9,... | collective-permute-start | bytes 294920
  623.2 19.7 %collective-permute-start.20 = (f32[8,3072]{1,0:T(8,128)S(1)}, f32[8,3072]{1,0:T(8,128)}, u32[]{:S(2)}, u32[]{:S(2)}) collective-permute-start(f32[8,3072]{1,0:T(8,128)S(1)} %fusion), channel_id=1, source_target_pairs={{0,17},{1,18},{2,19},{3,20},{4,21},{5,22},{6,23},{7,24},{8,25},{9,... | collective-permute-start | bytes 294920
  631.5 48.2 %collective-permute-start.18 = (f32[8,3072]{1,0:T(8,128)S(1)}, f32[8,3072]{1,0:T(8,128)S(1)}, u32[]{:S(2)}, u32[]{:S(2)}) collective-permute-start(f32[8,3072]{1,0:T(8,128)S(1)} %fusion), channel_id=1, source_target_pairs={{0,15},{1,16},{2,17},{3,18},{4,19},{5,20},{6,21},{7,22},{8,23},{9,... | collective-permute-start | bytes 294920
  633.0 50.0 %collective-permute-start.17 = (f32[8,3072]{1,0:T(8,128)S(1)}, f32[8,3072]{1,0:T(8,128)S(1)}, u32[]{:S(2)}, u32[]{:S(2)}) collective-permute-start(f32[8,3072]{1,0:T(8,128)S(1)} %fusion), channel_id=1, source_target_pairs={{0,14},{1,15},{2,16},{3,17},{4,18},{5,19},{6,20},{7,21},{8,22},{9,... | collective-permute-start | bytes 294920
  636.3 48.0 %collective-permute-start.16 = (f32[8,3072]{1,0:T(8,128)S(1)}, f32[8,3072]{1,0:T(8,128)S(1)}, u32[]{:S(2)}, u32[]{:S(2)}) collective-permute-start(f32[8,3072]{1,0:T(8,128)S(1)} %fusion), channel_id=1, source_target_pairs={{0,13},{1,14},{2,15},{3,16},{4,17},{5,18},{6,19},{7,20},{8,21},{9,... | collective-permute-start | bytes 294920
  642.9 44.0 %collective-permute-start.15 = (f32[8,3072]{1,0:T(8,128)S(1)}, f32[8,3072]{1,0:T(8,128)S(1)}, u32[]{:S(2)}, u32[]{:S(2)}) collective-permute-start(f32[8,3072]{1,0:T(8,128)S(1)} %fusion), channel_id=1, source_target_pairs={{0,12},{1,13},{2,14},{3,15},{4,16},{5,17},{6,18},{7,19},{8,20},{9,... | collective-permute-start | bytes 294920
  644.6 46.0 %collective-permute-start.14 = (f32[8,3072]{1,0:T(8,128)S(1)}, f32[8,3072]{1,0:T(8,128)}, u32[]{:S(2)}, u32[]{:S(2)}) collective-permute-start(f32[8,3072]{1,0:T(8,128)S(1)} %fusion), channel_id=1, source_target_pairs={{0,11},{1,12},{2,13},{3,14},{4,15},{5,16},{6,17},{7,18},{8,19},{9,... | collective-permute-start | bytes 294920
  686.9 18.3 %collective-permute-start.10 = (f32[8,3072]{1,0:T(8,128)S(1)}, f32[8,3072]{1,0:T(8,128)S(1)}, u32[]{:S(2)}, u32[]{:S(2)}) collective-permute-start(f32[8,3072]{1,0:T(8,128)S(1)} %fusion), channel_id=1, source_target_pairs={{0,7},{1,8},{2,9},{3,10},{4,11},{5,12},{6,13},{7,14},{8,15},{9,16}... | collective-permute-start | bytes 294920
  690.6 18.4 %collective-permute-start.9 = (f32[8,3072]{1,0:T(8,128)S(1)}, f32[8,3072]{1,0:T(8,128)S(1)}, u32[]{:S(2)}, u32[]{:S(2)}) collective-permute-start(f32[8,3072]{1,0:T(8,128)S(1)} %fusion), channel_id=1, source_target_pairs={{0,6},{1,7},{2,8},{3,9},{4,10},{5,11},{6,12},{7,13},{8,14},{9,15},... | collective-permute-start | bytes 294920
  697.2 81.1 %collective-permute-start.8 = (f32[8,3072]{1,0:T(8,128)S(1)}, f32[8,3072]{1,0:T(8,128)}, u32[]{:S(2)}, u32[]{:S(2)}) collective-permute-start(f32[8,3072]{1,0:T(8,128)S(1)} %fusion), channel_id=1, source_target_pairs={{0,5},{1,6},{2,7},{3,8},{4,9},{5,10},{6,11},{7,12},{8,13},{9,14},{... | collective-permute-start | bytes 294920
  700.1 81.2 %collective-permute-start.7 = (f32[8,3072]{1,0:T(8,128)S(1)}, f32[8,3072]{1,0:T(8,128)}, u32[]{:S(2)}, u32[]{:S(2)}) collective-permute-start(f32[8,3072]{1,0:T(8,128)S(1)} %fusion), channel_id=1, source_target_pairs={{0,4},{1,5},{2,6},{3,7},{4,8},{5,9},{6,10},{7,11},{8,12},{9,13},{1... | collective-permute-start | bytes 294920
  702.1 80.5 %collective-permute-start.6 = (f32[8,3072]{1,0:T(8,128)S(1)}, f32[8,3072]{1,0:T(8,128)}, u32[]{:S(2)}, u32[]{:S(2)}) collective-permute-start(f32[8,3072]{1,0:T(8,128)S(1)} %fusion), channel_id=1, source_target_pairs={{0,3},{1,4},{2,5},{3,6},{4,7},{5,8},{6,9},{7,10},{8,11},{9,12},{10... | collective-permute-start | bytes 294920
  705.2 77.4 %collective-permute-start.5 = (f32[8,3072]{1,0:T(8,128)S(1)}, f32[8,3072]{1,0:T(8,128)}, u32[]{:S(2)}, u32[]{:S(2)}) collective-permute-start(f32[8,3072]{1,0:T(8,128)S(1)} %fusion), channel_id=1, source_target_pairs={{0,2},{1,3},{2,4},{3,5},{4,6},{5,7},{6,8},{7,9},{8,10},{9,11},{10,... | collective-permute-start | bytes 294920
  709.0 73.6 %collective-permute-start.4 = (f32[8,3072]{1,0:T(8,128)S(1)}, f32[8,3072]{1,0:T(8,128)}, u32[]{:S(2)}, u32[]{:S(2)}) collective-permute-start(f32[8,3072]{1,0:T(8,128)S(1)} %fusion), channel_id=1, source_target_pairs={{0,1},{1,2},{2,3},{3,4},{4,5},{5,6},{6,7},{7,8},{8,9},{9,10},{10,1... | collective-permute-start | bytes 294920
  778.3 62.0 %collective-permute-start.2 = (bf16[4,3,16,768]{3,2,1,0:T(8,128)(2,1)}, bf16[4,3,16,768]{3,2,1,0:T(8,128)(2,1)}, u32[]{:S(2)}, u32[]{:S(2)}) collective-permute-start(bf16[4,3,16,768]{3,2,1,0:T(8,128)(2,1)} %get-tuple-element.139), channel_id=1, source_target_pairs={{0,1},{1,2},{2,3},{4,5},{5,6},{6,7},{8,9},{9,10},{10,11},{12,13},{... | collective-permute-start | bytes 884744 | tf_op jit(solution)/shard_map/ppermute | solution.py:33
  781.3 60.2 %collective-permute-start.3 = (bf16[4,3,16,768]{3,2,1,0:T(8,128)(2,1)S(1)}, bf16[4,3,16,768]{3,2,1,0:T(8,128)(2,1)}, u32[]{:S(2)}, u32[]{:S(2)}) collective-permute-start(bf16[4,3,16,768]{3,2,1,0:T(8,128)(2,1)S(1)} %get-tuple-element.138), channel_id=1, source_target_pairs={{1,0},{2,1},{3,2},{5,4},{6,5},{7,6},{9,8},{10,9},{11,10},{13,12},{... | collective-permute-start | bytes 884744 | tf_op jit(solution)/shard_map/ppermute | solution.py:33
  (103 other events, 1660.6 us)
Sparse Core Ops, SparseCore 0:
  190.3 146.8 all-reduce.6
  343.6 219.6 reduce-scatter.3
where the time goes:
time: 866 us; the launch traced here: 854 us
  blocking collectives  428 us (49%)
  other arithmetic  171 us (20%)
  starting transfers between devices  109 us (13%)
  local copies, waits for them, and re-layouts  73 us (8%)
  matrix products  55.5 us (6%)
  between operations  17.1 us (2%)
    unnamed x1, blocking collectives  363 us
    unnamed x32, starting transfers between devices  98.5 us
    reduce_sum x1, other arithmetic, block_pass(): center = filtered - jnp.mean(filtered, axis=-1, keepdims=True)  79.6 us
    psum x1, blocking collectives, body(): lax.psum((results[4], results[5], results[6]), ('slide', 'row'))  64.8 us
    unnamed x188, local copies, waits for them, and re-layouts  64.6 us
    reduce_sum x3, other arithmetic, block_pass(): jnp.sum(padded[:, tap_row:tap_row + rows, tap_col:tap_col + cols] * d_fil...  44.2 us
    another operation x1, other arithmetic  32 us
  transfers between devices with their start and end apart: 38, of which 0 were waited for; matrix products, arithmetic and copies ran while one was open for 57% of the time, Pallas kernels for 0%

commit v1 on v0

v1 whole, which is shorter than its diff:
```python
import functools
import math

import jax
import jax.numpy as jnp
from jax import lax
from jax.experimental import pallas as pl
from jax.experimental.pallas import tpu as pltpu
from jax.sharding import PartitionSpec as P

epsilon = 1e-06
root_half = 1.0 / math.sqrt(2.0)
density = 1.0 / math.sqrt(2.0 * math.pi)
f32, bf16 = jnp.float32, jnp.bfloat16
REACH = 3
TAPS = 7
LEFT = 8
LANES = 128
MOST = 3
BLOCK = 768
CUT = 256


def same_core_groups():
    slides, rows = lax.axis_size("slide"), lax.axis_size("row")
    return [[s * rows + r for s in range(c, slides, 2) for r in range(rows)] for c in range(2)]


def after(*values):
    return lax.optimization_barrier(values)


def core_halves(term):
    slides = lax.axis_size("slide")
    core = lax.axis_index("slide") % 2
    halves = term.reshape(slides // 2, 2, -1, term.shape[1])
    mine = lax.dynamic_index_in_dim(halves, core, 1, keepdims=False)
    other = lax.dynamic_index_in_dim(halves, 1 - core, 1, keepdims=False)
    return mine, other


def from_other_core(half):
    return lax.ppermute(half, "slide", [(i, i ^ 1) for i in range(lax.axis_size("slide"))])


def exchanged(chip):
    return lax.all_to_all(
        chip.reshape(-1, chip.shape[-1]),
        ("slide", "row"),
        0,
        0,
        axis_index_groups=same_core_groups(),
        tiled=True,
    )


def added(parts):
    peers = lax.axis_size("slide") * lax.axis_size("row") // 2
    return jnp.sum(parts.reshape(peers, -1, parts.shape[-1]).astype(f32), axis=0)


def lane_major(chip):
    peers = lax.axis_size("slide") * lax.axis_size("row") // 2
    cells = chip.reshape(peers, -1, chip.shape[-1] // LANES, LANES)
    return jnp.swapaxes(cells, 1, 2).reshape(peers, -1, LANES)


def with_small(chip, small):
    cells = lane_major(chip)
    peers = cells.shape[0]
    share = -(-small.size // (peers * 8 * LANES)) * 8
    flat = jnp.pad(small.reshape(-1), (0, peers * share * LANES - small.size))
    return jnp.concatenate([cells, flat.astype(bf16).reshape(peers, share, LANES)], axis=1)


def everywhere(share, like):
    slides, rows = lax.axis_size("slide"), lax.axis_size("row")
    sent = jnp.broadcast_to(share[None], (slides * rows, *share.shape))
    got = lax.all_to_all(sent, ("slide", "row"), 0, 0, tiled=True)
    got = jnp.sum(got.reshape(slides // 2, 2, rows, -1), axis=1)
    return got.reshape(-1)[: like.size].reshape(like.shape)


def edges(cells):
    ends = lax.axis_size("row") - 1
    head = cells[:, :REACH]
    tail = cells[:, cells.shape[1] - REACH :]
    above = lax.ppermute(tail, "row", [(i, i + 1) for i in range(ends)])
    below = lax.ppermute(head, "row", [(i + 1, i) for i in range(ends)])
    return above, below


def fill_padded(pad, above_ref, cells_ref, below_ref, rows, cols):
    zeros = jnp.zeros((rows + 2 * REACH, LEFT, pad.shape[2]), f32)
    pad[:, 0:LEFT, :] = zeros
    pad[:, LEFT + cols : 2 * LEFT + cols, :] = zeros
    inner = pl.ds(LEFT, cols)
    pad[0:REACH, inner, :] = above_ref[0].astype(f32)
    pad[REACH : REACH + rows, inner, :] = cells_ref[...].reshape(rows, cols, -1).astype(f32)
    pad[REACH + rows : rows + 2 * REACH, inner, :] = below_ref[0].astype(f32)


def lane_blocks(chans, body):
    def step(i, carry):
        body(pl.ds(pl.multiple_of(i * LANES, LANES), LANES))
        return carry

    lax.fori_loop(0, chans // LANES, step, 0)


def stencil(pad, wide, rows, cols, flip, emit):
    def over(lanes):
        for half in range(cols // 8):
            total = [jnp.zeros((8, LANES), f32) for _ in range(rows)]
            for b in range(TAPS):
                at = pl.ds(LEFT - REACH + b + 8 * half, 8)
                line = [pad[r, at, lanes] for r in range(rows + 2 * REACH)]
                for a in range(TAPS):
                    tap = a * TAPS + b
                    weight = wide[TAPS * TAPS - 1 - tap if flip else tap, :, lanes]
                    for p in range(rows):
                        total[p] = total[p] + weight * line[p + a]
            for p in range(rows):
                emit(p, half, lanes, total[p])

    lane_blocks(pad.shape[2], over)


def spread_kernel(wide, kernel_ref):
    for tap in range(TAPS * TAPS):
        wide[tap] = jnp.broadcast_to(kernel_ref[tap : tap + 1, :], wide.shape[1:])


def forward_kernel(
    count, tiles, above, below, cotan, kernel, gain, scale, normed, unit, spread, held_out, pad, wide, filt
):
    slot = pl.program_id(0)
    rows, cols, chans = tiles.shape[2:]

    @pl.when(slot == 0)
    def _():
        spread_kernel(wide, kernel)

    fill_padded(pad, above, tiles, below, rows, cols)

    def emit(p, half, lanes, value):
        filt[pl.ds(p * cols + 8 * half, 8), lanes] = value

    stencil(pad, wide, rows, cols, False, emit)
    weight = (slot < count[0]).astype(f32)
    held = cotan[...].reshape(rows * cols, chans).astype(f32) * weight
    held_out[...] = (held * scale[...]).astype(bf16)

    def norm(i, carry):
        at = pl.ds(pl.multiple_of(i * 32, 32), 32)
        value = filt[at, :]
        center = value - jnp.mean(value, axis=-1, keepdims=True)
        inv_std = lax.rsqrt(jnp.mean(center * center, axis=-1, keepdims=True) + epsilon)
        one = center * inv_std
        unit[at, :] = one
        normed[at, :] = (one * gain[...]).astype(bf16)
        spread[at, :] = jnp.broadcast_to(inv_std, (32, LANES))
        return carry

    lax.fori_loop(0, rows * cols // 32, norm, 0)


def gelu_parts(pre):
    size = jnp.abs(pre)
    bell = jnp.exp(pre * pre * -0.5)
    t = 1.0 / (1.0 + (0.3275911 * root_half) * size)
    poly = t * (
        0.5 * 0.254829592
        + t * (0.5 * -0.284496736 + t * (0.5 * 1.421413741 + t * (0.5 * -1.453152027 + t * (0.5 * 1.061405429))))
    )
    tail = poly * bell
    return jnp.where(pre < 0.0, tail, 1.0 - tail), bell * density


def hidden_kernel(normed, spread, first, act, slope, term, turned, total):
    step = pl.program_id(0)

    @pl.when(step == 0)
    def _():
        turned[...] = spread[...].T

    for part in range(BLOCK // CUT):
        cut = slice(part * CUT, (part + 1) * CUT)
        pre = lax.dot_general(
            normed[...], first[cut, :], (((1,), (1,)), ((), ())), preferred_element_type=f32
        )
        cdf, pdf = gelu_parts(pre)
        active = (pre * cdf).astype(bf16)
        act[:, cut] = active
        slope[:, cut] = (cdf + pre * pdf).astype(bf16)
        grad = jnp.dot(turned[...], active, preferred_element_type=f32)
        for lane in range(CUT // LANES):
            total[part * (CUT // LANES) + lane, pl.ds(step, grad.shape[0], stride=4), :] = grad[
                :, lane * LANES : (lane + 1) * LANES
            ]

    @pl.when(step == pl.num_programs(0) - 1)
    def _():
        for lane in range(BLOCK // LANES):
            term[:, lane * LANES : (lane + 1) * LANES] = total[lane].astype(bf16)


def back_kernel(
    normed, spread, slope, first, second, unit, inv, gain, term, d_filt, gain_grad, total, d_pre
):
    step = pl.program_id(0)
    pixels, chans = normed.shape
    for part in range(BLOCK // CUT):
        cut = slice(part * CUT, (part + 1) * CUT)
        d_act = jnp.dot(spread[...], second[:, cut], preferred_element_type=f32)
        d_cut = (d_act * slope[:, cut].astype(f32)).astype(bf16)
        d_pre[:, cut] = d_cut
        term[cut, :] = lax.dot_general(
            d_cut, normed[...], (((0,), (0,)), ((), ())), preferred_element_type=f32
        ).astype(bf16)
    d_normed = jnp.dot(d_pre[...], first[...], preferred_element_type=f32)

    @pl.when(step == 0)
    def _():
        total[...] = d_normed

    @pl.when(step > 0)
    def _():
        total[...] += d_normed

    @pl.when(step == pl.num_programs(0) - 1)
    def _():
        def norm(i, kept):
            at = pl.ds(pl.multiple_of(i * 16, 16), 16)
            grad, one = total[at, :], unit[at, :]
            turn = grad * one
            kept = kept + (turn[:8] + turn[8:])
            scaled = grad * gain[...]
            mean = jnp.mean(scaled, axis=-1, keepdims=True)
            along = jnp.mean(scaled * one, axis=-1, keepdims=True)
            d_filt[at, :] = inv[at, 0:1] * (scaled - mean - one * along)
            return kept

        gain_grad[...] = lax.fori_loop(0, pixels // 16, norm, jnp.zeros((8, chans), f32))


def tap_kernel(tiles, above, below, d_filt, grad, pad, total):
    slot = pl.program_id(0)
    rows, cols, chans = tiles.shape[2:]
    fill_padded(pad, above, tiles, below, rows, cols)

    @pl.when(slot == 0)
    def _():
        total[...] = jnp.zeros_like(total)

    def over(lanes):
        for half in range(cols // 8):
            back = [d_filt[pl.ds(p * cols + 8 * half, 8), lanes] for p in range(rows)]
            for b in range(TAPS):
                at = pl.ds(LEFT - REACH + b + 8 * half, 8)
                line = [pad[r, at, lanes] for r in range(rows + 2 * REACH)]
                for a in range(TAPS):
                    acc = line[a] * back[0]
                    for p in range(1, rows):
                        acc = acc + line[p + a] * back[p]
                    total[a * TAPS + b, :, lanes] += acc

    lane_blocks(chans, over)

    @pl.when(slot == pl.num_programs(0) - 1)
    def _():
        for tap in range(TAPS * TAPS):
            grad[tap : tap + 1, :] = jnp.sum(total[tap], axis=0, keepdims=True)


def input_kernel(count, d_filt, above, below, cotan, kernel, out, pad, wide):
    slot = pl.program_id(0)
    rows, cols, chans = out.shape[2:]

    @pl.when(slot == 0)
    def _():
        spread_kernel(wide, kernel)

    @pl.when(slot < MOST)
    def _():
        fill_padded(pad, above, d_filt, below, rows, cols)
        weight = (slot < count[0]).astype(f32)

        def emit(p, half, lanes, value):
            at = pl.ds(8 * half, 8)
            out[0, 0, p, at, lanes] = value + cotan[0, 0, p, at, lanes].astype(f32) * weight

        stencil(pad, wide, rows, cols, True, emit)

    @pl.when(slot >= MOST)
    def _():
        out[...] = jnp.zeros_like(out)


def out_kernel(count, act, second, tiles, cotan, scale, out, scale_grad):
    slot = pl.program_id(0)
    rows, cols, chans = tiles.shape[2:]

    @pl.when(slot == 0)
    def _():
        scale_grad[...] = jnp.zeros_like(scale_grad)

    @pl.when(slot < count[0])
    def _():
        branch = lax.dot_general(
            act[...], second[...], (((1,), (1,)), ((), ())), preferred_element_type=f32
        )
        cells = tiles[...].reshape(rows * cols, chans).astype(f32)
        held = cotan[...].reshape(rows * cols, chans).astype(f32)
        scale_grad[...] += jnp.sum((held * branch).reshape(-1, 8, chans), axis=0)
        out[...] = (cells + scale[...] * branch).astype(bf16).reshape(out.shape)

    @pl.when(slot >= count[0])
    def _():
        out[...] = jnp.zeros_like(out)


def body(tiles, cotangent, tile_counts, dw_kernel, ln_gain, fc1_weight, fc2_weight, layer_scale):
    _, slots, rows, cols, chans = tiles.shape
    hidden = fc1_weight.shape[0]
    pixels = rows * cols
    every = MOST * pixels
    taps = dw_kernel.reshape(TAPS * TAPS, chans)
    gain, scale = ln_gain[None], layer_scale[None]
    above, below = edges(tiles[0, :MOST])

    params = pltpu.CompilerParams(
        vmem_limit_bytes=60 * 1024 * 1024, dimension_semantics=("arbitrary",)
    )
    shape = jax.ShapeDtypeStruct
    brief = pl.CostEstimate(flops=1, bytes_accessed=1, transcendentals=0)
    smem = pl.BlockSpec(memory_space=pltpu.SMEM)
    tile = pl.BlockSpec((1, 1, rows, cols, chans), lambda s: (0, s, 0, 0, 0))
    tile_live = pl.BlockSpec(
        (1, 1, rows, cols, chans), lambda s: (0, jnp.minimum(s, MOST - 1), 0, 0, 0)
    )
    edge = pl.BlockSpec((1, REACH, cols, chans), lambda s: (s, 0, 0, 0))
    edge_live = pl.BlockSpec(
        (1, REACH, cols, chans), lambda s: (jnp.minimum(s, MOST - 1), 0, 0, 0)
    )
    flat = pl.BlockSpec((pixels, chans), lambda s: (s, 0))
    flat_live = pl.BlockSpec((pixels, chans), lambda s: (jnp.minimum(s, MOST - 1), 0))

    def whole(*dims):
        return pl.BlockSpec(dims, lambda s: (0,) * len(dims))

    pad = pltpu.VMEM((rows + 2 * REACH, cols + 2 * LEFT, chans), f32)
    wide = pltpu.VMEM((TAPS * TAPS, 8, chans), f32)

    normed, unit, inv, spread = pl.pallas_call(
        forward_kernel,
        grid=(MOST,),
        in_specs=[smem, tile, edge, edge, tile, whole(TAPS * TAPS, chans), whole(1, chans), whole(1, chans)],
        out_specs=[flat, flat, pl.BlockSpec((pixels, LANES), lambda s: (s, 0)), flat],
        out_shape=[
            shape((every, chans), bf16),
            shape((every, chans), f32),
            shape((every, LANES), f32),
            shape((every, chans), bf16),
        ],
        scratch_shapes=[pad, wide, pltpu.VMEM((pixels, chans), f32)],
        compiler_params=params,
        cost_estimate=brief,
        name="forward",
    )(tile_counts, tiles, above, below, cotangent, taps, gain, scale)

    rows_of = pl.BlockSpec((BLOCK, chans), lambda j: (j, 0))
    cols_of = pl.BlockSpec((chans, BLOCK), lambda j: (0, j))
    wide_of = pl.BlockSpec((every, BLOCK), lambda j: (0, j))
    act, slope, term2 = pl.pallas_call(
        hidden_kernel,
        grid=(hidden // BLOCK,),
        in_specs=[whole(every, chans), whole(every, chans), rows_of],
        out_specs=[wide_of, wide_of, whole(hidden, chans)],
        out_shape=[
            shape((every, hidden), bf16),
            shape((every, hidden), bf16),
            shape((hidden, chans), bf16),
        ],
        scratch_shapes=[pltpu.VMEM((chans, every), bf16), pltpu.VMEM((chans // LANES, hidden, LANES), f32)],
        compiler_params=params,
        cost_estimate=brief,
        name="hidden",
    )(normed, spread, fc1_weight)

    mine2, other2 = core_halves(term2)
    act, other2 = after(act, other2)
    got2 = from_other_core(other2)
    block_out, scale_grad = pl.pallas_call(
        out_kernel,
        grid=(slots,),
        in_specs=[
            smem,
            pl.BlockSpec((pixels, hidden), lambda s: (jnp.minimum(s, MOST - 1), 0)),
            whole(chans, hidden),
            tile_live,
            tile_live,
            whole(1, chans),
        ],
        out_specs=[tile, whole(8, chans)],
        out_shape=[shape(tiles.shape, bf16), shape((8, chans), f32)],
        compiler_params=params,
        cost_estimate=brief,
        name="outs",
    )(tile_counts, act, fc2_weight, tiles, cotangent, scale)

    chip2 = mine2.astype(f32) + got2.astype(f32)
    chip2 = chip2.astype(bf16)
    chip2, slope, block_out = after(chip2, slope, block_out)
    parts2 = exchanged(chip2)

    term1, d_filt, gain_grad = pl.pallas_call(
        back_kernel,
        grid=(hidden // BLOCK,),
        in_specs=[
            whole(every, chans),
            whole(every, chans),
            wide_of,
            rows_of,
            cols_of,
            whole(every, chans),
            whole(every, LANES),
            whole(1, chans),
        ],
        out_specs=[rows_of, whole(every, chans), whole(8, chans)],
        out_shape=[
            shape((hidden, chans), bf16),
            shape((every, chans), f32),
            shape((8, chans), f32),
        ],
        scratch_shapes=[pltpu.VMEM((every, chans), f32), pltpu.VMEM((every, BLOCK), bf16)],
        compiler_params=params,
        cost_estimate=brief,
        name="back",
    )(normed, spread, slope, fc1_weight, fc2_weight, unit, inv, gain)

    mine1, other1 = core_halves(term1)
    d_filt, other1 = after(d_filt, other1)
    got1 = from_other_core(other1)
    d_cells = d_filt.reshape(MOST, rows, cols, chans)
    d_above, d_below = edges(d_cells.astype(bf16))

    tap_grad = pl.pallas_call(
        tap_kernel,
        grid=(MOST,),
        in_specs=[tile, edge, edge, flat],
        out_specs=whole(TAPS * TAPS, chans),
        out_shape=shape((TAPS * TAPS, chans), f32),
        scratch_shapes=[pad, wide],
        compiler_params=params,
        cost_estimate=brief,
        name="taps",
    )(tiles, above, below, d_filt)

    scale_row = jnp.sum(scale_grad, axis=0)
    gain_row = jnp.sum(gain_grad, axis=0)
    small = jnp.concatenate([tap_grad, gain_row[None], scale_row[None]])
    chip1 = with_small(mine1.astype(f32) + got1.astype(f32), small).astype(bf16)
    chip1, parts2 = after(chip1, parts2)
    parts1 = exchanged(chip1)
    d_filt, chip1 = after(d_filt, chip1)

    grad_input = pl.pallas_call(
        input_kernel,
        grid=(slots,),
        in_specs=[smem, flat_live, edge_live, edge_live, tile_live, whole(TAPS * TAPS, chans)],
        out_specs=tile,
        out_shape=shape(tiles.shape, f32),
        scratch_shapes=[pad, wide],
        compiler_params=params,
        cost_estimate=brief,
        name="inputs",
    )(tile_counts, d_filt, d_above, d_below, cotangent, taps)

    grad_fc2 = added(parts2).reshape(-1, hidden)
    sums = added(parts1)
    own = hidden * chans // (LANES * lax.axis_size("slide") * lax.axis_size("row"))
    grad_fc1 = jnp.swapaxes(sums[:own].reshape(chans // LANES, -1, LANES), 0, 1)
    grad_fc1 = grad_fc1.reshape(-1, chans)
    small_share, grad_input = after(sums[own:], grad_input)
    small = everywhere(small_share, small)
    grad_kernel = small[: TAPS * TAPS].reshape(dw_kernel.shape)
    return (
        block_out,
        grad_input,
        grad_fc1,
        grad_fc2,
        grad_kernel,
        small[TAPS * TAPS],
        small[TAPS * TAPS + 1],
    )


def solution(mesh):
    in_specs = (
        P("slide", None, "row", None, None),
        P("slide", None, "row", None, None),
        P("slide"),
        P(),
        P(),
        P(),
        P(),
        P(),
    )
    out_specs = (
        P("slide", None, "row", None, None),
        P("slide", None, "row", None, None),
        P(("slide", "row"), None),
        P(("slide", "row"), None),
        P(),
        P(),
        P(),
    )
    return jax.shard_map(body, mesh=mesh, in_specs=in_specs, out_specs=out_specs, check_vma=False)
```

time: 866 us -> 234 us (0.27); the launches traced: 854 us -> 233 us
  blocking collectives: 428 us -> 0 us
  other arithmetic: 171 us -> 14.6 us
  Pallas kernels: 0 us -> 112 us
  starting transfers between devices: 109 us -> 43.7 us
  matrix products: 55.5 us -> 0 us
  local copies, waits for them, and re-layouts: 73 us -> 20.8 us
  waiting for transfers between devices: 0.13 us -> 40.6 us
  between operations: 17.1 us -> 1.54 us
    unnamed x1 -> x0, blocking collectives: 363 us -> none
    reduce_sum x6 -> x5, other arithmetic: 126 us -> 4.31 us  [the longest x2 4.09 us: added(): jnp.sum(parts.reshape(peers, -1, parts.shape[-1]).astype(f32), axis=0)]
    pallas_call x0 -> x6, Pallas kernels: none -> 112 us  [the longest x1 23.6 us: body(): pl.pallas_call(back_kernel, grid=(hidden // BLOCK,), in_specs=[whole(ever...]
    unnamed x32 -> x0, starting transfers between devices: 98.5 us -> none
    psum x1 -> x0, blocking collectives: 64.8 us -> none  [body(): lax.psum((results[4], results[5], results[6]), ('slide', 'row'))]
    unnamed x188 -> x21, local copies, waits for them, and re-layouts: 64.6 us -> 2.11 us
    dot_general x6 -> x0, matrix products: 55.5 us -> none  [the longest x1 11.5 us: block_pass(): d_act = jnp.dot(d_branch, second, preferred_element_type=jnp.float32)]
    all_to_all x0 -> x3, starting transfers between devices: none -> 30.5 us  [the longest x2 22.2 us: exchanged(): lax.all_to_all(chip.reshape(-1, chip.shape[-1]), ('slide', 'row'), 0, 0,...]
  transfers between devices with their start and end apart: 38 -> 9, of which waited for: 0 -> 4; matrix products, arithmetic and copies ran while one was open for 57% -> 7% of each run, Pallas kernels for 0% -> 19%
where the time goes in v1:
time: 234 us; the launch traced here: 233 us
  Pallas kernels  112 us (48%)
  starting transfers between devices  43.7 us (19%)
  waiting for transfers between devices  40.6 us (17%)
  local copies, waits for them, and re-layouts  20.8 us (9%)
  other arithmetic  14.6 us (6%)
    ppermute x2, waiting for transfers between devices, edges(): below = lax.ppermute(head, 'row', [(i + 1, i) for i in range(ends)])  29.3 us
    pallas_call x1, Pallas kernels, body(): pl.pallas_call(back_kernel, grid=(hidden // BLOCK,), in_specs=[whole(ever...  23.6 us
    pallas_call x1, Pallas kernels, body(): pl.pallas_call(hidden_kernel, grid=(hidden // BLOCK,), in_specs=[whole(ev...  23 us
    all_to_all x2, starting transfers between devices, exchanged(): lax.all_to_all(chip.reshape(-1, chip.shape[-1]), ('slide', 'row'), 0, 0,...  22.2 us
    pallas_call x1, Pallas kernels, body(): pl.pallas_call(forward_kernel, grid=(MOST,), in_specs=[smem, tile, edge,...  21.1 us
    pallas_call x1, Pallas kernels, body(): pl.pallas_call(tap_kernel, grid=(MOST,), in_specs=[tile, edge, edge, flat...  19.6 us
    pallas_call x1, Pallas kernels, body(): pl.pallas_call(input_kernel, grid=(slots,), in_specs=[smem, flat_live, ed...  16 us
    all_to_all x1, waiting for transfers between devices, everywhere(): got = lax.all_to_all(sent, ('slide', 'row'), 0, 0, tiled=True)  10.4 us
  transfers between devices with their start and end apart: 9, of which 4 were waited for; matrix products, arithmetic and copies ran while one was open for 7% of the time, Pallas kernels for 19%

profile of v1, /device:TPU:1, one launch (start us, length us, event | category | flops | bytes accessed | tf_op | source)
XLA Modules:
  0.0 233.3 jit_solution(5793163239057678798)
XLA Ops:
  0.7 1.4 slice_bitcast_fusion
  3.4 5.0 %collective-permute-start = (bf16[3,3,16,768]{3,2,1,0:T(8,128)(2,1)S(1)}, bf16[3,3,16,768]{3,2,1,0:T(8,128)(2,1)S(1)}, u32[]{:S(2)}, u32[]{:S(2)}) collective-permute-start(bf16[3,3,16,768]{3,2,1,0:T(8,128)(2,1)S(1)} %get-tuple-element.58), channel_id=1, source_target_pairs={{0,1},{1,2},{2,3},{4,5},{5,6},{6,7},{8,9},{9,10},{10,11},{12,13},{... | collective-permute-start | bytes 663560 | tf_op jit(solution)/shard_map/ppermute | solution.py:88
  13.1 21.1 %forward.1 = (bf16[768,768]{1,0:T(8,128)(2,1)}, f32[768,768]{1,0:T(8,128)}, f32[768,128]{1,0:T(8,128)}, bf16[768,768]{1,0:T(8,128)(2,1)}) custom-call(s32[1]{0:T(128)S(6)} %copy.32.count, bf16[1,4,16,16,768]{4,3,2,1,0:T(8,128)(2,1)} %tiles.5, bf16[3,3,16,768]{3,2,1,0:T(8,128)(2,1)} %copy-done.2, bf16[3,3,16,768]{3,2,1,0:T(8,128)(2,1)} %copy-done.1, ...), custom_call_target="tpu_custom_call" | custom-call | flops 1 | bytes 1 | tf_op jit(solution)/shard_map/forward/pallas_call | solution.py:355
  34.2 23.0 %hidden.1 = (bf16[768,3072]{1,0:T(8,128)(2,1)}, bf16[768,3072]{1,0:T(8,128)(2,1)}, bf16[3072,768]{1,0:T(8,128)(2,1)}) custom-call(bf16[768,768]{1,0:T(8,128)(2,1)} %get-tuple-element.31.normed, bf16[768,768]{1,0:T(8,128)(2,1)} %get-tuple-element.32.spread, bf16[3072,768]{1,0:T(8,128)(2,1)} %first.3), custom_call_target="tpu_custom_call" | custom-call | flops 1 | bytes 1 | tf_op jit(solution)/shard_map/hidden/pallas_call | solution.py:375
  57.2 3.2 %dynamic-slice_bitcast_fusion.1 = bf16[16,96,768]{2,1,0:T(8,128)(2,1)} fusion(bf16[16,2,96,768]{3,2,1,0:T(8,128)(2,1)} %bitcast.38, s32[]{:T(128)S(6)} %select_n.20), kind=kLoop, calls=%fused_computation.8 | loop fusion | bytes 4718596 | tf_op jit(solution)/shard_map/jit(dynamic_index_in_dim)/squeeze | solution.py:38
  60.4 1.6 collective-permute-start.2
  62.0 8.8 %outs.1 = (bf16[1,4,16,16,768]{4,3,2,1,0:T(8,128)(2,1)}, f32[8,768]{1,0:T(8,128)}) custom-call(s32[1]{0:T(128)S(6)} %copy.32.count, bf16[768,3072]{1,0:T(8,128)(2,1)} %get-tuple-element.37.act, bf16[768,3072]{1,0:T(8,128)(2,1)} %second.3, bf16[1,4,16,16,768]{4,3,2,1,0:T(8,128)(2,1)} %tiles.5, bf16[1,4,16,16,768]{4,3,2,1,0:T(8,128)(2,1)} %cotan.5, ...), custom_call_target="tpu_custom_call" | custom-call | flops 1 | bytes 1 | tf_op jit(solution)/shard_map/outs/pallas_call | solution.py:394
  70.8 3.8 %fusion.1 = bf16[16,96,768]{2,1,0:T(8,128)(2,1)} fusion(bf16[16,96,768]{2,1,0:T(8,128)(2,1)S(1)} %collective-permute-done.2, bf16[16,2,96,768]{3,2,1,0:T(8,128)(2,1)} %bitcast.39, s32[]{:T(128)S(6)} %select_n.19), kind=kLoop, calls=%fused_computation.5 | loop fusion | flops 4718592 | bytes 7077892 | tf_op jit(solution)/shard_map/convert_element_type | solution.py:413
  74.5 23.6 %back.1 = (bf16[3072,768]{1,0:T(8,128)(2,1)}, f32[768,768]{1,0:T(8,128)}, f32[8,768]{1,0:T(8,128)}) custom-call(bf16[768,768]{1,0:T(8,128)(2,1)} %get-tuple-element.31.normed, bf16[768,768]{1,0:T(8,128)(2,1)} %get-tuple-element.32.spread, bf16[768,3072]{1,0:T(8,128)(2,1)} %get-tuple-element.40.slope, bf16[3072,768]{1,0:T(8,128)(2,1)} %first.3, ...), custom_call_target="tpu_custom_call" | custom-call | flops 1 | bytes 1 | tf_op jit(solution)/shard_map/back/pallas_call | solution.py:417
  98.2 3.2 %dynamic-slice_bitcast_fusion = bf16[16,96,768]{2,1,0:T(8,128)(2,1)} fusion(bf16[16,2,96,768]{3,2,1,0:T(8,128)(2,1)} %bitcast.36, s32[]{:T(128)S(6)} %select_n.20), kind=kLoop, calls=%fused_computation.7 | loop fusion | bytes 4718596 | tf_op jit(solution)/shard_map/jit(dynamic_index_in_dim)/squeeze | solution.py:38
  101.4 12.2 %all-to-all-start = ((bf16[64,24,768]{2,1,0:T(8,128)(2,1)}), bf16[64,24,768]{2,1,0:T(8,128)(2,1)}, u32[]{:S(2)}, u32[]{:S(2)}) async-start(bf16[64,24,768]{2,1,0:T(8,128)(2,1)} %bitcast.10), calls=%async_computation | async-start | bytes 4718592 | tf_op jit(solution)/shard_map/all_to_all | solution.py:47
  113.7 19.6 %taps.1 = f32[49,768]{1,0:T(8,128)} custom-call(bf16[1,4,16,16,768]{4,3,2,1,0:T(8,128)(2,1)} %tiles.5, bf16[3,3,16,768]{3,2,1,0:T(8,128)(2,1)} %copy-done.2, bf16[3,3,16,768]{3,2,1,0:T(8,128)(2,1)} %copy-done.1, f32[768,768]{1,0:T(8,128)} %get-tuple-element.51.d_filt), custom_call_target="tpu_custom_call" | custom-call | flops 1 | bytes 1 | tf_op jit(solution)/shard_map/taps/pallas_call | solution.py:448
  134.4 3.8 %fusion = bf16[16,96,768]{2,1,0:T(8,128)(2,1)} fusion(bf16[16,96,768]{2,1,0:T(8,128)(2,1)S(1)} %collective-permute-done.3, bf16[16,2,96,768]{3,2,1,0:T(8,128)(2,1)} %bitcast.37, s32[]{:T(128)S(6)} %select_n.19), kind=kLoop, calls=%fused_computation.3 | loop fusion | flops 4718592 | bytes 7077892 | tf_op jit(solution)/shard_map/convert.8
  138.1 4.8 %reshape.86 = bf16[64,24,6,128]{3,2,1,0:T(8,128)(2,1)S(1)} reshape(bf16[16,96,768]{2,1,0:T(8,128)(2,1)} %fusion) | data formatting | bytes 4718592 | tf_op jit(solution)/shard_map/reshape | solution.py:64
  143.3 1.7 pad_maximum_fusion
  145.0 10.1 %all-to-all-start.1 = ((bf16[64,152,128]{2,1,0:T(8,128)(2,1)}), bf16[64,152,128]{2,1,0:T(8,128)(2,1)}, u32[]{:S(2)}, u32[]{:S(2)}) async-start(bf16[64,152,128]{2,1,0:T(8,128)(2,1)} %pad_maximum_fusion), calls=%async_computation.1 | async-start | bytes 4980736 | tf_op jit(solution)/shard_map/all_to_all | solution.py:47
  155.3 1.3 collective-permute-start.5
  156.6 4.0 %collective-permute-start.4 = (bf16[3,3,16,768]{3,2,1,0:T(8,128)(2,1)S(1)}, bf16[3,3,16,768]{3,2,1,0:T(8,128)(2,1)S(1)}, u32[]{:S(2)}, u32[]{:S(2)}) collective-permute-start(bf16[3,3,16,768]{3,2,1,0:T(8,128)(2,1)S(1)} %get-tuple-element.56), channel_id=1, source_target_pairs={{0,1},{1,2},{2,3},{4,5},{5,6},{6,7},{8,9},{9,10},{10,11},{12,13},{... | collective-permute-start | bytes 663560 | tf_op jit(solution)/shard_map/ppermute | solution.py:88
  160.6 28.6 %collective-permute-done.5.below = bf16[3,3,16,768]{3,2,1,0:T(8,128)(2,1)S(1)} collective-permute-done((bf16[3,3,16,768]{3,2,1,0:T(8,128)(2,1)S(1)}, bf16[3,3,16,768]{3,2,1,0:T(8,128)(2,1)S(1)}, u32[]{:S(2)}, u32[]{:S(2)}) %collective-permute-start.5) | collective-permute-done | bytes 221216 | tf_op jit(solution)/shard_map/ppermute | solution.py:89
  190.6 16.0 %inputs.1 = f32[1,4,16,16,768]{4,3,2,1,0:T(8,128)} custom-call(s32[1]{0:T(128)S(6)} %copy.32.count, f32[768,768]{1,0:T(8,128)} %get-tuple-element.51.d_filt, bf16[3,3,16,768]{3,2,1,0:T(8,128)(2,1)} %copy-done.4, bf16[3,3,16,768]{3,2,1,0:T(8,128)(2,1)} %copy-done.3, bf16[1,4,16,16,768]{4,3,2,1,0:T(8,128)(2,1)} %cotan.5, f32[49,768]{1,0:T(8,128)} %reshape.83.kernel), custom_call_target="tpu_custom_call" | custom-call | flops 1 | bytes 1 | tf_op jit(solution)/shard_map/inputs/pallas_call | solution.py:468
  206.6 2.1 convert_reduce_fusion
  209.5 8.3 %all-to-all-start.2 = ((f32[128,8,128]{2,1,0:T(8,128)}), f32[128,8,128]{2,1,0:T(8,128)S(1)}, u32[]{:S(2)}, u32[]{:S(2)}) async-start(f32[128,8,128]{2,1,0:T(8,128)} %broadcast_in_dim.24), calls=%async_computation.2 | async-start | bytes 1048576 | tf_op jit(solution)/shard_map/all_to_all | solution.py:79
  217.8 2.0 convert_reduce_fusion.1
  221.1 10.4 %all-to-all-done.2 = f32[128,8,128]{2,1,0:T(8,128)S(1)} async-done(((f32[128,8,128]{2,1,0:T(8,128)}), f32[128,8,128]{2,1,0:T(8,128)S(1)}, u32[]{:S(2)}, u32[]{:S(2)}) %all-to-all-start.2) | async-done | bytes 524320 | tf_op jit(solution)/shard_map/all_to_all | solution.py:79
  (55 shorter events, 12.3 us)
Async XLA Ops:
  0.6 8.4 %copy-start.8 = (f32[768]{0:T(1024)S(1)}, f32[768]{0:T(1024)}, u32[]{:S(2)}) copy-start(f32[768]{0:T(1024)} %param.12) | copy-start | bytes 9220
  0.6 9.0 %copy-start.9 = (f32[768]{0:T(1024)S(1)}, f32[768]{0:T(1024)}, u32[]{:S(2)}) copy-start(f32[768]{0:T(1024)} %param.15) | copy-start | bytes 9220
  0.7 9.6 %copy-start.5 = (f32[7,7,768]{2,1,0:T(8,128)S(1)}, f32[7,7,768]{2,1,0:T(8,128)}, u32[]{:S(2)}) copy-start(f32[7,7,768]{2,1,0:T(8,128)} %param.11) | copy-start | bytes 451588
  2.1 9.5 %collective-permute-start.1 = (bf16[3,3,16,768]{3,2,1,0:T(8,128)(2,1)S(1)}, bf16[3,3,16,768]{3,2,1,0:T(8,128)(2,1)S(1)}, u32[]{:S(2)}, u32[]{:S(2)}) collective-permute-start(bf16[3,3,16,768]{3,2,1,0:T(8,128)(2,1)S(1)} %get-tuple-element.57), channel_id=1, source_target_pairs={{1,0},{2,1},{3,2},{5,4},{6,5},{7,6},{9,8},{10,9},{11,10},{13,12},{... | collective-permute-start | bytes 663560 | tf_op jit(solution)/shard_map/ppermute | solution.py:89
  3.4 9.1 %collective-permute-start = (bf16[3,3,16,768]{3,2,1,0:T(8,128)(2,1)S(1)}, bf16[3,3,16,768]{3,2,1,0:T(8,128)(2,1)S(1)}, u32[]{:S(2)}, u32[]{:S(2)}) collective-permute-start(bf16[3,3,16,768]{3,2,1,0:T(8,128)(2,1)S(1)} %get-tuple-element.58), channel_id=1, source_target_pairs={{0,1},{1,2},{2,3},{4,5},{5,6},{6,7},{8,9},{9,10},{10,11},{12,13},{... | collective-permute-start | bytes 663560 | tf_op jit(solution)/shard_map/ppermute | solution.py:88
  11.6 0.9 copy-start.1
  12.5 0.7 copy-start.2
  60.4 10.4 %collective-permute-start.2 = (bf16[16,96,768]{2,1,0:T(8,128)(2,1)}, bf16[16,96,768]{2,1,0:T(8,128)(2,1)S(1)}, u32[]{:S(2)}, u32[]{:S(2)}) collective-permute-start(bf16[16,96,768]{2,1,0:T(8,128)(2,1)} %dynamic-slice_bitcast_fusion.1), channel_id=1, source_target_pairs={{0,4},{4,0},{8,12},{12,8},{16,20},{20,16},{24,28},{28,24},{32,36},... | collective-permute-start | bytes 7077896 | tf_op jit(solution)/shard_map/ppermute | solution.py:43
  101.4 32.9 %collective-permute-start.3 = (bf16[16,96,768]{2,1,0:T(8,128)(2,1)}, bf16[16,96,768]{2,1,0:T(8,128)(2,1)S(1)}, u32[]{:S(2)}, u32[]{:S(2)}) collective-permute-start(bf16[16,96,768]{2,1,0:T(8,128)(2,1)} %dynamic-slice_bitcast_fusion), channel_id=1, source_target_pairs={{0,4},{4,0},{8,12},{12,8},{16,20},{20,16},{24,28},{28,24},{32,36},... | collective-permute-start | bytes 7077896 | tf_op jit(solution)/shard_map/ppermute | solution.py:43
  101.4 12.2 %copy-start.6 = (f32[8,768]{1,0:T(8,128)S(1)}, f32[8,768]{1,0:T(8,128)}, u32[]{:S(2)}) copy-start(f32[8,768]{1,0:T(8,128)} %get-tuple-element.48) | copy-start | bytes 73732
  101.4 43.6 %all-to-all-start = ((bf16[64,24,768]{2,1,0:T(8,128)(2,1)}), bf16[64,24,768]{2,1,0:T(8,128)(2,1)}, u32[]{:S(2)}, u32[]{:S(2)}) async-start(bf16[64,24,768]{2,1,0:T(8,128)(2,1)} %bitcast.10), calls=%async_computation | async-start | bytes 4718592 | tf_op jit(solution)/shard_map/all_to_all | solution.py:47
  113.6 19.6 %copy-start.7 = (f32[8,768]{1,0:T(8,128)S(1)}, f32[8,768]{1,0:T(8,128)}, u32[]{:S(2)}) copy-start(f32[8,768]{1,0:T(8,128)} %get-tuple-element.47) | copy-start | bytes 73732
  145.0 10.1 %copy-start = (f32[768,768]{1,0:T(8,128)S(1)}, f32[768,768]{1,0:T(8,128)}, u32[]{:S(2)}) copy-start(f32[768,768]{1,0:T(8,128)} %get-tuple-element.51.d_filt) | copy-start | bytes 7077892
  145.0 61.6 %all-to-all-start.1 = ((bf16[64,152,128]{2,1,0:T(8,128)(2,1)}), bf16[64,152,128]{2,1,0:T(8,128)(2,1)}, u32[]{:S(2)}, u32[]{:S(2)}) async-start(bf16[64,152,128]{2,1,0:T(8,128)(2,1)} %pad_maximum_fusion), calls=%async_computation.1 | async-start | bytes 4980736 | tf_op jit(solution)/shard_map/all_to_all | solution.py:47
  155.3 33.9 %collective-permute-start.5 = (bf16[3,3,16,768]{3,2,1,0:T(8,128)(2,1)S(1)}, bf16[3,3,16,768]{3,2,1,0:T(8,128)(2,1)S(1)}, u32[]{:S(2)}, u32[]{:S(2)}) collective-permute-start(bf16[3,3,16,768]{3,2,1,0:T(8,128)(2,1)S(1)} %get-tuple-element.55), channel_id=1, source_target_pairs={{1,0},{2,1},{3,2},{5,4},{6,5},{7,6},{9,8},{10,9},{11,10},{13,12},{... | collective-permute-start | bytes 663560 | tf_op jit(solution)/shard_map/ppermute | solution.py:89
  156.6 32.6 %collective-permute-start.4 = (bf16[3,3,16,768]{3,2,1,0:T(8,128)(2,1)S(1)}, bf16[3,3,16,768]{3,2,1,0:T(8,128)(2,1)S(1)}, u32[]{:S(2)}, u32[]{:S(2)}) collective-permute-start(bf16[3,3,16,768]{3,2,1,0:T(8,128)(2,1)S(1)} %get-tuple-element.56), channel_id=1, source_target_pairs={{0,1},{1,2},{2,3},{4,5},{5,6},{6,7},{8,9},{9,10},{10,11},{12,13},{... | collective-permute-start | bytes 663560 | tf_op jit(solution)/shard_map/ppermute | solution.py:88
  189.2 0.7 copy-start.3
  189.9 0.7 copy-start.4
  209.5 22.1 %all-to-all-start.2 = ((f32[128,8,128]{2,1,0:T(8,128)}), f32[128,8,128]{2,1,0:T(8,128)S(1)}, u32[]{:S(2)}, u32[]{:S(2)}) async-start(f32[128,8,128]{2,1,0:T(8,128)} %broadcast_in_dim.24), calls=%async_computation.2 | async-start | bytes 1048576 | tf_op jit(solution)/shard_map/all_to_all | solution.py:79

commit v2 on v1

v2 whole, which is shorter than its diff:
```python
import itertools
import math

import jax
import jax.numpy as jnp
from jax import lax
from jax.experimental import pallas as pl
from jax.experimental.pallas import tpu as pltpu
from jax.sharding import PartitionSpec as P

epsilon = 1e-06
root_half = 1.0 / math.sqrt(2.0)
density = 1.0 / math.sqrt(2.0 * math.pi)
f32, bf16 = jnp.float32, jnp.bfloat16
REACH = 3
TAPS = 7
LEFT = 8
LANES = 128
MOST = 3
BLOCK = 768
SIDE = 4
PITCH = 24


def place(y, x, core, z):
    return ((y * SIDE + x) * 2 + core) * SIDE + z


def after(*values):
    return lax.optimization_barrier(values)


def from_other_core(half):
    return lax.ppermute(half, "slide", [(i, i ^ 1) for i in range(lax.axis_size("slide"))])


def quarters(mine, got):
    core = lax.axis_index("slide") % 2
    own = jnp.where(core == 0, lax.axis_index("row"), lax.axis_index("slide") // 2 % SIDE)

    def cut(half, by):
        cells = half.reshape(SIDE, SIDE, SIDE, -1, half.shape[-1])
        at = (own + by) % SIDE
        along_z = lax.dynamic_index_in_dim(cells, at, 2, keepdims=False)
        along_x = lax.dynamic_index_in_dim(cells, at, 1, keepdims=False)
        return jnp.where(core == 0, along_z, along_x).astype(f32)

    return [(cut(mine, by) + cut(got, by)).astype(bf16) for by in range(SIDE)]


def ring_sent(parts):
    every = [range(SIDE)] * 3
    pairs = [
        [
            move
            for y, x, z in itertools.product(*every)
            for move in (
                (place(y, x, 0, z), place(y, x, 0, (z + by) % SIDE)),
                (place(y, x, 1, z), place(y, (x + by) % SIDE, 1, z)),
            )
        ]
        for by in range(SIDE)
    ]
    return [lax.ppermute(parts[by], ("slide", "row"), pairs[by]) for by in range(1, SIDE)]


def total_of(own, got):
    total = own.astype(f32)
    for part in got:
        total = total + part.astype(f32)
    return total.astype(bf16).reshape(SIDE * SIDE, -1, own.shape[-1])


def plane_exchanged(blocks):
    every = [range(SIDE)] * 2
    groups = [[place(y, x, 0, z) for y, x in itertools.product(*every)] for z in range(SIDE)]
    groups += [[place(y, x, 1, z) for y, z in itertools.product(*every)] for x in range(SIDE)]
    got = lax.all_to_all(
        blocks.reshape(-1, blocks.shape[-1]),
        ("slide", "row"),
        0,
        0,
        axis_index_groups=groups,
        tiled=True,
    )
    return jnp.sum(got.reshape(blocks.shape).astype(f32), axis=0)


def everywhere(share):
    count = lax.axis_size("slide") * lax.axis_size("row")
    cells = share.astype(bf16).reshape(-1, LANES)
    sent = jnp.broadcast_to(cells[None], (count, *cells.shape))
    got = lax.all_to_all(sent, ("slide", "row"), 0, 0, tiled=True)
    got = got.reshape(SIDE, SIDE, 2, SIDE, *cells.shape).astype(f32)
    whole = jnp.sum(got[:, :, 0], axis=2) + jnp.sum(got[:, :, 1], axis=1)
    return whole.reshape(-1, share.shape[-1])


def edges(cells):
    ends = lax.axis_size("row") - 1
    head = cells[:, :REACH]
    tail = cells[:, cells.shape[1] - REACH :]
    above = lax.ppermute(tail, "row", [(i, i + 1) for i in range(ends)])
    below = lax.ppermute(head, "row", [(i + 1, i) for i in range(ends)])
    return above, below


def clear_padded(pad):
    pad[...] = jnp.zeros_like(pad)


def lane_blocks(chans, body):
    def step(i, carry):
        body(i, pl.ds(pl.multiple_of(i * LANES, LANES), LANES))
        return carry

    lax.fori_loop(0, chans // LANES, step, 0)


def fill_padded(pad, above, line_of, below, rows, cols, chans):
    def over(i, lanes):
        for r in range(REACH):
            pad[i, pl.ds(r * PITCH + LEFT, cols), :] = above[0, r, :, lanes].astype(f32)
            at = (rows + REACH + r) * PITCH + LEFT
            pad[i, pl.ds(at, cols), :] = below[0, r, :, lanes].astype(f32)
        for r in range(rows):
            pad[i, pl.ds((REACH + r) * PITCH + LEFT, cols), :] = line_of(r, lanes).astype(f32)

    lane_blocks(chans, over)


def window(pad, i, half, b, rows):
    shift = LEFT - REACH + b + 8 * half
    return [pad[i, pl.ds(r * PITCH + shift, 8), :] for r in range(rows + 2 * REACH)]


def stencil(pad, wide, rows, cols, chans, flip, emit):
    def over(i, lanes):
        for half in range(cols // 8):
            total = [None] * rows
            for b in range(TAPS):
                line = window(pad, i, half, b, rows)
                weights = []
                for a in range(TAPS):
                    tap = a * TAPS + b
                    weights.append(wide[TAPS * TAPS - 1 - tap if flip else tap, :, lanes])
                for p in range(rows):
                    m = [weights[a] * line[p + a] for a in range(TAPS)]
                    part = ((m[0] + m[1]) + (m[2] + m[3])) + ((m[4] + m[5]) + m[6])
                    total[p] = part if total[p] is None else total[p] + part
            for p in range(rows):
                emit(p, half, lanes, total[p])

    lane_blocks(chans, over)


def spread_kernel(wide, kernel_ref):
    for tap in range(TAPS * TAPS):
        wide[tap] = jnp.broadcast_to(kernel_ref[tap : tap + 1, :], wide.shape[1:])


def forward_kernel(
    count, tiles, above, below, cotan, kernel, gain, scale, normed, unit, spread, held_out, pad, wide, filt
):
    slot = pl.program_id(0)
    rows, cols, chans = tiles.shape[2:]

    @pl.when(slot == 0)
    def _():
        spread_kernel(wide, kernel)
        clear_padded(pad)

    def line_of(r, lanes):
        return tiles[0, 0, r, :, lanes]

    fill_padded(pad, above, line_of, below, rows, cols, chans)

    def emit(p, half, lanes, value):
        filt[pl.ds(p * cols + 8 * half, 8), lanes] = value

    stencil(pad, wide, rows, cols, chans, False, emit)
    weight = (slot < count[0]).astype(f32)
    held = cotan[...].reshape(rows * cols, chans).astype(f32) * weight
    held_out[...] = (held * scale[...]).astype(bf16)

    def norm(i, carry):
        at = pl.ds(pl.multiple_of(i * 64, 64), 64)
        value = filt[at, :]
        center = value - jnp.mean(value, axis=-1, keepdims=True)
        inv_std = lax.rsqrt(jnp.mean(center * center, axis=-1, keepdims=True) + epsilon)
        one = center * inv_std
        unit[at, :] = one
        normed[at, :] = (one * gain[...]).astype(bf16)
        spread[at, :] = jnp.broadcast_to(inv_std, (64, LANES))
        return carry

    lax.fori_loop(0, rows * cols // 64, norm, 0)


def gelu_parts(pre):
    size = jnp.abs(pre)
    bell = jnp.exp(pre * pre * -0.5)
    t = 1.0 / (1.0 + (0.3275911 * root_half) * size)
    poly = t * (
        0.5 * 0.254829592
        + t * (0.5 * -0.284496736 + t * (0.5 * 1.421413741 + t * (0.5 * -1.453152027 + t * (0.5 * 1.061405429))))
    )
    tail = poly * bell
    return jnp.where(pre < 0.0, tail, 1.0 - tail), bell * density


def hidden_kernel(core, normed, spread, first, act, slope, mine, other, turned, total):
    step = pl.program_id(0)

    @pl.when(step == 0)
    def _():
        turned[...] = spread[...].T

    pre = lax.dot_general(
        normed[...], first[...], (((1,), (1,)), ((), ())), preferred_element_type=f32
    )
    cdf, pdf = gelu_parts(pre)
    active = (pre * cdf).astype(bf16)
    act[...] = active
    slope[...] = (cdf + pre * pdf).astype(bf16)
    grad = jnp.dot(turned[...], active, preferred_element_type=f32)
    for i in range(BLOCK // LANES):
        total[i, pl.ds(step, grad.shape[0], stride=4), :] = grad[:, i * LANES : (i + 1) * LANES]

    @pl.when(step == pl.num_programs(0) - 1)
    def _():
        count = mine.shape[1]
        for chip in range(mine.shape[0]):
            for half, which in ((mine, core[0]), (other, 1 - core[0])):
                at = pl.ds(pl.multiple_of((2 * chip + which) * count, 32), count)
                for i in range(BLOCK // LANES):
                    half[chip, :, i * LANES : (i + 1) * LANES] = total[i, at, :].astype(bf16)


def back_kernel(
    core, normed, spread, slope, first, second, unit, inv, gain, mine, other, d_filt, gain_grad, total, term
):
    step = pl.program_id(0)
    pixels, chans = normed.shape
    d_act = jnp.dot(spread[...], second[...], preferred_element_type=f32)
    d_pre = (d_act * slope[...].astype(f32)).astype(bf16)
    term[...] = lax.dot_general(
        d_pre, normed[...], (((0,), (0,)), ((), ())), preferred_element_type=f32
    ).astype(bf16)
    d_normed = jnp.dot(d_pre, first[...], preferred_element_type=f32)
    count = mine.shape[1]
    for chip in range(mine.shape[0]):
        for half, which in ((mine, core[0]), (other, 1 - core[0])):
            at = pl.ds(pl.multiple_of((2 * chip + which) * count, 32), count)
            half[chip] = term[at, :]

    @pl.when(step == 0)
    def _():
        total[...] = d_normed

    @pl.when(step > 0)
    def _():
        total[...] += d_normed

    @pl.when(step == pl.num_programs(0) - 1)
    def _():
        def norm(i, kept):
            at = pl.ds(pl.multiple_of(i * 64, 64), 64)
            grad, one = total[at, :], unit[at, :]
            kept = kept + jnp.sum((grad * one).reshape(8, 8, chans), axis=0)
            scaled = grad * gain[...]
            mean = jnp.mean(scaled, axis=-1, keepdims=True)
            along = jnp.mean(scaled * one, axis=-1, keepdims=True)
            d_filt[at, :] = inv[at, 0:1] * (scaled - mean - one * along)
            return kept

        gain_grad[...] = lax.fori_loop(0, pixels // 64, norm, jnp.zeros((8, chans), f32))


def tap_kernel(tiles, above, below, d_filt, grad, pad, total):
    slot = pl.program_id(0)
    rows, cols, chans = tiles.shape[2:]

    @pl.when(slot == 0)
    def _():
        clear_padded(pad)
        total[...] = jnp.zeros_like(total)

    def line_of(r, lanes):
        return tiles[0, 0, r, :, lanes]

    fill_padded(pad, above, line_of, below, rows, cols, chans)

    def over(i, lanes):
        for half in range(cols // 8):
            back = [d_filt[pl.ds(p * cols + 8 * half, 8), lanes] for p in range(rows)]
            for b in range(TAPS):
                line = window(pad, i, half, b, rows)
                for a in range(TAPS):
                    m = [line[p + a] * back[p] for p in range(rows)]
                    while len(m) > 1:
                        m = [m[p] + m[p + 1] for p in range(0, len(m), 2)]
                    total[a * TAPS + b, :, lanes] += m[0]

    lane_blocks(chans, over)

    @pl.when(slot == pl.num_programs(0) - 1)
    def _():
        for tap in range(TAPS * TAPS):
            grad[tap : tap + 1, :] = jnp.sum(total[tap], axis=0, keepdims=True)


def input_kernel(count, d_filt, above, below, cotan, kernel, out, pad, wide):
    slot = pl.program_id(0)
    rows, cols, chans = out.shape[2:]

    @pl.when(slot == 0)
    def _():
        spread_kernel(wide, kernel)
        clear_padded(pad)

    @pl.when(slot < MOST)
    def _():
        def line_of(r, lanes):
            return d_filt[pl.ds(r * cols, cols), lanes]

        fill_padded(pad, above, line_of, below, rows, cols, chans)
        weight = (slot < count[0]).astype(f32)

        def emit(p, half, lanes, value):
            at = pl.ds(8 * half, 8)
            out[0, 0, p, at, lanes] = value + cotan[0, 0, p, at, lanes].astype(f32) * weight

        stencil(pad, wide, rows, cols, chans, True, emit)

    @pl.when(slot >= MOST)
    def _():
        out[...] = jnp.zeros_like(out)


def out_kernel(count, act, second, tiles, cotan, scale, out, scale_grad):
    slot = pl.program_id(0)
    rows, cols, chans = tiles.shape[2:]

    @pl.when(slot == 0)
    def _():
        scale_grad[...] = jnp.zeros_like(scale_grad)

    @pl.when(slot < count[0])
    def _():
        branch = lax.dot_general(
            act[...], second[...], (((1,), (1,)), ((), ())), preferred_element_type=f32
        )
        cells = tiles[...].reshape(rows * cols, chans).astype(f32)
        held = cotan[...].reshape(rows * cols, chans).astype(f32)
        scale_grad[...] += jnp.sum((held * branch).reshape(-1, 8, chans), axis=0)
        out[...] = (cells + scale[...] * branch).astype(bf16).reshape(out.shape)

    @pl.when(slot >= count[0])
    def _():
        out[...] = jnp.zeros_like(out)


def body(tiles, cotangent, tile_counts, dw_kernel, ln_gain, fc1_weight, fc2_weight, layer_scale):
    _, slots, rows, cols, chans = tiles.shape
    hidden = fc1_weight.shape[0]
    pixels = rows * cols
    every = MOST * pixels
    taps = dw_kernel.reshape(TAPS * TAPS, chans)
    gain, scale = ln_gain[None], layer_scale[None]
    above, below = edges(tiles[0, :MOST])

    params = pltpu.CompilerParams(
        vmem_limit_bytes=60 * 1024 * 1024, dimension_semantics=("arbitrary",)
    )
    shape = jax.ShapeDtypeStruct
    brief = pl.CostEstimate(flops=1, bytes_accessed=1, transcendentals=0)
    smem = pl.BlockSpec(memory_space=pltpu.SMEM)
    tile = pl.BlockSpec((1, 1, rows, cols, chans), lambda s: (0, s, 0, 0, 0))
    tile_live = pl.BlockSpec(
        (1, 1, rows, cols, chans), lambda s: (0, jnp.minimum(s, MOST - 1), 0, 0, 0)
    )
    edge = pl.BlockSpec((1, REACH, cols, chans), lambda s: (s, 0, 0, 0))
    edge_live = pl.BlockSpec(
        (1, REACH, cols, chans), lambda s: (jnp.minimum(s, MOST - 1), 0, 0, 0)
    )
    flat = pl.BlockSpec((pixels, chans), lambda s: (s, 0))
    flat_live = pl.BlockSpec((pixels, chans), lambda s: (jnp.minimum(s, MOST - 1), 0))

    def whole(*dims):
        return pl.BlockSpec(dims, lambda s: (0,) * len(dims))

    pad = pltpu.VMEM((chans // LANES, (rows + 2 * REACH) * PITCH + 8, LANES), f32)
    wide = pltpu.VMEM((TAPS * TAPS, 8, chans), f32)

    normed, unit, inv, spread = pl.pallas_call(
        forward_kernel,
        grid=(MOST,),
        in_specs=[smem, tile, edge, edge, tile, whole(TAPS * TAPS, chans), whole(1, chans), whole(1, chans)],
        out_specs=[flat, flat, pl.BlockSpec((pixels, LANES), lambda s: (s, 0)), flat],
        out_shape=[
            shape((every, chans), bf16),
            shape((every, chans), f32),
            shape((every, LANES), f32),
            shape((every, chans), bf16),
        ],
        scratch_shapes=[pad, wide, pltpu.VMEM((pixels, chans), f32)],
        compiler_params=params,
        cost_estimate=brief,
        name="forward",
    )(tile_counts, tiles, above, below, cotangent, taps, gain, scale)

    rows_of = pl.BlockSpec((BLOCK, chans), lambda j: (j, 0))
    cols_of = pl.BlockSpec((chans, BLOCK), lambda j: (0, j))
    wide_of = pl.BlockSpec((every, BLOCK), lambda j: (0, j))
    chips = SIDE * SIDE
    halves = shape((chips, hidden // (2 * chips), chans), bf16)
    core = (lax.axis_index("slide") % 2).reshape(1)
    act, slope, mine2, other2 = pl.pallas_call(
        hidden_kernel,
        grid=(hidden // BLOCK,),
        in_specs=[smem, whole(every, chans), whole(every, chans), rows_of],
        out_specs=[wide_of, wide_of, whole(*halves.shape), whole(*halves.shape)],
        out_shape=[shape((every, hidden), bf16), shape((every, hidden), bf16), halves, halves],
        scratch_shapes=[
            pltpu.VMEM((chans, every), bf16),
            pltpu.VMEM((chans // LANES, hidden, LANES), f32),
        ],
        compiler_params=params,
        cost_estimate=brief,
        name="hidden",
    )(core, normed, spread, fc1_weight)

    act, other2 = after(act, other2)
    got2 = from_other_core(other2)
    block_out, scale_grad = pl.pallas_call(
        out_kernel,
        grid=(slots,),
        in_specs=[
            smem,
            pl.BlockSpec((pixels, hidden), lambda s: (jnp.minimum(s, MOST - 1), 0)),
            whole(chans, hidden),
            tile_live,
            tile_live,
            whole(1, chans),
        ],
        out_specs=[tile, whole(8, chans)],
        out_shape=[shape(tiles.shape, bf16), shape((8, chans), f32)],
        compiler_params=params,
        cost_estimate=brief,
        name="outs",
    )(tile_counts, act, fc2_weight, tiles, cotangent, scale)

    mine2, got2, block_out = after(mine2, got2, block_out)
    parts2 = quarters(mine2, got2)
    slope, *parts2 = after(slope, *parts2)
    ring2 = ring_sent(parts2)

    quarter_of = pl.BlockSpec((SIDE, *halves.shape[1:]), lambda j: (j, 0, 0))
    mine1, other1, d_filt, gain_grad = pl.pallas_call(
        back_kernel,
        grid=(hidden // BLOCK,),
        in_specs=[
            smem,
            whole(every, chans),
            whole(every, chans),
            wide_of,
            rows_of,
            cols_of,
            whole(every, chans),
            whole(every, LANES),
            whole(1, chans),
        ],
        out_specs=[quarter_of, quarter_of, whole(every, chans), whole(8, chans)],
        out_shape=[halves, halves, shape((every, chans), f32), shape((8, chans), f32)],
        scratch_shapes=[pltpu.VMEM((every, chans), f32), pltpu.VMEM((BLOCK, chans), bf16)],
        compiler_params=params,
        cost_estimate=brief,
        name="back",
    )(core, normed, spread, slope, fc1_weight, fc2_weight, unit, inv, gain)

    sum2 = total_of(parts2[0], ring2)
    other1, sum2 = after(other1, sum2)
    got1 = from_other_core(other1)
    d_cells = d_filt.reshape(MOST, rows, cols, chans)
    d_above, d_below = edges(d_cells.astype(bf16))
    parts1 = quarters(mine1, got1)
    d_filt, *parts1 = after(d_filt, *parts1)
    ring1 = ring_sent(parts1)

    tap_grad = pl.pallas_call(
        tap_kernel,
        grid=(MOST,),
        in_specs=[tile, edge, edge, flat],
        out_specs=whole(TAPS * TAPS, chans),
        out_shape=shape((TAPS * TAPS, chans), f32),
        scratch_shapes=[pad, wide],
        compiler_params=params,
        cost_estimate=brief,
        name="taps",
    )(tiles, above, below, d_filt)

    scale_row = jnp.sum(scale_grad, axis=0)
    gain_row = jnp.sum(gain_grad, axis=0)
    small = jnp.concatenate([tap_grad, gain_row[None], scale_row[None]]).astype(bf16)
    lines = -(-small.shape[0] // chips)
    small = jnp.pad(small, ((0, chips * lines - small.shape[0]), (0, 0)))
    small = jnp.pad(small.reshape(chips, lines, chans), ((0, 0), (0, -lines % 8), (0, 0)))
    blocks = jnp.concatenate([sum2, total_of(parts1[0], ring1), small], axis=1)
    blocks, d_above, d_below, d_filt = after(blocks, d_above, d_below, d_filt)
    sums = plane_exchanged(blocks)

    grad_input = pl.pallas_call(
        input_kernel,
        grid=(slots,),
        in_specs=[smem, flat_live, edge_live, edge_live, tile_live, whole(TAPS * TAPS, chans)],
        out_specs=tile,
        out_shape=shape(tiles.shape, f32),
        scratch_shapes=[pad, wide],
        compiler_params=params,
        cost_estimate=brief,
        name="inputs",
    )(tile_counts, d_filt, d_above, d_below, cotangent, taps)

    own = hidden // (8 * chips)
    grad_fc2 = sums[:own].reshape(-1, hidden)
    grad_fc1 = sums[own : 2 * own]
    share, grad_input = after(sums[2 * own : 2 * own + lines], grad_input)
    small = everywhere(share)
    grad_kernel = small[: TAPS * TAPS].reshape(dw_kernel.shape)
    return (
        block_out,
        grad_input,
        grad_fc1,
        grad_fc2,
        grad_kernel,
        small[TAPS * TAPS],
        small[TAPS * TAPS + 1],
    )


def solution(mesh):
    in_specs = (
        P("slide", None, "row", None, None),
        P("slide", None, "row", None, None),
        P("slide"),
        P(),
        P(),
        P(),
        P(),
        P(),
    )
    out_specs = (
        P("slide", None, "row", None, None),
        P("slide", None, "row", None, None),
        P(("slide", "row"), None),
        P(("slide", "row"), None),
        P(),
        P(),
        P(),
    )
    return jax.shard_map(body, mesh=mesh, in_specs=in_specs, out_specs=out_specs, check_vma=False)
```

time: 234 us -> 176 us (0.75)
  Pallas kernels: 112 us -> 85.9 us
  waiting for transfers between devices: 40.6 us -> 28.5 us
  local copies, waits for them, and re-layouts: 20.8 us -> 9.56 us
  starting transfers between devices: 43.7 us -> 35.4 us
    ppermute x2, waiting for transfers between devices: 29.3 us -> 0.66 us  [edges(): below = lax.ppermute(head, 'row', [(i + 1, i) for i in range(ends)])]
    all_to_all x2 -> x1, starting transfers between devices: 22.2 us -> 6.4 us  [plane_exchanged(): lax.all_to_all(blocks.reshape(-1, blocks.shape[-1]), ('slide', 'row'), 0,...]
    ppermute x0 -> x6, starting transfers between devices: none -> 9.71 us  [ring_sent(): lax.ppermute(parts[by], ('slide', 'row'), pairs[by])]
    pallas_call x1, Pallas kernels: 19.6 us -> 10.7 us  [body(): pl.pallas_call(tap_kernel, grid=(MOST,), in_specs=[tile, edge, edge, flat...]
    all_to_all x2 -> x1, waiting for transfers between devices: 0.01 us -> 7.95 us  [plane_exchanged(): lax.all_to_all(blocks.reshape(-1, blocks.shape[-1]), ('slide', 'row'), 0,...]
    pallas_call x2, Pallas kernels: 46.6 us -> 38.7 us  [the longest x1 20.4 us: body(): pl.pallas_call(back_kernel, grid=(hidden // BLOCK,), in_specs=[smem, whol...]
    squeeze x2 -> x0, local copies, waits for them, and re-layouts: 6.48 us -> none  [core_halves(): other = lax.dynamic_index_in_dim(halves, 1 - core, 1, keepdims=False)]
    reshape x5 -> x2, local copies, waits for them, and re-layouts: 6.38 us -> 0.69 us  [the longest x1 0.66 us: body(): grad_fc2 = sums[:own].reshape(-1, hidden)]
  transfers between devices with their start and end apart: 9 -> 14, of which waited for: 4 -> 5; matrix products, arithmetic and copies ran while one was open for 7% -> 6% of each run, Pallas kernels for 19% -> 30%
where the time goes in v2:
time: 176 us
  Pallas kernels  85.9 us (49%)
  starting transfers between devices  35.4 us (20%)
  waiting for transfers between devices  28.5 us (16%)
  other arithmetic  14.5 us (8%)
  local copies, waits for them, and re-layouts  9.56 us (5%)
    pallas_call x1, Pallas kernels, body(): pl.pallas_call(back_kernel, grid=(hidden // BLOCK,), in_specs=[smem, whol...  20.4 us
    pallas_call x1, Pallas kernels, body(): pl.pallas_call(hidden_kernel, grid=(hidden // BLOCK,), in_specs=[smem, wh...  18.3 us
    pallas_call x1, Pallas kernels, body(): pl.pallas_call(forward_kernel, grid=(MOST,), in_specs=[smem, tile, edge,...  15.6 us
    all_to_all x1, waiting for transfers between devices, everywhere(): got = lax.all_to_all(sent, ('slide', 'row'), 0, 0, tiled=True)  14.7 us
    pallas_call x1, Pallas kernels, body(): pl.pallas_call(input_kernel, grid=(slots,), in_specs=[smem, flat_live, ed...  13.3 us
    pallas_call x1, Pallas kernels, body(): pl.pallas_call(tap_kernel, grid=(MOST,), in_specs=[tile, edge, edge, flat...  10.7 us
    ppermute x6, starting transfers between devices, ring_sent(): lax.ppermute(parts[by], ('slide', 'row'), pairs[by])  9.71 us
    ppermute x2, starting transfers between devices, edges(): above = lax.ppermute(tail, 'row', [(i, i + 1) for i in range(ends)])  9.01 us
  transfers between devices with their start and end apart: 14, of which 5 were waited for; matrix products, arithmetic and copies ran while one was open for 6% of the time, Pallas kernels for 30%

profile of v2, /device:TPU:1, one launch (start us, length us, event | category | flops | bytes accessed | tf_op | source)
XLA Modules:
  0.0 175.5 jit_solution(5133867456199172031)
XLA Ops:
  0.7 1.4 slice_bitcast_fusion
  2.1 1.3 collective-permute-start.1
  3.4 5.0 %collective-permute-start = (bf16[3,3,16,768]{3,2,1,0:T(8,128)(2,1)S(1)}, bf16[3,3,16,768]{3,2,1,0:T(8,128)(2,1)S(1)}, u32[]{:S(2)}, u32[]{:S(2)}) collective-permute-start(bf16[3,3,16,768]{3,2,1,0:T(8,128)(2,1)S(1)} %get-tuple-element.96), channel_id=1, source_target_pairs={{0,1},{1,2},{2,3},{4,5},{5,6},{6,7},{8,9},{9,10},{10,11},{12,13},{... | collective-permute-start | bytes 663560 | tf_op jit(solution)/shard_map/ppermute | solution.py:103
  13.2 15.6 %forward.1 = (bf16[768,768]{1,0:T(8,128)(2,1)}, f32[768,768]{1,0:T(8,128)}, f32[768,128]{1,0:T(8,128)}, bf16[768,768]{1,0:T(8,128)(2,1)}) custom-call(s32[1]{0:T(128)S(6)} %copy.15.count, bf16[1,4,16,16,768]{4,3,2,1,0:T(8,128)(2,1)} %tiles.5, bf16[3,3,16,768]{3,2,1,0:T(8,128)(2,1)} %copy-done.4, bf16[3,3,16,768]{3,2,1,0:T(8,128)(2,1)} %copy-done.3, ...), custom_call_target="tpu_custom_call" | custom-call | flops 1 | bytes 1 | tf_op jit(solution)/shard_map/forward/pallas_call | solution.py:396
  28.8 18.3 %hidden.1 = (bf16[768,3072]{1,0:T(8,128)(2,1)}, bf16[768,3072]{1,0:T(8,128)(2,1)}, bf16[16,96,768]{2,1,0:T(8,128)(2,1)}, bf16[16,96,768]{2,1,0:T(8,128)(2,1)}) custom-call(s32[1]{0:T(128)} %bitcast.core, bf16[768,768]{1,0:T(8,128)(2,1)} %get-tuple-element.44.normed, bf16[768,768]{1,0:T(8,128)(2,1)} %get-tuple-element.45.spread, bf16[3072,768]{1,0:T(8,128)(2,1)} %first.3), custom_call_target="tpu_custom_call" | custom-call | flops 1 | bytes 1 | tf_op jit(solution)/shard_map/hidden/pallas_call | solution.py:419
  47.1 1.6 collective-permute-start.2
  48.8 7.6 %outs.1 = (bf16[1,4,16,16,768]{4,3,2,1,0:T(8,128)(2,1)}, f32[8,768]{1,0:T(8,128)}) custom-call(s32[1]{0:T(128)S(6)} %copy.15.count, bf16[768,3072]{1,0:T(8,128)(2,1)} %get-tuple-element.50.act, bf16[768,3072]{1,0:T(8,128)(2,1)} %second.3, bf16[1,4,16,16,768]{4,3,2,1,0:T(8,128)(2,1)} %tiles.5, bf16[1,4,16,16,768]{4,3,2,1,0:T(8,128)(2,1)} %cotan.5, ...), custom_call_target="tpu_custom_call" | custom-call | flops 1 | bytes 1 | tf_op jit(solution)/shard_map/outs/pallas_call | solution.py:436
  56.4 4.9 %add_convert_fusion.6 = (bf16[4,4,24,768]{3,2,1,0:T(8,128)(2,1)S(1)}, bf16[4,4,24,768]{3,2,1,0:T(8,128)(2,1)}, bf16[4,4,24,768]{3,2,1,0:T(8,128)(2,1)}, bf16[4,4,24,768]{3,2,1,0:T(8,128)(2,1)S(1)}) fusion(bf16[4,4,4,24,768]{4,3,2,1,0:T(8,128)(2,1)} %bitcast.5, s32[]{:T(128)S(6)} %select_n.194, bf16[4,4,4,24,768]{4,3,2,1,0:T(8,128)(2,1)S(1)} %bitcast.111, ...), kind=kLoop, calls=%fused_computation.10 | loop fusion | flops 7077888 | bytes 11796497 | tf_op jit(solution)/shard_map/convert_element_type | solution.py:48
  62.4 2.9 %collective-permute-start.4 = (bf16[4,4,24,768]{3,2,1,0:T(8,128)(2,1)}, bf16[4,4,24,768]{3,2,1,0:T(8,128)(2,1)S(1)}, u32[]{:S(2)}, u32[]{:S(2)}) collective-permute-start(bf16[4,4,24,768]{3,2,1,0:T(8,128)(2,1)} %get-tuple-element.62), channel_id=1, source_target_pairs={{0,2},{4,20},{1,3},{5,21},{2,0},{6,22},{3,1},{7,23},{8,10},{12,28}... | collective-permute-start | bytes 1769480 | tf_op jit(solution)/shard_map/ppermute | solution.py:64
  65.3 2.1 %collective-permute-start.5 = (bf16[4,4,24,768]{3,2,1,0:T(8,128)(2,1)S(1)}, bf16[4,4,24,768]{3,2,1,0:T(8,128)(2,1)S(1)}, u32[]{:S(2)}, u32[]{:S(2)}) collective-permute-start(bf16[4,4,24,768]{3,2,1,0:T(8,128)(2,1)S(1)} %get-tuple-element.63), channel_id=1, source_target_pairs={{0,3},{4,28},{1,0},{5,29},{2,1},{6,30},{3,2},{7,31},{8,11},{12,4},... | collective-permute-start | bytes 1769480 | tf_op jit(solution)/shard_map/ppermute | solution.py:64
  67.3 20.4 %back.1 = (bf16[16,96,768]{2,1,0:T(8,128)(2,1)}, bf16[16,96,768]{2,1,0:T(8,128)(2,1)}, f32[768,768]{1,0:T(8,128)}, f32[8,768]{1,0:T(8,128)}) custom-call(s32[1]{0:T(128)} %bitcast.core, bf16[768,768]{1,0:T(8,128)(2,1)} %get-tuple-element.44.normed, bf16[768,768]{1,0:T(8,128)(2,1)} %get-tuple-element.45.spread, bf16[768,3072]{1,0:T(8,128)(2,1)} %get-tuple-element.56.slope, ...), custom_call_target="tpu_custom_call" | custom-call | flops 1 | bytes 1 | tf_op jit(solution)/shard_map/back/pallas_call | solution.py:460
  88.0 2.5 %collective-permute-start.6 = (bf16[16,96,768]{2,1,0:T(8,128)(2,1)}, bf16[16,96,768]{2,1,0:T(8,128)(2,1)S(1)}, u32[]{:S(2)}, u32[]{:S(2)}) collective-permute-start(bf16[16,96,768]{2,1,0:T(8,128)(2,1)} %get-tuple-element.67), channel_id=1, source_target_pairs={{0,4},{4,0},{8,12},{12,8},{16,20},{20,16},{24,28},{28,24},{32,36},... | collective-permute-start | bytes 7077896 | tf_op jit(solution)/shard_map/ppermute | solution.py:34
  90.5 4.4 %collective-permute-done.6 = bf16[16,96,768]{2,1,0:T(8,128)(2,1)S(1)} collective-permute-done((bf16[16,96,768]{2,1,0:T(8,128)(2,1)}, bf16[16,96,768]{2,1,0:T(8,128)(2,1)S(1)}, u32[]{:S(2)}, u32[]{:S(2)}) %collective-permute-start.6) | collective-permute-done | bytes 2359328 | tf_op jit(solution)/shard_map/ppermute | solution.py:34
  94.9 2.4 %add_convert_fusion.1 = (bf16[4,4,24,768]{3,2,1,0:T(8,128)(2,1)}, bf16[4,4,24,768]{3,2,1,0:T(8,128)(2,1)}, bf16[4,4,24,768]{3,2,1,0:T(8,128)(2,1)}, bf16[4,4,24,768]{3,2,1,0:T(8,128)(2,1)S(1)}) fusion(bf16[4,4,4,24,768]{4,3,2,1,0:T(8,128)(2,1)S(1)} %bitcast.113, s32[]{:T(128)S(6)} %select_n.194, bf16[4,4,4,24,768]{4,3,2,1,0:T(8,128)(2,1)S(1)} %bitcast.112, ...), kind=kLoop, calls=%fused_computation.5 | loop fusion | flops 7077888 | bytes 11796497 | tf_op jit(solution)/shard_map/convert_element_type | solution.py:48
  98.5 1.4 collective-permute-start.8
  104.7 1.3 collective-permute-start.11
  106.0 4.0 %collective-permute-start.10 = (bf16[3,3,16,768]{3,2,1,0:T(8,128)(2,1)S(1)}, bf16[3,3,16,768]{3,2,1,0:T(8,128)(2,1)S(1)}, u32[]{:S(2)}, u32[]{:S(2)}) collective-permute-start(bf16[3,3,16,768]{3,2,1,0:T(8,128)(2,1)S(1)} %get-tuple-element.94), channel_id=1, source_target_pairs={{0,1},{1,2},{2,3},{4,5},{5,6},{6,7},{8,9},{9,10},{10,11},{12,13},{... | collective-permute-start | bytes 663560 | tf_op jit(solution)/shard_map/ppermute | solution.py:103
  110.0 10.7 %taps.1 = f32[49,768]{1,0:T(8,128)} custom-call(bf16[1,4,16,16,768]{4,3,2,1,0:T(8,128)(2,1)} %tiles.5, bf16[3,3,16,768]{3,2,1,0:T(8,128)(2,1)} %copy-done.4, bf16[3,3,16,768]{3,2,1,0:T(8,128)(2,1)} %copy-done.3, f32[768,768]{1,0:T(8,128)} %get-tuple-element.76.d_filt), custom_call_target="tpu_custom_call" | custom-call | flops 1 | bytes 1 | tf_op jit(solution)/shard_map/taps/pallas_call | solution.py:491
  121.7 1.7 add_convert_fusion
  125.4 6.4 %all-to-all-start = ((bf16[16,56,768]{2,1,0:T(8,128)(2,1)}), bf16[16,56,768]{2,1,0:T(8,128)(2,1)S(1)}, u32[]{:S(2)}, u32[]{:S(2)}) async-start(bf16[16,56,768]{2,1,0:T(8,128)(2,1)} %fusion.1), calls=%async_computation | async-start | bytes 2752512 | tf_op jit(solution)/shard_map/all_to_all | solution.py:78
  131.9 13.3 %inputs.1 = f32[1,4,16,16,768]{4,3,2,1,0:T(8,128)} custom-call(s32[1]{0:T(128)S(6)} %copy.15.count, f32[768,768]{1,0:T(8,128)} %get-tuple-element.76.d_filt, bf16[3,3,16,768]{3,2,1,0:T(8,128)(2,1)} %copy-done.6, bf16[3,3,16,768]{3,2,1,0:T(8,128)(2,1)} %copy-done.5, bf16[1,4,16,16,768]{4,3,2,1,0:T(8,128)(2,1)} %cotan.5, f32[49,768]{1,0:T(8,128)} %reshape.76.kernel), custom_call_target="tpu_custom_call" | custom-call | flops 1 | bytes 1 | tf_op jit(solution)/shard_map/inputs/pallas_call | solution.py:513
  145.1 8.0 %all-to-all-done = bf16[16,56,768]{2,1,0:T(8,128)(2,1)S(1)} async-done(((bf16[16,56,768]{2,1,0:T(8,128)(2,1)}), bf16[16,56,768]{2,1,0:T(8,128)(2,1)S(1)}, u32[]{:S(2)}, u32[]{:S(2)}) %all-to-all-start) | async-done | bytes 1376288 | tf_op jit(solution)/shard_map/all_to_all | solution.py:78
  154.3 3.6 %all-to-all-start.1 = ((bf16[128,24,128]{2,1,0:T(8,128)(2,1)}), bf16[128,24,128]{2,1,0:T(8,128)(2,1)S(1)}, u32[]{:S(2)}, u32[]{:S(2)}) async-start(bf16[128,24,128]{2,1,0:T(8,128)(2,1)} %broadcast_in_dim.26), calls=%async_computation.1 | async-start | bytes 1572864 | tf_op jit(solution)/shard_map/all_to_all | solution.py:93
  159.2 14.7 %all-to-all-done.1 = bf16[128,24,128]{2,1,0:T(8,128)(2,1)S(1)} async-done(((bf16[128,24,128]{2,1,0:T(8,128)(2,1)}), bf16[128,24,128]{2,1,0:T(8,128)(2,1)S(1)}, u32[]{:S(2)}, u32[]{:S(2)}) %all-to-all-start.1) | async-done | bytes 786464 | tf_op jit(solution)/shard_map/all_to_all | solution.py:93
  (62 shorter events, 18.7 us)
Async XLA Ops:
  0.6 8.4 %copy-start.8 = (f32[768]{0:T(1024)S(1)}, f32[768]{0:T(1024)}, u32[]{:S(2)}) copy-start(f32[768]{0:T(1024)} %param.12) | copy-start | bytes 9220
  0.6 9.0 %copy-start.9 = (f32[768]{0:T(1024)S(1)}, f32[768]{0:T(1024)}, u32[]{:S(2)}) copy-start(f32[768]{0:T(1024)} %param.15) | copy-start | bytes 9220
  0.7 9.6 %copy-start.7 = (f32[7,7,768]{2,1,0:T(8,128)S(1)}, f32[7,7,768]{2,1,0:T(8,128)}, u32[]{:S(2)}) copy-start(f32[7,7,768]{2,1,0:T(8,128)} %param.11) | copy-start | bytes 451588
  2.1 9.5 %collective-permute-start.1 = (bf16[3,3,16,768]{3,2,1,0:T(8,128)(2,1)S(1)}, bf16[3,3,16,768]{3,2,1,0:T(8,128)(2,1)S(1)}, u32[]{:S(2)}, u32[]{:S(2)}) collective-permute-start(bf16[3,3,16,768]{3,2,1,0:T(8,128)(2,1)S(1)} %get-tuple-element.95), channel_id=1, source_target_pairs={{1,0},{2,1},{3,2},{5,4},{6,5},{7,6},{9,8},{10,9},{11,10},{13,12},{... | collective-permute-start | bytes 663560 | tf_op jit(solution)/shard_map/ppermute | solution.py:104
  3.4 9.1 %collective-permute-start = (bf16[3,3,16,768]{3,2,1,0:T(8,128)(2,1)S(1)}, bf16[3,3,16,768]{3,2,1,0:T(8,128)(2,1)S(1)}, u32[]{:S(2)}, u32[]{:S(2)}) collective-permute-start(bf16[3,3,16,768]{3,2,1,0:T(8,128)(2,1)S(1)} %get-tuple-element.96), channel_id=1, source_target_pairs={{0,1},{1,2},{2,3},{4,5},{5,6},{6,7},{8,9},{9,10},{10,11},{12,13},{... | collective-permute-start | bytes 663560 | tf_op jit(solution)/shard_map/ppermute | solution.py:103
  11.6 0.9 copy-start.3
  12.5 0.7 copy-start.4
  47.1 9.2 %collective-permute-start.2 = (bf16[16,96,768]{2,1,0:T(8,128)(2,1)}, bf16[16,96,768]{2,1,0:T(8,128)(2,1)}, u32[]{:S(2)}, u32[]{:S(2)}) collective-permute-start(bf16[16,96,768]{2,1,0:T(8,128)(2,1)} %get-tuple-element.49), channel_id=1, source_target_pairs={{0,4},{4,0},{8,12},{12,8},{16,20},{20,16},{24,28},{28,24},{32,36},... | collective-permute-start | bytes 7077896 | tf_op jit(solution)/shard_map/ppermute | solution.py:34
  48.8 7.6 %copy-start.1 = (bf16[16,96,768]{2,1,0:T(8,128)(2,1)S(1)}, bf16[16,96,768]{2,1,0:T(8,128)(2,1)}, u32[]{:S(2)}) copy-start(bf16[16,96,768]{2,1,0:T(8,128)(2,1)} %get-tuple-element.54) | copy-start | bytes 7077892
  61.2 26.5 %collective-permute-start.3 = (bf16[4,4,24,768]{3,2,1,0:T(8,128)(2,1)}, bf16[4,4,24,768]{3,2,1,0:T(8,128)(2,1)S(1)}, u32[]{:S(2)}, u32[]{:S(2)}) collective-permute-start(bf16[4,4,24,768]{3,2,1,0:T(8,128)(2,1)} %get-tuple-element.61), channel_id=1, source_target_pairs={{0,1},{4,12},{1,2},{5,13},{2,3},{6,14},{3,0},{7,15},{8,9},{12,20},... | collective-permute-start | bytes 1769480 | tf_op jit(solution)/shard_map/ppermute | solution.py:64
  62.4 25.3 %collective-permute-start.4 = (bf16[4,4,24,768]{3,2,1,0:T(8,128)(2,1)}, bf16[4,4,24,768]{3,2,1,0:T(8,128)(2,1)S(1)}, u32[]{:S(2)}, u32[]{:S(2)}) collective-permute-start(bf16[4,4,24,768]{3,2,1,0:T(8,128)(2,1)} %get-tuple-element.62), channel_id=1, source_target_pairs={{0,2},{4,20},{1,3},{5,21},{2,0},{6,22},{3,1},{7,23},{8,10},{12,28}... | collective-permute-start | bytes 1769480 | tf_op jit(solution)/shard_map/ppermute | solution.py:64
  65.3 22.5 %collective-permute-start.5 = (bf16[4,4,24,768]{3,2,1,0:T(8,128)(2,1)S(1)}, bf16[4,4,24,768]{3,2,1,0:T(8,128)(2,1)S(1)}, u32[]{:S(2)}, u32[]{:S(2)}) collective-permute-start(bf16[4,4,24,768]{3,2,1,0:T(8,128)(2,1)S(1)} %get-tuple-element.63), channel_id=1, source_target_pairs={{0,3},{4,28},{1,0},{5,29},{2,1},{6,30},{3,2},{7,31},{8,11},{12,4},... | collective-permute-start | bytes 1769480 | tf_op jit(solution)/shard_map/ppermute | solution.py:64
  87.7 7.2 %copy-start.2 = (bf16[16,96,768]{2,1,0:T(8,128)(2,1)S(1)}, bf16[16,96,768]{2,1,0:T(8,128)(2,1)}, u32[]{:S(2)}) copy-start(bf16[16,96,768]{2,1,0:T(8,128)(2,1)} %get-tuple-element.66) | copy-start | bytes 7077892
  88.0 6.9 %collective-permute-start.6 = (bf16[16,96,768]{2,1,0:T(8,128)(2,1)}, bf16[16,96,768]{2,1,0:T(8,128)(2,1)S(1)}, u32[]{:S(2)}, u32[]{:S(2)}) collective-permute-start(bf16[16,96,768]{2,1,0:T(8,128)(2,1)} %get-tuple-element.67), channel_id=1, source_target_pairs={{0,4},{4,0},{8,12},{12,8},{16,20},{20,16},{24,28},{28,24},{32,36},... | collective-permute-start | bytes 7077896 | tf_op jit(solution)/shard_map/ppermute | solution.py:34
  94.9 6.8 %copy-start = (f32[768,768]{1,0:T(8,128)S(1)}, f32[768,768]{1,0:T(8,128)}, u32[]{:S(2)}) copy-start(f32[768,768]{1,0:T(8,128)} %get-tuple-element.76.d_filt) | copy-start | bytes 7077892
  97.3 24.4 %collective-permute-start.7 = (bf16[4,4,24,768]{3,2,1,0:T(8,128)(2,1)}, bf16[4,4,24,768]{3,2,1,0:T(8,128)(2,1)}, u32[]{:S(2)}, u32[]{:S(2)}) collective-permute-start(bf16[4,4,24,768]{3,2,1,0:T(8,128)(2,1)} %get-tuple-element.69), channel_id=1, source_target_pairs={{0,1},{4,12},{1,2},{5,13},{2,3},{6,14},{3,0},{7,15},{8,9},{12,20},... | collective-permute-start | bytes 1769480 | tf_op jit(solution)/shard_map/ppermute | solution.py:64
  98.5 23.2 %collective-permute-start.8 = (bf16[4,4,24,768]{3,2,1,0:T(8,128)(2,1)}, bf16[4,4,24,768]{3,2,1,0:T(8,128)(2,1)}, u32[]{:S(2)}, u32[]{:S(2)}) collective-permute-start(bf16[4,4,24,768]{3,2,1,0:T(8,128)(2,1)} %get-tuple-element.70), channel_id=1, source_target_pairs={{0,2},{4,20},{1,3},{5,21},{2,0},{6,22},{3,1},{7,23},{8,10},{12,28}... | collective-permute-start | bytes 1769480 | tf_op jit(solution)/shard_map/ppermute | solution.py:64
  99.9 21.8 %collective-permute-start.9 = (bf16[4,4,24,768]{3,2,1,0:T(8,128)(2,1)}, bf16[4,4,24,768]{3,2,1,0:T(8,128)(2,1)}, u32[]{:S(2)}, u32[]{:S(2)}) collective-permute-start(bf16[4,4,24,768]{3,2,1,0:T(8,128)(2,1)} %get-tuple-element.71), channel_id=1, source_target_pairs={{0,3},{4,28},{1,0},{5,29},{2,1},{6,30},{3,2},{7,31},{8,11},{12,4},... | collective-permute-start | bytes 1769480 | tf_op jit(solution)/shard_map/ppermute | solution.py:64
  104.7 20.0 %collective-permute-start.11 = (bf16[3,3,16,768]{3,2,1,0:T(8,128)(2,1)S(1)}, bf16[3,3,16,768]{3,2,1,0:T(8,128)(2,1)S(1)}, u32[]{:S(2)}, u32[]{:S(2)}) collective-permute-start(bf16[3,3,16,768]{3,2,1,0:T(8,128)(2,1)S(1)} %get-tuple-element.93), channel_id=1, source_target_pairs={{1,0},{2,1},{3,2},{5,4},{6,5},{7,6},{9,8},{10,9},{11,10},{13,12},{... | collective-permute-start | bytes 663560 | tf_op jit(solution)/shard_map/ppermute | solution.py:104
  106.0 18.7 %collective-permute-start.10 = (bf16[3,3,16,768]{3,2,1,0:T(8,128)(2,1)S(1)}, bf16[3,3,16,768]{3,2,1,0:T(8,128)(2,1)S(1)}, u32[]{:S(2)}, u32[]{:S(2)}) collective-permute-start(bf16[3,3,16,768]{3,2,1,0:T(8,128)(2,1)S(1)} %get-tuple-element.94), channel_id=1, source_target_pairs={{0,1},{1,2},{2,3},{4,5},{5,6},{6,7},{8,9},{9,10},{10,11},{12,13},{... | collective-permute-start | bytes 663560 | tf_op jit(solution)/shard_map/ppermute | solution.py:103
  124.7 0.7 copy-start.5
  124.7 0.8 copy-start.6
  125.4 27.6 %all-to-all-start = ((bf16[16,56,768]{2,1,0:T(8,128)(2,1)}), bf16[16,56,768]{2,1,0:T(8,128)(2,1)S(1)}, u32[]{:S(2)}, u32[]{:S(2)}) async-start(bf16[16,56,768]{2,1,0:T(8,128)(2,1)} %fusion.1), calls=%async_computation | async-start | bytes 2752512 | tf_op jit(solution)/shard_map/all_to_all | solution.py:78
  154.3 19.5 %all-to-all-start.1 = ((bf16[128,24,128]{2,1,0:T(8,128)(2,1)}), bf16[128,24,128]{2,1,0:T(8,128)(2,1)S(1)}, u32[]{:S(2)}, u32[]{:S(2)}) async-start(bf16[128,24,128]{2,1,0:T(8,128)(2,1)} %broadcast_in_dim.26), calls=%async_computation.1 | async-start | bytes 1572864 | tf_op jit(solution)/shard_map/all_to_all | solution.py:93

commit v3 on v2

--- a/solution.py
+++ b/solution.py
@@ -209,72 +209,83 @@
     return jnp.where(pre < 0.0, tail, 1.0 - tail), bell * density
 
 
-def hidden_kernel(core, normed, spread, first, act, slope, mine, other, turned, total):
-    step = pl.program_id(0)
-
-    @pl.when(step == 0)
-    def _():
-        turned[...] = spread[...].T
-
-    pre = lax.dot_general(
-        normed[...], first[...], (((1,), (1,)), ((), ())), preferred_element_type=f32
-    )
-    cdf, pdf = gelu_parts(pre)
-    active = (pre * cdf).astype(bf16)
-    act[...] = active
-    slope[...] = (cdf + pre * pdf).astype(bf16)
-    grad = jnp.dot(turned[...], active, preferred_element_type=f32)
-    for i in range(BLOCK // LANES):
-        total[i, pl.ds(step, grad.shape[0], stride=4), :] = grad[:, i * LANES : (i + 1) * LANES]
-
-    @pl.when(step == pl.num_programs(0) - 1)
-    def _():
-        count = mine.shape[1]
-        for chip in range(mine.shape[0]):
-            for half, which in ((mine, core[0]), (other, 1 - core[0])):
-                at = pl.ds(pl.multiple_of((2 * chip + which) * count, 32), count)
-                for i in range(BLOCK // LANES):
-                    half[chip, :, i * LANES : (i + 1) * LANES] = total[i, at, :].astype(bf16)
-
-
-def back_kernel(
-    core, normed, spread, slope, first, second, unit, inv, gain, mine, other, d_filt, gain_grad, total, term
+def split_rows(core, mine, other, rows_at):
+    count = mine.shape[1]
+    for chip in range(mine.shape[0]):
+        for half, which in ((mine, core[0]), (other, 1 - core[0])):
+            rows_at(half, chip, pl.ds(pl.multiple_of((2 * chip + which) * count, 32), count))
+
+
+def mlp_kernel(
+    core, count, normed, spread, first, second, unit, inv, gain, scale, tiles, cotan,
+    mine1, other1, mine2, other2, d_filt, out, gain_grad, scale_grad,
+    turned, total2, term, back, branch,
 ):
     step = pl.program_id(0)
     pixels, chans = normed.shape
+    rows, cols = tiles.shape[2:4]
+
+    @pl.when(step == 0)
+    def _():
+        turned[...] = spread[...].T
+        back[...] = jnp.zeros_like(back)
+        branch[...] = jnp.zeros_like(branch)
+
+    pre = lax.dot_general(
+        normed[...], first[...], (((1,), (1,)), ((), ())), preferred_element_type=f32
+    )
     d_act = jnp.dot(spread[...], second[...], preferred_element_type=f32)
-    d_pre = (d_act * slope[...].astype(f32)).astype(bf16)
+    cdf, pdf = gelu_parts(pre)
+    active = (pre * cdf).astype(bf16)
+    d_pre = (d_act * (cdf + pre * pdf)).astype(bf16)
+    grad = jnp.dot(turned[...], active, preferred_element_type=f32)
+    for i in range(BLOCK // LANES):
+        total2[i, pl.ds(step, chans, stride=4), :] = grad[:, i * LANES : (i + 1) * LANES]
+    branch[...] += lax.dot_general(
+        active, second[...], (((1,), (1,)), ((), ())), preferred_element_type=f32
+    )
     term[...] = lax.dot_general(
         d_pre, normed[...], (((0,), (0,)), ((), ())), preferred_element_type=f32
     ).astype(bf16)
-    d_normed = jnp.dot(d_pre, first[...], preferred_element_type=f32)
-    count = mine.shape[1]
-    for chip in range(mine.shape[0]):
-        for half, which in ((mine, core[0]), (other, 1 - core[0])):
-            at = pl.ds(pl.multiple_of((2 * chip + which) * count, 32), count)
-            half[chip] = term[at, :]
-
-    @pl.when(step == 0)
-    def _():
-        total[...] = d_normed
-
-    @pl.when(step > 0)
-    def _():
-        total[...] += d_normed
+
+    def copy1(half, chip, at):
+        half[chip] = term[at, :]
+
+    split_rows(core, mine1, other1, copy1)
+    back[...] += jnp.dot(d_pre, first[...], preferred_element_type=f32)
 
     @pl.when(step == pl.num_programs(0) - 1)
     def _():
-        def norm(i, kept):
+        def copy2(half, chip, at):
+            for i in range(BLOCK // LANES):
+                half[chip, :, i * LANES : (i + 1) * LANES] = total2[i, at, :].astype(bf16)
+
+        split_rows(core, mine2, other2, copy2)
+        lines = 64 // cols
+
+        def finish(i, kept):
+            gains, scales = kept
             at = pl.ds(pl.multiple_of(i * 64, 64), 64)
-            grad, one = total[at, :], unit[at, :]
-            kept = kept + jnp.sum((grad * one).reshape(8, 8, chans), axis=0)
+            grad, one = back[at, :], unit[at, :]
+            gains = gains + jnp.sum((grad * one).reshape(8, 8, chans), axis=0)
             scaled = grad * gain[...]
             mean = jnp.mean(scaled, axis=-1, keepdims=True)
             along = jnp.mean(scaled * one, axis=-1, keepdims=True)
             d_filt[at, :] = inv[at, 0:1] * (scaled - mean - one * along)
-            return kept
-
-        gain_grad[...] = lax.fori_loop(0, pixels // 64, norm, jnp.zeros((8, chans), f32))
+            slot = i * lines // rows
+            weight = (slot < count[0]).astype(f32)
+            line = pl.ds(i * lines - slot * rows, lines)
+            value = branch[at, :]
+            held = cotan[0, slot, line].reshape(64, chans).astype(f32) * weight
+            scales = scales + jnp.sum((held * value).reshape(8, 8, chans), axis=0)
+            cells = tiles[0, slot, line].reshape(64, chans).astype(f32)
+            filled = ((cells + scale[...] * value) * weight).astype(bf16)
+            out[0, slot, line] = filled.reshape(lines, cols, chans)
+            return gains, scales
+
+        start = jnp.zeros((8, chans), f32)
+        gain_grad[...], scale_grad[...] = lax.fori_loop(0, pixels // 64, finish, (start, start))
+        out[0, MOST:] = jnp.zeros((out.shape[1] - MOST, rows, cols, chans), bf16)
 
 
 def tap_kernel(tiles, above, below, d_filt, grad, pad, total):
@@ -334,29 +345,6 @@
         stencil(pad, wide, rows, cols, chans, True, emit)
 
     @pl.when(slot >= MOST)
-    def _():
-        out[...] = jnp.zeros_like(out)
-
-
-def out_kernel(count, act, second, tiles, cotan, scale, out, scale_grad):
-    slot = pl.program_id(0)
-    rows, cols, chans = tiles.shape[2:]
-
-    @pl.when(slot == 0)
-    def _():
-        scale_grad[...] = jnp.zeros_like(scale_grad)
-
-    @pl.when(slot < count[0])
-    def _():
-        branch = lax.dot_general(
-            act[...], second[...], (((1,), (1,)), ((), ())), preferred_element_type=f32
-        )
-        cells = tiles[...].reshape(rows * cols, chans).astype(f32)
-        held = cotan[...].reshape(rows * cols, chans).astype(f32)
-        scale_grad[...] += jnp.sum((held * branch).reshape(-1, 8, chans), axis=0)
-        out[...] = (cells + scale[...] * branch).astype(bf16).reshape(out.shape)
-
-    @pl.when(slot >= count[0])
     def _():
         out[...] = jnp.zeros_like(out)
 
@@ -410,83 +398,69 @@
         name="forward",
     )(tile_counts, tiles, above, below, cotangent, taps, gain, scale)
 
-    rows_of = pl.BlockSpec((BLOCK, chans), lambda j: (j, 0))
-    cols_of = pl.BlockSpec((chans, BLOCK), lambda j: (0, j))
-    wide_of = pl.BlockSpec((every, BLOCK), lambda j: (0, j))
     chips = SIDE * SIDE
     halves = shape((chips, hidden // (2 * chips), chans), bf16)
     core = (lax.axis_index("slide") % 2).reshape(1)
-    act, slope, mine2, other2 = pl.pallas_call(
-        hidden_kernel,
+
+    def once(*dims):
+        return pl.BlockSpec(dims, lambda s: (0,) * len(dims), pipeline_mode=pl.Buffered(1))
+
+    quarter_of = pl.BlockSpec((SIDE, *halves.shape[1:]), lambda j: (j, 0, 0))
+    live = once(1, MOST, rows, cols, chans)
+    mine1, other1, mine2, other2, d_filt, block_out, gain_grad, scale_grad = pl.pallas_call(
+        mlp_kernel,
         grid=(hidden // BLOCK,),
-        in_specs=[smem, whole(every, chans), whole(every, chans), rows_of],
-        out_specs=[wide_of, wide_of, whole(*halves.shape), whole(*halves.shape)],
-        out_shape=[shape((every, hidden), bf16), shape((every, hidden), bf16), halves, halves],
+        in_specs=[
+            smem,
+            smem,
+            once(every, chans),
+            once(every, chans),
+            pl.BlockSpec((BLOCK, chans), lambda j: (j, 0)),
+            pl.BlockSpec((chans, BLOCK), lambda j: (0, j)),
+            once(every, chans),
+            once(every, LANES),
+            once(1, chans),
+            once(1, chans),
+            live,
+            live,
+        ],
+        out_specs=[
+            quarter_of,
+            quarter_of,
+            once(*halves.shape),
+            once(*halves.shape),
+            once(every, chans),
+            once(*tiles.shape),
+            once(8, chans),
+            once(8, chans),
+        ],
+        out_shape=[
+            halves,
+            halves,
+            halves,
+            halves,
+            shape((every, chans), f32),
+            shape(tiles.shape, bf16),
+            shape((8, chans), f32),
+            shape((8, chans), f32),
+        ],
         scratch_shapes=[
             pltpu.VMEM((chans, every), bf16),
             pltpu.VMEM((chans // LANES, hidden, LANES), f32),
+            pltpu.VMEM((BLOCK, chans), bf16),
+            pltpu.VMEM((every, chans), f32),
+            pltpu.VMEM((every, chans), f32),
         ],
         compiler_params=params,
         cost_estimate=brief,
-        name="hidden",
-    )(core, normed, spread, fc1_weight)
-
-    act, other2 = after(act, other2)
-    got2 = from_other_core(other2)
-    block_out, scale_grad = pl.pallas_call(
-        out_kernel,
-        grid=(slots,),
-        in_specs=[
-            smem,
-            pl.BlockSpec((pixels, hidden), lambda s: (jnp.minimum(s, MOST - 1), 0)),
-            whole(chans, hidden),
-            tile_live,
-            tile_live,
-            whole(1, chans),
-        ],
-        out_specs=[tile, whole(8, chans)],
-        out_shape=[shape(tiles.shape, bf16), shape((8, chans), f32)],
-        compiler_params=params,
-        cost_estimate=brief,
-        name="outs",
-    )(tile_counts, act, fc2_weight, tiles, cotangent, scale)
-
-    mine2, got2, block_out = after(mine2, got2, block_out)
-    parts2 = quarters(mine2, got2)
-    slope, *parts2 = after(slope, *parts2)
-    ring2 = ring_sent(parts2)
-
-    quarter_of = pl.BlockSpec((SIDE, *halves.shape[1:]), lambda j: (j, 0, 0))
-    mine1, other1, d_filt, gain_grad = pl.pallas_call(
-        back_kernel,
-        grid=(hidden // BLOCK,),
-        in_specs=[
-            smem,
-            whole(every, chans),
-            whole(every, chans),
-            wide_of,
-            rows_of,
-            cols_of,
-            whole(every, chans),
-            whole(every, LANES),
-            whole(1, chans),
-        ],
-        out_specs=[quarter_of, quarter_of, whole(every, chans), whole(8, chans)],
-        out_shape=[halves, halves, shape((every, chans), f32), shape((8, chans), f32)],
-        scratch_shapes=[pltpu.VMEM((every, chans), f32), pltpu.VMEM((BLOCK, chans), bf16)],
-        compiler_params=params,
-        cost_estimate=brief,
-        name="back",
-    )(core, normed, spread, slope, fc1_weight, fc2_weight, unit, inv, gain)
-
-    sum2 = total_of(parts2[0], ring2)
-    other1, sum2 = after(other1, sum2)
-    got1 = from_other_core(other1)
+        name="mlp",
+    )(
+        core, tile_counts, normed, spread, fc1_weight, fc2_weight, unit, inv, gain, scale, tiles, cotangent
+    )
+
+    got2, got1 = from_other_core(other2), from_other_core(other1)
     d_cells = d_filt.reshape(MOST, rows, cols, chans)
     d_above, d_below = edges(d_cells.astype(bf16))
-    parts1 = quarters(mine1, got1)
-    d_filt, *parts1 = after(d_filt, *parts1)
-    ring1 = ring_sent(parts1)
 
     tap_grad = pl.pallas_call(
         tap_kernel,
@@ -506,9 +480,15 @@
     lines = -(-small.shape[0] // chips)
     small = jnp.pad(small, ((0, chips * lines - small.shape[0]), (0, 0)))
     small = jnp.pad(small.reshape(chips, lines, chans), ((0, 0), (0, -lines % 8), (0, 0)))
-    blocks = jnp.concatenate([sum2, total_of(parts1[0], ring1), small], axis=1)
-    blocks, d_above, d_below, d_filt = after(blocks, d_above, d_below, d_filt)
-    sums = plane_exchanged(blocks)
+    small, d_above, d_below, mine1, got1, mine2, got2 = after(
+        small, d_above, d_below, mine1, got1, mine2, got2
+    )
+    share = plane_exchanged(small)[:lines]
+    parts = quarters(mine2, got2) + quarters(mine1, got1)
+    ring2, ring1 = ring_sent(parts[:SIDE]), ring_sent(parts[SIDE:])
+    share, _, _ = after(share, parts[SIDE - 1], parts[-1])
+    share, d_filt, d_above, d_below = after(share, d_filt, d_above, d_below)
+    small = everywhere(share)
 
     grad_input = pl.pallas_call(
         input_kernel,
@@ -522,12 +502,13 @@
         name="inputs",
     )(tile_counts, d_filt, d_above, d_below, cotangent, taps)
 
+    grad_kernel = small[: TAPS * TAPS].reshape(dw_kernel.shape)
+    blocks = jnp.concatenate([total_of(parts[0], ring2), total_of(parts[SIDE], ring1)], axis=1)
+    blocks, small, grad_input = after(blocks, small, grad_input)
+    sums = plane_exchanged(blocks)
     own = hidden // (8 * chips)
     grad_fc2 = sums[:own].reshape(-1, hidden)
-    grad_fc1 = sums[own : 2 * own]
-    share, grad_input = after(sums[2 * own : 2 * own + lines], grad_input)
-    small = everywhere(share)
-    grad_kernel = small[: TAPS * TAPS].reshape(dw_kernel.shape)
+    grad_fc1 = sums[own:]
     return (
         block_out,
         grad_input,

time: 176 us -> 177 us (level)
  starting transfers between devices: 35.4 us -> 47.8 us
  waiting for transfers between devices: 28.5 us -> 19.4 us
  Pallas kernels: 85.9 us -> 78 us
  other arithmetic: 14.5 us -> 18.3 us
    all_to_all x1, waiting for transfers between devices: 14.7 us -> 0.01 us  [everywhere(): got = lax.all_to_all(sent, ('slide', 'row'), 0, 0, tiled=True)]
    all_to_all x1 -> x2, waiting for transfers between devices: 7.95 us -> 17.9 us  [plane_exchanged(): lax.all_to_all(blocks.reshape(-1, blocks.shape[-1]), ('slide', 'row'), 0,...]
    all_to_all x1 -> x2, starting transfers between devices: 6.4 us -> 14.6 us  [plane_exchanged(): lax.all_to_all(blocks.reshape(-1, blocks.shape[-1]), ('slide', 'row'), 0,...]
    pallas_call x3 -> x1, Pallas kernels: 46.3 us -> 38.3 us  [body(): pl.pallas_call(mlp_kernel, grid=(hidden // BLOCK,), in_specs=[smem, smem,...]
    all_to_all x1, starting transfers between devices: 3.55 us -> 11.3 us  [everywhere(): got = lax.all_to_all(sent, ('slide', 'row'), 0, 0, tiled=True)]
    ppermute x2, waiting for transfers between devices: 4.37 us -> 0.01 us  [from_other_core(): lax.ppermute(half, 'slide', [(i, i ^ 1) for i in range(lax.axis_size('sli...]
    convert_element_type x2, other arithmetic: 2 us -> 4.79 us  [total_of(): return total.astype(bf16).reshape(SIDE * SIDE, -1, own.shape[-1])]
    ppermute x2, starting transfers between devices: 4.15 us -> 1.74 us  [from_other_core(): lax.ppermute(half, 'slide', [(i, i ^ 1) for i in range(lax.axis_size('sli...]
  transfers between devices with their start and end apart: 14 -> 15, of which waited for: 5 -> 4; matrix products, arithmetic and copies ran while one was open for 6% -> 10% of each run, Pallas kernels for 30% -> 14%
where the time goes in v3:
time: 177 us; the launch traced here: 176 us
  Pallas kernels  78 us (44%)
  starting transfers between devices  47.8 us (27%)
  waiting for transfers between devices  19.4 us (11%)
  other arithmetic  18.3 us (10%)
  local copies, waits for them, and re-layouts  10.7 us (6%)
    pallas_call x1, Pallas kernels, body(): pl.pallas_call(mlp_kernel, grid=(hidden // BLOCK,), in_specs=[smem, smem,...  38.3 us
    all_to_all x2, waiting for transfers between devices, plane_exchanged(): lax.all_to_all(blocks.reshape(-1, blocks.shape[-1]), ('slide', 'row'), 0,...  17.9 us
    pallas_call x1, Pallas kernels, body(): pl.pallas_call(forward_kernel, grid=(MOST,), in_specs=[smem, tile, edge,...  15.6 us
    all_to_all x2, starting transfers between devices, plane_exchanged(): lax.all_to_all(blocks.reshape(-1, blocks.shape[-1]), ('slide', 'row'), 0,...  14.6 us
    pallas_call x1, Pallas kernels, body(): pl.pallas_call(input_kernel, grid=(slots,), in_specs=[smem, flat_live, ed...  13.3 us
    all_to_all x1, starting transfers between devices, everywhere(): got = lax.all_to_all(sent, ('slide', 'row'), 0, 0, tiled=True)  11.3 us
    pallas_call x1, Pallas kernels, body(): pl.pallas_call(tap_kernel, grid=(MOST,), in_specs=[tile, edge, edge, flat...  10.8 us
    ppermute x2, starting transfers between devices, edges(): above = lax.ppermute(tail, 'row', [(i, i + 1) for i in range(ends)])  9.76 us
  transfers between devices with their start and end apart: 15, of which 4 were waited for; matrix products, arithmetic and copies ran while one was open for 10% of the time, Pallas kernels for 14%

profile of v3, /device:TPU:1, one launch (start us, length us, event | category | flops | bytes accessed | tf_op | source)
XLA Modules:
  0.0 175.9 jit_solution(14242281513295310547)
XLA Ops:
  0.7 1.4 slice_bitcast_fusion
  2.1 1.3 collective-permute-start.1
  3.4 5.0 %collective-permute-start = (bf16[3,3,16,768]{3,2,1,0:T(8,128)(2,1)S(1)}, bf16[3,3,16,768]{3,2,1,0:T(8,128)(2,1)S(1)}, u32[]{:S(2)}, u32[]{:S(2)}) collective-permute-start(bf16[3,3,16,768]{3,2,1,0:T(8,128)(2,1)S(1)} %get-tuple-element.74), channel_id=1, source_target_pairs={{0,1},{1,2},{2,3},{4,5},{5,6},{6,7},{8,9},{9,10},{10,11},{12,13},{... | collective-permute-start | bytes 663560 | tf_op jit(solution)/shard_map/ppermute | solution.py:103
  13.2 15.6 %forward.1 = (bf16[768,768]{1,0:T(8,128)(2,1)}, f32[768,768]{1,0:T(8,128)}, f32[768,128]{1,0:T(8,128)}, bf16[768,768]{1,0:T(8,128)(2,1)}) custom-call(s32[1]{0:T(128)S(6)} %copy.15.count, bf16[1,4,16,16,768]{4,3,2,1,0:T(8,128)(2,1)} %tiles.5, bf16[3,3,16,768]{3,2,1,0:T(8,128)(2,1)} %copy-done.4, bf16[3,3,16,768]{3,2,1,0:T(8,128)(2,1)} %copy-done.3, ...), custom_call_target="tpu_custom_call" | custom-call | flops 1 | bytes 1 | tf_op jit(solution)/shard_map/forward/pallas_call | solution.py:384
  28.8 38.3 %mlp.1 = (bf16[16,96,768]{2,1,0:T(8,128)(2,1)}, bf16[16,96,768]{2,1,0:T(8,128)(2,1)}, bf16[16,96,768]{2,1,0:T(8,128)(2,1)}, bf16[16,96,768]{2,1,0:T(8,128)(2,1)}...) custom-call(s32[1]{0:T(128)} %bitcast.core, ...), custom_call_target="tpu_custom_call" | custom-call | flops 1 | bytes 1 | tf_op jit(solution)/shard_map/mlp/pallas_call | solution.py:410
  67.1 1.6 collective-permute-start.4
  68.9 1.8 %convert_element_type.128 = bf16[768,768]{1,0:T(8,128)(2,1)S(1)} convert(f32[768,768]{1,0:T(8,128)} %get-tuple-element.55.d_filt) | non-fusion elementwise | flops 589824 | bytes 3538944 | tf_op jit(solution)/shard_map/convert_element_type | solution.py:463
  71.4 1.3 collective-permute-start.3
  72.7 4.7 %collective-permute-start.2 = (bf16[3,3,16,768]{3,2,1,0:T(8,128)(2,1)S(1)}, bf16[3,3,16,768]{3,2,1,0:T(8,128)(2,1)S(1)}, u32[]{:S(2)}, u32[]{:S(2)}) collective-permute-start(bf16[3,3,16,768]{3,2,1,0:T(8,128)(2,1)S(1)} %get-tuple-element.72), channel_id=1, source_target_pairs={{0,1},{1,2},{2,3},{4,5},{5,6},{6,7},{8,9},{9,10},{10,11},{12,13},{... | collective-permute-start | bytes 663560 | tf_op jit(solution)/shard_map/ppermute | solution.py:103
  77.5 10.8 %taps.1 = f32[49,768]{1,0:T(8,128)} custom-call(bf16[1,4,16,16,768]{4,3,2,1,0:T(8,128)(2,1)} %tiles.5, bf16[3,3,16,768]{3,2,1,0:T(8,128)(2,1)} %copy-done.4, bf16[3,3,16,768]{3,2,1,0:T(8,128)(2,1)} %copy-done.3, f32[768,768]{1,0:T(8,128)} %get-tuple-element.55.d_filt), custom_call_target="tpu_custom_call" | custom-call | flops 1 | bytes 1 | tf_op jit(solution)/shard_map/taps/pallas_call | solution.py:465
  90.1 1.5 copy-done.1
  91.6 5.1 %add_convert_fusion.8 = (bf16[4,4,24,768]{3,2,1,0:T(8,128)(2,1)}, bf16[4,4,24,768]{3,2,1,0:T(8,128)(2,1)}, bf16[4,4,24,768]{3,2,1,0:T(8,128)(2,1)}) fusion(bf16[4,4,4,24,768]{4,3,2,1,0:T(8,128)(2,1)} %bitcast.6, s32[]{:T(128)S(6)} %select_n.186, bf16[4,4,4,24,768]{4,3,2,1,0:T(8,128)(2,1)} %bitcast.115, pred[]{:T(512)S(6)} %eq.42, s32[]{:T(128)S(6)} %select_n.190, ...), kind=kLoop, calls=%fused_computation.10 | loop fusion | flops 5308416 | bytes 8847373 | tf_op jit(solution)/shard_map/convert_element_type | solution.py:48
  96.7 1.5 collective-permute-start.6
  98.2 2.5 %collective-permute-start.7 = (bf16[4,4,24,768]{3,2,1,0:T(8,128)(2,1)}, bf16[4,4,24,768]{3,2,1,0:T(8,128)(2,1)}, u32[]{:S(2)}, u32[]{:S(2)}) collective-permute-start(bf16[4,4,24,768]{3,2,1,0:T(8,128)(2,1)} %get-tuple-element.66), channel_id=1, source_target_pairs={{0,2},{4,20},{1,3},{5,21},{2,0},{6,22},{3,1},{7,23},{8,10},{12,28}... | collective-permute-start | bytes 1769480 | tf_op jit(solution)/shard_map/ppermute | solution.py:64
  100.6 1.2 collective-permute-start.8
  101.8 7.4 %all-to-all-start = ((bf16[16,8,768]{2,1,0:T(8,128)(2,1)}), bf16[16,8,768]{2,1,0:T(8,128)(2,1)S(1)}, u32[]{:S(2)}, u32[]{:S(2)}) async-start(bf16[16,8,768]{2,1,0:T(8,128)(2,1)} %pad.9), calls=%async_computation | async-start | bytes 393216 | tf_op jit(solution)/shard_map/all_to_all | solution.py:78
  109.2 4.1 %add_convert_fusion.3 = (bf16[4,4,24,768]{3,2,1,0:T(8,128)(2,1)}, bf16[4,4,24,768]{3,2,1,0:T(8,128)(2,1)}, bf16[4,4,24,768]{3,2,1,0:T(8,128)(2,1)}) fusion(bf16[4,4,4,24,768]{4,3,2,1,0:T(8,128)(2,1)} %bitcast.113, s32[]{:T(128)S(6)} %select_n.186, bf16[4,4,4,24,768]{4,3,2,1,0:T(8,128)(2,1)S(1)} %bitcast.111, pred[]{:T(512)S(6)} %eq.42, s32[]{:T(128)S(6)} %select_n.190, ...), kind=kLoop, calls=%fused_computation.5 | loop fusion | flops 5308416 | bytes 8847373 | tf_op jit(solution)/shard_map/convert_element_type | solution.py:48
  114.4 1.6 collective-permute-start.11
  117.4 11.3 %all-to-all-start.1 = ((bf16[128,24,128]{2,1,0:T(8,128)(2,1)}), bf16[128,24,128]{2,1,0:T(8,128)(2,1)S(1)}, u32[]{:S(2)}, u32[]{:S(2)}) async-start(bf16[128,24,128]{2,1,0:T(8,128)(2,1)} %broadcast_in_dim.26), calls=%async_computation.1 | async-start | bytes 1572864 | tf_op jit(solution)/shard_map/all_to_all | solution.py:93
  128.7 13.3 %inputs.1 = f32[1,4,16,16,768]{4,3,2,1,0:T(8,128)} custom-call(s32[1]{0:T(128)S(6)} %copy.15.count, f32[768,768]{1,0:T(8,128)} %get-tuple-element.55.d_filt, bf16[3,3,16,768]{3,2,1,0:T(8,128)(2,1)} %copy-done.7, bf16[3,3,16,768]{3,2,1,0:T(8,128)(2,1)} %copy-done.6, bf16[1,4,16,16,768]{4,3,2,1,0:T(8,128)(2,1)} %cotan.5, f32[49,768]{1,0:T(8,128)} %reshape.82.kernel), custom_call_target="tpu_custom_call" | custom-call | flops 1 | bytes 1 | tf_op jit(solution)/shard_map/inputs/pallas_call | solution.py:493
  142.0 2.8 %add_convert_fusion.5 = bf16[4,4,24,768]{3,2,1,0:T(8,128)(2,1)S(1)} fusion(bf16[4,4,24,768]{3,2,1,0:T(8,128)(2,1)} %collective-permute-done.8, bf16[4,4,24,768]{3,2,1,0:T(8,128)(2,1)} %collective-permute-done.7, bf16[4,4,24,768]{3,2,1,0:T(8,128)(2,1)} %copy-done.5, bf16[4,4,4,24,768]{4,3,2,1,0:T(8,128)(2,1)} %bitcast.6, s32[]{:T(128)S(6)} %select_n.182, ...), kind=kLoop, calls=%fused_computation.7 | loop fusion | flops 4128768 | bytes 4718597 | tf_op jit(solution)/shard_map/convert_element_type | solution.py:71
  144.9 2.0 %add_convert_fusion = bf16[4,4,24,768]{3,2,1,0:T(8,128)(2,1)S(1)} fusion(bf16[4,4,24,768]{3,2,1,0:T(8,128)(2,1)} %collective-permute-done.11, bf16[4,4,24,768]{3,2,1,0:T(8,128)(2,1)} %collective-permute-done.10, bf16[4,4,24,768]{3,2,1,0:T(8,128)(2,1)} %collective-permute-done.9, bf16[4,4,4,24,768]{4,3,2,1,0:T(8,128)(2,1)S(1)} %bitcast.114, s32[]{:T(128)S(6)} %select_n.182, ...), kind=kLoop, calls=%fused_computation.2 | loop fusion | flops 4128768 | bytes 4718597 | tf_op jit(solution)/shard_map/convert_element_type | solution.py:71
  148.4 7.2 %all-to-all-start.2 = ((bf16[16,48,768]{2,1,0:T(8,128)(2,1)}), bf16[16,48,768]{2,1,0:T(8,128)(2,1)S(1)}, u32[]{:S(2)}, u32[]{:S(2)}) async-start(bf16[16,48,768]{2,1,0:T(8,128)(2,1)} %pad_maximum_fusion), calls=%async_computation.2 | async-start | bytes 2359296 | tf_op jit(solution)/shard_map/all_to_all | solution.py:78
  156.9 17.5 %all-to-all-done.2 = bf16[16,48,768]{2,1,0:T(8,128)(2,1)S(1)} async-done(((bf16[16,48,768]{2,1,0:T(8,128)(2,1)}), bf16[16,48,768]{2,1,0:T(8,128)(2,1)S(1)}, u32[]{:S(2)}, u32[]{:S(2)}) %all-to-all-start.2) | async-done | bytes 1179680 | tf_op jit(solution)/shard_map/all_to_all | solution.py:78
  (70 shorter events, 13.5 us)
Async XLA Ops:
  0.6 8.4 %copy-start.11 = (f32[768]{0:T(1024)S(1)}, f32[768]{0:T(1024)}, u32[]{:S(2)}) copy-start(f32[768]{0:T(1024)} %param.12) | copy-start | bytes 9220
  0.6 9.0 %copy-start.12 = (f32[768]{0:T(1024)S(1)}, f32[768]{0:T(1024)}, u32[]{:S(2)}) copy-start(f32[768]{0:T(1024)} %param.15) | copy-start | bytes 9220
  0.7 9.6 %copy-start.8 = (f32[7,7,768]{2,1,0:T(8,128)S(1)}, f32[7,7,768]{2,1,0:T(8,128)}, u32[]{:S(2)}) copy-start(f32[7,7,768]{2,1,0:T(8,128)} %param.11) | copy-start | bytes 451588
  2.1 9.5 %collective-permute-start.1 = (bf16[3,3,16,768]{3,2,1,0:T(8,128)(2,1)S(1)}, bf16[3,3,16,768]{3,2,1,0:T(8,128)(2,1)S(1)}, u32[]{:S(2)}, u32[]{:S(2)}) collective-permute-start(bf16[3,3,16,768]{3,2,1,0:T(8,128)(2,1)S(1)} %get-tuple-element.73), channel_id=1, source_target_pairs={{1,0},{2,1},{3,2},{5,4},{6,5},{7,6},{9,8},{10,9},{11,10},{13,12},{... | collective-permute-start | bytes 663560 | tf_op jit(solution)/shard_map/ppermute | solution.py:104
  3.4 9.1 %collective-permute-start = (bf16[3,3,16,768]{3,2,1,0:T(8,128)(2,1)S(1)}, bf16[3,3,16,768]{3,2,1,0:T(8,128)(2,1)S(1)}, u32[]{:S(2)}, u32[]{:S(2)}) collective-permute-start(bf16[3,3,16,768]{3,2,1,0:T(8,128)(2,1)S(1)} %get-tuple-element.74), channel_id=1, source_target_pairs={{0,1},{1,2},{2,3},{4,5},{5,6},{6,7},{8,9},{9,10},{10,11},{12,13},{... | collective-permute-start | bytes 663560 | tf_op jit(solution)/shard_map/ppermute | solution.py:103
  67.1 23.0 %collective-permute-start.4 = (bf16[16,96,768]{2,1,0:T(8,128)(2,1)}, bf16[16,96,768]{2,1,0:T(8,128)(2,1)S(1)}, u32[]{:S(2)}, u32[]{:S(2)}) collective-permute-start(bf16[16,96,768]{2,1,0:T(8,128)(2,1)} %get-tuple-element.43), channel_id=1, source_target_pairs={{0,4},{4,0},{8,12},{12,8},{16,20},{20,16},{24,28},{28,24},{32,36},... | collective-permute-start | bytes 7077896 | tf_op jit(solution)/shard_map/ppermute | solution.py:34
  68.8 21.3 %collective-permute-start.5 = (bf16[16,96,768]{2,1,0:T(8,128)(2,1)}, bf16[16,96,768]{2,1,0:T(8,128)(2,1)}, u32[]{:S(2)}, u32[]{:S(2)}) collective-permute-start(bf16[16,96,768]{2,1,0:T(8,128)(2,1)} %get-tuple-element.45), channel_id=1, source_target_pairs={{0,4},{4,0},{8,12},{12,8},{16,20},{20,16},{24,28},{28,24},{32,36},... | collective-permute-start | bytes 7077896 | tf_op jit(solution)/shard_map/ppermute | solution.py:34
  71.4 18.7 %collective-permute-start.3 = (bf16[3,3,16,768]{3,2,1,0:T(8,128)(2,1)}, bf16[3,3,16,768]{3,2,1,0:T(8,128)(2,1)S(1)}, u32[]{:S(2)}, u32[]{:S(2)}) collective-permute-start(bf16[3,3,16,768]{3,2,1,0:T(8,128)(2,1)} %get-tuple-element.71), channel_id=1, source_target_pairs={{1,0},{2,1},{3,2},{5,4},{6,5},{7,6},{9,8},{10,9},{11,10},{13,12},{... | collective-permute-start | bytes 663560 | tf_op jit(solution)/shard_map/ppermute | solution.py:104
  72.7 17.4 %collective-permute-start.2 = (bf16[3,3,16,768]{3,2,1,0:T(8,128)(2,1)S(1)}, bf16[3,3,16,768]{3,2,1,0:T(8,128)(2,1)S(1)}, u32[]{:S(2)}, u32[]{:S(2)}) collective-permute-start(bf16[3,3,16,768]{3,2,1,0:T(8,128)(2,1)S(1)} %get-tuple-element.72), channel_id=1, source_target_pairs={{0,1},{1,2},{2,3},{4,5},{5,6},{6,7},{8,9},{9,10},{10,11},{12,13},{... | collective-permute-start | bytes 663560 | tf_op jit(solution)/shard_map/ppermute | solution.py:103
  77.5 11.7 %copy-start.10 = (f32[8,768]{1,0:T(8,128)S(1)}, f32[8,768]{1,0:T(8,128)}, u32[]{:S(2)}) copy-start(f32[8,768]{1,0:T(8,128)} %get-tuple-element.40) | copy-start | bytes 73732
  77.5 11.7 %copy-start.9 = (f32[8,768]{1,0:T(8,128)S(1)}, f32[8,768]{1,0:T(8,128)}, u32[]{:S(2)}) copy-start(f32[8,768]{1,0:T(8,128)} %get-tuple-element.41) | copy-start | bytes 73732
  90.1 6.6 %copy-start.6 = (bf16[3,3,16,768]{3,2,1,0:T(8,128)(2,1)}, bf16[3,3,16,768]{3,2,1,0:T(8,128)(2,1)S(1)}, u32[]{:S(2)}) copy-start(bf16[3,3,16,768]{3,2,1,0:T(8,128)(2,1)S(1)} %collective-permute-done.3.below) | copy-start | bytes 663556
  90.1 6.6 %copy-start.7 = (bf16[3,3,16,768]{3,2,1,0:T(8,128)(2,1)}, bf16[3,3,16,768]{3,2,1,0:T(8,128)(2,1)S(1)}, u32[]{:S(2)}) copy-start(bf16[3,3,16,768]{3,2,1,0:T(8,128)(2,1)S(1)} %collective-permute-done.2.above) | copy-start | bytes 663556
  91.6 17.6 %copy-start = (bf16[16,96,768]{2,1,0:T(8,128)(2,1)S(1)}, bf16[16,96,768]{2,1,0:T(8,128)(2,1)}, u32[]{:S(2)}) copy-start(bf16[16,96,768]{2,1,0:T(8,128)(2,1)} %get-tuple-element.48) | copy-start | bytes 7077892
  96.7 17.7 %collective-permute-start.6 = (bf16[4,4,24,768]{3,2,1,0:T(8,128)(2,1)}, bf16[4,4,24,768]{3,2,1,0:T(8,128)(2,1)S(1)}, u32[]{:S(2)}, u32[]{:S(2)}) collective-permute-start(bf16[4,4,24,768]{3,2,1,0:T(8,128)(2,1)} %get-tuple-element.65), channel_id=1, source_target_pairs={{0,1},{4,12},{1,2},{5,13},{2,3},{6,14},{3,0},{7,15},{8,9},{12,20},... | collective-permute-start | bytes 1769480 | tf_op jit(solution)/shard_map/ppermute | solution.py:64
  98.2 43.9 %collective-permute-start.7 = (bf16[4,4,24,768]{3,2,1,0:T(8,128)(2,1)}, bf16[4,4,24,768]{3,2,1,0:T(8,128)(2,1)}, u32[]{:S(2)}, u32[]{:S(2)}) collective-permute-start(bf16[4,4,24,768]{3,2,1,0:T(8,128)(2,1)} %get-tuple-element.66), channel_id=1, source_target_pairs={{0,2},{4,20},{1,3},{5,21},{2,0},{6,22},{3,1},{7,23},{8,10},{12,28}... | collective-permute-start | bytes 1769480 | tf_op jit(solution)/shard_map/ppermute | solution.py:64
  100.6 41.4 %collective-permute-start.8 = (bf16[4,4,24,768]{3,2,1,0:T(8,128)(2,1)}, bf16[4,4,24,768]{3,2,1,0:T(8,128)(2,1)}, u32[]{:S(2)}, u32[]{:S(2)}) collective-permute-start(bf16[4,4,24,768]{3,2,1,0:T(8,128)(2,1)} %get-tuple-element.67), channel_id=1, source_target_pairs={{0,3},{4,28},{1,0},{5,29},{2,1},{6,30},{3,2},{7,31},{8,11},{12,4},... | collective-permute-start | bytes 1769480 | tf_op jit(solution)/shard_map/ppermute | solution.py:64
  101.8 14.6 %all-to-all-start = ((bf16[16,8,768]{2,1,0:T(8,128)(2,1)}), bf16[16,8,768]{2,1,0:T(8,128)(2,1)S(1)}, u32[]{:S(2)}, u32[]{:S(2)}) async-start(bf16[16,8,768]{2,1,0:T(8,128)(2,1)} %pad.9), calls=%async_computation | async-start | bytes 393216 | tf_op jit(solution)/shard_map/all_to_all | solution.py:78
  113.3 31.6 %collective-permute-start.9 = (bf16[4,4,24,768]{3,2,1,0:T(8,128)(2,1)}, bf16[4,4,24,768]{3,2,1,0:T(8,128)(2,1)}, u32[]{:S(2)}, u32[]{:S(2)}) collective-permute-start(bf16[4,4,24,768]{3,2,1,0:T(8,128)(2,1)} %get-tuple-element.68), channel_id=1, source_target_pairs={{0,1},{4,12},{1,2},{5,13},{2,3},{6,14},{3,0},{7,15},{8,9},{12,20},... | collective-permute-start | bytes 1769480 | tf_op jit(solution)/shard_map/ppermute | solution.py:64
  113.5 31.4 %collective-permute-start.10 = (bf16[4,4,24,768]{3,2,1,0:T(8,128)(2,1)}, bf16[4,4,24,768]{3,2,1,0:T(8,128)(2,1)}, u32[]{:S(2)}, u32[]{:S(2)}) collective-permute-start(bf16[4,4,24,768]{3,2,1,0:T(8,128)(2,1)} %get-tuple-element.69), channel_id=1, source_target_pairs={{0,2},{4,20},{1,3},{5,21},{2,0},{6,22},{3,1},{7,23},{8,10},{12,28}... | collective-permute-start | bytes 1769480 | tf_op jit(solution)/shard_map/ppermute | solution.py:64
  114.4 3.1 %copy-start.5 = (bf16[4,4,24,768]{3,2,1,0:T(8,128)(2,1)}, bf16[4,4,24,768]{3,2,1,0:T(8,128)(2,1)S(1)}, u32[]{:S(2)}) copy-start(bf16[4,4,24,768]{3,2,1,0:T(8,128)(2,1)S(1)} %collective-permute-done.6) | copy-start | bytes 1769476
  114.4 30.5 %collective-permute-start.11 = (bf16[4,4,24,768]{3,2,1,0:T(8,128)(2,1)}, bf16[4,4,24,768]{3,2,1,0:T(8,128)(2,1)}, u32[]{:S(2)}, u32[]{:S(2)}) collective-permute-start(bf16[4,4,24,768]{3,2,1,0:T(8,128)(2,1)} %get-tuple-element.70), channel_id=1, source_target_pairs={{0,3},{4,28},{1,0},{5,29},{2,1},{6,30},{3,2},{7,31},{8,11},{12,4},... | collective-permute-start | bytes 1769480 | tf_op jit(solution)/shard_map/ppermute | solution.py:64
  117.4 30.6 %all-to-all-start.1 = ((bf16[128,24,128]{2,1,0:T(8,128)(2,1)}), bf16[128,24,128]{2,1,0:T(8,128)(2,1)S(1)}, u32[]{:S(2)}, u32[]{:S(2)}) async-start(bf16[128,24,128]{2,1,0:T(8,128)(2,1)} %broadcast_in_dim.26), calls=%async_computation.1 | async-start | bytes 1572864 | tf_op jit(solution)/shard_map/all_to_all | solution.py:93
  148.4 26.1 %all-to-all-start.2 = ((bf16[16,48,768]{2,1,0:T(8,128)(2,1)}), bf16[16,48,768]{2,1,0:T(8,128)(2,1)S(1)}, u32[]{:S(2)}, u32[]{:S(2)}) async-start(bf16[16,48,768]{2,1,0:T(8,128)(2,1)} %pad_maximum_fusion), calls=%async_computation.2 | async-start | bytes 2359296 | tf_op jit(solution)/shard_map/all_to_all | solution.py:78
  (4 other events, 6.0 us)

commit v4 on v3

--- a/solution.py
+++ b/solution.py
@@ -16,7 +16,7 @@
 TAPS = 7
 LEFT = 8
 LANES = 128
-MOST = 3
+WORK = 2
 BLOCK = 768
 SIDE = 4
 PITCH = 24
@@ -39,11 +39,7 @@
     own = jnp.where(core == 0, lax.axis_index("row"), lax.axis_index("slide") // 2 % SIDE)
 
     def cut(half, by):
-        cells = half.reshape(SIDE, SIDE, SIDE, -1, half.shape[-1])
-        at = (own + by) % SIDE
-        along_z = lax.dynamic_index_in_dim(cells, at, 2, keepdims=False)
-        along_x = lax.dynamic_index_in_dim(cells, at, 1, keepdims=False)
-        return jnp.where(core == 0, along_z, along_x).astype(f32)
+        return lax.dynamic_index_in_dim(half, (own + by) % SIDE, 0, keepdims=False).astype(f32)
 
     return [(cut(mine, by) + cut(got, by)).astype(bf16) for by in range(SIDE)]
 
@@ -96,10 +92,8 @@
     return whole.reshape(-1, share.shape[-1])
 
 
-def edges(cells):
+def edges(head, tail):
     ends = lax.axis_size("row") - 1
-    head = cells[:, :REACH]
-    tail = cells[:, cells.shape[1] - REACH :]
     above = lax.ppermute(tail, "row", [(i, i + 1) for i in range(ends)])
     below = lax.ppermute(head, "row", [(i + 1, i) for i in range(ends)])
     return above, below
@@ -160,18 +154,15 @@
 
 
 def forward_kernel(
-    count, tiles, above, below, cotan, kernel, gain, scale, normed, unit, spread, held_out, pad, wide, filt
+    tiles, above, below, cotan, kernel, gain, scale, *refs
 ):
-    slot = pl.program_id(0)
-    rows, cols, chans = tiles.shape[2:]
-
-    @pl.when(slot == 0)
-    def _():
-        spread_kernel(wide, kernel)
-        clear_padded(pad)
+    normed, unit, spread, held_out, pad, wide, filt = refs[-7:]
+    rows, cols, chans = tiles.shape[1:]
+    spread_kernel(wide, kernel)
+    clear_padded(pad)
 
     def line_of(r, lanes):
-        return tiles[0, 0, r, :, lanes]
+        return tiles[0, r, :, lanes]
 
     fill_padded(pad, above, line_of, below, rows, cols, chans)
 
@@ -179,8 +170,7 @@
         filt[pl.ds(p * cols + 8 * half, 8), lanes] = value
 
     stencil(pad, wide, rows, cols, chans, False, emit)
-    weight = (slot < count[0]).astype(f32)
-    held = cotan[...].reshape(rows * cols, chans).astype(f32) * weight
+    held = cotan[...].reshape(rows * cols, chans).astype(f32)
     held_out[...] = (held * scale[...]).astype(bf16)
 
     def norm(i, carry):
@@ -209,21 +199,23 @@
     return jnp.where(pre < 0.0, tail, 1.0 - tail), bell * density
 
 
-def split_rows(core, mine, other, rows_at):
-    count = mine.shape[1]
-    for chip in range(mine.shape[0]):
-        for half, which in ((mine, core[0]), (other, 1 - core[0])):
-            rows_at(half, chip, pl.ds(pl.multiple_of((2 * chip + which) * count, 32), count))
+def split_rows(core, mine, other, y, first, rows_at):
+    count = mine.shape[3]
+    for x, z in itertools.product(range(SIDE), repeat=2):
+        flipped = [jnp.where(core[0] == 0, *pair) for pair in ((z, x), (x, z))]
+        for half, which, at in ((mine, core[0], flipped), (other, 1 - core[0], flipped[::-1])):
+            begin = pl.multiple_of(first + ((2 * x + which) * SIDE + z) * count, 8)
+            rows_at(half, (at[0], y, at[1]), pl.ds(begin, count))
 
 
 def mlp_kernel(
-    core, count, normed, spread, first, second, unit, inv, gain, scale, tiles, cotan,
-    mine1, other1, mine2, other2, d_filt, out, gain_grad, scale_grad,
+    core, normed, spread, first, second, unit, inv, gain, scale, tiles, cotan,
+    mine1, other1, mine2, other2, d_filt, d_head, d_tail, out, gain_grad, scale_grad,
     turned, total2, term, back, branch,
 ):
     step = pl.program_id(0)
     pixels, chans = normed.shape
-    rows, cols = tiles.shape[2:4]
+    rows, cols = tiles.shape[1:3]
 
     @pl.when(step == 0)
     def _():
@@ -246,21 +238,26 @@
     )
     term[...] = lax.dot_general(
         d_pre, normed[...], (((0,), (0,)), ((), ())), preferred_element_type=f32
-    ).astype(bf16)
+    )
 
     def copy1(half, chip, at):
-        half[chip] = term[at, :]
-
-    split_rows(core, mine1, other1, copy1)
+        half[chip] = term[at, :].astype(bf16)
+
+    split_rows(core, mine1, other1, 0, 0, copy1)
     back[...] += jnp.dot(d_pre, first[...], preferred_element_type=f32)
 
     @pl.when(step == pl.num_programs(0) - 1)
     def _():
         def copy2(half, chip, at):
             for i in range(BLOCK // LANES):
-                half[chip, :, i * LANES : (i + 1) * LANES] = total2[i, at, :].astype(bf16)
-
-        split_rows(core, mine2, other2, copy2)
+                lanes = slice(i * LANES, (i + 1) * LANES)
+                half[(*chip, slice(None), lanes)] = total2[i, at, :].astype(bf16)
+
+        def over(y, carry):
+            split_rows(core, mine2, other2, y, y * (total2.shape[1] // SIDE), copy2)
+            return carry
+
+        lax.fori_loop(0, SIDE, over, 0)
         lines = 64 // cols
 
         def finish(i, kept):
@@ -273,24 +270,28 @@
             along = jnp.mean(scaled * one, axis=-1, keepdims=True)
             d_filt[at, :] = inv[at, 0:1] * (scaled - mean - one * along)
             slot = i * lines // rows
-            weight = (slot < count[0]).astype(f32)
             line = pl.ds(i * lines - slot * rows, lines)
             value = branch[at, :]
-            held = cotan[0, slot, line].reshape(64, chans).astype(f32) * weight
+            held = cotan[slot, line].reshape(64, chans).astype(f32)
             scales = scales + jnp.sum((held * value).reshape(8, 8, chans), axis=0)
-            cells = tiles[0, slot, line].reshape(64, chans).astype(f32)
-            filled = ((cells + scale[...] * value) * weight).astype(bf16)
-            out[0, slot, line] = filled.reshape(lines, cols, chans)
+            cells = tiles[slot, line].reshape(64, chans).astype(f32)
+            filled = (cells + scale[...] * value).astype(bf16)
+            out[slot, line] = filled.reshape(lines, cols, chans)
             return gains, scales
 
         start = jnp.zeros((8, chans), f32)
         gain_grad[...], scale_grad[...] = lax.fori_loop(0, pixels // 64, finish, (start, start))
-        out[0, MOST:] = jnp.zeros((out.shape[1] - MOST, rows, cols, chans), bf16)
-
-
-def tap_kernel(tiles, above, below, d_filt, grad, pad, total):
+        for slot in range(WORK):
+            begin, end = slot * rows * cols, (slot + 1) * rows * cols
+            ends = (REACH, cols, chans)
+            d_head[slot] = d_filt[begin : begin + REACH * cols, :].reshape(ends).astype(bf16)
+            d_tail[slot] = d_filt[end - REACH * cols : end, :].reshape(ends).astype(bf16)
+
+
+def tap_kernel(tiles, above, below, d_filt, gains, scales, small, pad, total, lines):
     slot = pl.program_id(0)
-    rows, cols, chans = tiles.shape[2:]
+    rows, cols, chans = tiles.shape[1:]
+    share = -(-(TAPS * TAPS + 2) // small.shape[0])
 
     @pl.when(slot == 0)
     def _():
@@ -298,7 +299,7 @@
         total[...] = jnp.zeros_like(total)
 
     def line_of(r, lanes):
-        return tiles[0, 0, r, :, lanes]
+        return tiles[0, r, :, lanes]
 
     fill_padded(pad, above, line_of, below, rows, cols, chans)
 
@@ -317,46 +318,65 @@
 
     @pl.when(slot == pl.num_programs(0) - 1)
     def _():
-        for tap in range(TAPS * TAPS):
-            grad[tap : tap + 1, :] = jnp.sum(total[tap], axis=0, keepdims=True)
-
-
-def input_kernel(count, d_filt, above, below, cotan, kernel, out, pad, wide):
-    slot = pl.program_id(0)
-    rows, cols, chans = out.shape[2:]
-
-    @pl.when(slot == 0)
+        lines[...] = jnp.zeros_like(lines)
+        for i in range(TAPS * TAPS + 2):
+            value = total[i] if i < TAPS * TAPS else (gains, scales)[i - TAPS * TAPS][...]
+            at = i // share * small.shape[1] + i % share
+            lines[at : at + 1, :] = jnp.sum(value, axis=0, keepdims=True)
+        for i in range(small.shape[0]):
+            small[i] = lines[i * small.shape[1] : (i + 1) * small.shape[1], :].astype(bf16)
+
+
+def input_kernel(d_filt, above, below, cotan, kernel, out, sent, pad, wide):
+    rows, cols, chans = out.shape[1:]
+
+    @pl.when(pl.program_id(0) == 0)
     def _():
         spread_kernel(wide, kernel)
         clear_padded(pad)
 
-    @pl.when(slot < MOST)
-    def _():
-        def line_of(r, lanes):
-            return d_filt[pl.ds(r * cols, cols), lanes]
-
-        fill_padded(pad, above, line_of, below, rows, cols, chans)
-        weight = (slot < count[0]).astype(f32)
-
-        def emit(p, half, lanes, value):
-            at = pl.ds(8 * half, 8)
-            out[0, 0, p, at, lanes] = value + cotan[0, 0, p, at, lanes].astype(f32) * weight
-
-        stencil(pad, wide, rows, cols, chans, True, emit)
-
-    @pl.when(slot >= MOST)
-    def _():
-        out[...] = jnp.zeros_like(out)
+    def line_of(r, lanes):
+        return d_filt[pl.ds(r * cols, cols), lanes]
+
+    fill_padded(pad, above, line_of, below, rows, cols, chans)
+
+    def emit(p, half, lanes, value):
+        at = pl.ds(8 * half, 8)
+        out[0, p, at, lanes] = value + cotan[0, p, at, lanes].astype(f32)
+
+    stencil(pad, wide, rows, cols, chans, True, emit)
+    sent[...] = out[...].astype(bf16)
+
+
+def to_partner(cells):
+    slides = lax.axis_size("slide")
+    return lax.ppermute(cells, "slide", [(i, (i + slides // 2) % slides) for i in range(slides)])
+
+
+def all_slots(done, returned, count, slots):
+    first, second = done[0], done[1]
+    third = returned.astype(done.dtype)
+    none = jnp.zeros_like(first)
+    kept = [first, jnp.where(count >= 2, second, none), jnp.where(count >= 3, third, none)]
+    return jnp.stack(kept + [none] * (slots - len(kept)))[None]
 
 
 def body(tiles, cotangent, tile_counts, dw_kernel, ln_gain, fc1_weight, fc2_weight, layer_scale):
     _, slots, rows, cols, chans = tiles.shape
     hidden = fc1_weight.shape[0]
     pixels = rows * cols
-    every = MOST * pixels
+    every = WORK * pixels
+    count = tile_counts[0]
+    lone = tiles[0, :1]
+    above0, below0 = edges(lone[:, :REACH], lone[:, rows - REACH :])
+    moved = to_partner(tiles[0, 2]), to_partner(cotangent[0, 2])
+    second_tile, second_cotan = (
+        jnp.where(count >= 2, own[0, 1], came)[None]
+        for own, came in zip((tiles, cotangent), moved, strict=True)
+    )
+    above1, below1 = edges(second_tile[:, :REACH], second_tile[:, rows - REACH :])
     taps = dw_kernel.reshape(TAPS * TAPS, chans)
     gain, scale = ln_gain[None], layer_scale[None]
-    above, below = edges(tiles[0, :MOST])
 
     params = pltpu.CompilerParams(
         vmem_limit_bytes=60 * 1024 * 1024, dimension_semantics=("arbitrary",)
@@ -364,16 +384,9 @@
     shape = jax.ShapeDtypeStruct
     brief = pl.CostEstimate(flops=1, bytes_accessed=1, transcendentals=0)
     smem = pl.BlockSpec(memory_space=pltpu.SMEM)
-    tile = pl.BlockSpec((1, 1, rows, cols, chans), lambda s: (0, s, 0, 0, 0))
-    tile_live = pl.BlockSpec(
-        (1, 1, rows, cols, chans), lambda s: (0, jnp.minimum(s, MOST - 1), 0, 0, 0)
-    )
+    tile = pl.BlockSpec((1, rows, cols, chans), lambda s: (s, 0, 0, 0))
     edge = pl.BlockSpec((1, REACH, cols, chans), lambda s: (s, 0, 0, 0))
-    edge_live = pl.BlockSpec(
-        (1, REACH, cols, chans), lambda s: (jnp.minimum(s, MOST - 1), 0, 0, 0)
-    )
     flat = pl.BlockSpec((pixels, chans), lambda s: (s, 0))
-    flat_live = pl.BlockSpec((pixels, chans), lambda s: (jnp.minimum(s, MOST - 1), 0))
 
     def whole(*dims):
         return pl.BlockSpec(dims, lambda s: (0,) * len(dims))
@@ -381,37 +394,49 @@
     pad = pltpu.VMEM((chans // LANES, (rows + 2 * REACH) * PITCH + 8, LANES), f32)
     wide = pltpu.VMEM((TAPS * TAPS, 8, chans), f32)
 
-    normed, unit, inv, spread = pl.pallas_call(
-        forward_kernel,
-        grid=(MOST,),
-        in_specs=[smem, tile, edge, edge, tile, whole(TAPS * TAPS, chans), whole(1, chans), whole(1, chans)],
-        out_specs=[flat, flat, pl.BlockSpec((pixels, LANES), lambda s: (s, 0)), flat],
-        out_shape=[
-            shape((every, chans), bf16),
-            shape((every, chans), f32),
-            shape((every, LANES), f32),
-            shape((every, chans), bf16),
-        ],
-        scratch_shapes=[pad, wide, pltpu.VMEM((pixels, chans), f32)],
-        compiler_params=params,
-        cost_estimate=brief,
-        name="forward",
-    )(tile_counts, tiles, above, below, cotangent, taps, gain, scale)
+    def forward(at, tile_in, above, below, cotan, earlier):
+        one = pl.BlockSpec((1, rows, cols, chans), lambda s: (0, 0, 0, 0))
+        line = pl.BlockSpec((1, REACH, cols, chans), lambda s: (0, 0, 0, 0))
+        block = pl.BlockSpec((pixels, chans), lambda s: (at, 0))
+        return pl.pallas_call(
+            forward_kernel,
+            grid=(1,),
+            in_specs=[one, line, line, one, whole(TAPS * TAPS, chans), whole(1, chans), whole(1, chans)]
+            + [pl.BlockSpec(memory_space=pl.ANY)] * len(earlier),
+            out_specs=[block, block, pl.BlockSpec((pixels, LANES), lambda s: (at, 0)), block],
+            out_shape=[
+                shape((every, chans), bf16),
+                shape((every, chans), f32),
+                shape((every, LANES), f32),
+                shape((every, chans), bf16),
+            ],
+            scratch_shapes=[pad, wide, pltpu.VMEM((pixels, chans), f32)],
+            input_output_aliases={7 + i: i for i in range(len(earlier))},
+            compiler_params=params,
+            cost_estimate=brief,
+            name="forward",
+        )(tile_in, above, below, cotan, taps, gain, scale, *earlier)
+
+    earlier = forward(0, lone, above0, below0, cotangent[0, :1], [])
+    normed, unit, inv, spread = forward(1, second_tile, above1, below1, second_cotan, earlier)
+    above, below = jnp.concatenate([above0, above1]), jnp.concatenate([below0, below1])
+    cotangent = jnp.concatenate([cotangent[0, :1], second_cotan])
+    tiles = jnp.concatenate([lone, second_tile])
 
     chips = SIDE * SIDE
-    halves = shape((chips, hidden // (2 * chips), chans), bf16)
+    halves = shape((SIDE, SIDE, SIDE, hidden // (8 * chips), chans), bf16)
+    d_edge = shape((WORK, REACH, cols, chans), bf16)
     core = (lax.axis_index("slide") % 2).reshape(1)
 
     def once(*dims):
         return pl.BlockSpec(dims, lambda s: (0,) * len(dims), pipeline_mode=pl.Buffered(1))
 
-    quarter_of = pl.BlockSpec((SIDE, *halves.shape[1:]), lambda j: (j, 0, 0))
-    live = once(1, MOST, rows, cols, chans)
-    mine1, other1, mine2, other2, d_filt, block_out, gain_grad, scale_grad = pl.pallas_call(
+    quarter_of = pl.BlockSpec((SIDE, 1, *halves.shape[2:]), lambda j: (0, j, 0, 0, 0))
+    live = once(*tiles.shape)
+    mine1, other1, mine2, other2, d_filt, d_head, d_tail, block_out, gain_grad, scale_grad = pl.pallas_call(
         mlp_kernel,
         grid=(hidden // BLOCK,),
         in_specs=[
-            smem,
             smem,
             once(every, chans),
             once(every, chans),
@@ -430,6 +455,8 @@
             once(*halves.shape),
             once(*halves.shape),
             once(every, chans),
+            once(*d_edge.shape),
+            once(*d_edge.shape),
             once(*tiles.shape),
             once(8, chans),
             once(8, chans),
@@ -440,6 +467,8 @@
             halves,
             halves,
             shape((every, chans), f32),
+            d_edge,
+            d_edge,
             shape(tiles.shape, bf16),
             shape((8, chans), f32),
             shape((8, chans), f32),
@@ -447,7 +476,7 @@
         scratch_shapes=[
             pltpu.VMEM((chans, every), bf16),
             pltpu.VMEM((chans // LANES, hidden, LANES), f32),
-            pltpu.VMEM((BLOCK, chans), bf16),
+            pltpu.VMEM((BLOCK, chans), f32),
             pltpu.VMEM((every, chans), f32),
             pltpu.VMEM((every, chans), f32),
         ],
@@ -455,31 +484,26 @@
         cost_estimate=brief,
         name="mlp",
     )(
-        core, tile_counts, normed, spread, fc1_weight, fc2_weight, unit, inv, gain, scale, tiles, cotangent
+        core, normed, spread, fc1_weight, fc2_weight, unit, inv, gain, scale, tiles, cotangent
     )
 
     got2, got1 = from_other_core(other2), from_other_core(other1)
-    d_cells = d_filt.reshape(MOST, rows, cols, chans)
-    d_above, d_below = edges(d_cells.astype(bf16))
-
-    tap_grad = pl.pallas_call(
+    d_above, d_below = edges(d_head, d_tail)
+
+    lines = -(-(TAPS * TAPS + 2) // chips)
+    small = shape((chips, -(-lines // 8) * 8, chans), bf16)
+    small = pl.pallas_call(
         tap_kernel,
-        grid=(MOST,),
-        in_specs=[tile, edge, edge, flat],
-        out_specs=whole(TAPS * TAPS, chans),
-        out_shape=shape((TAPS * TAPS, chans), f32),
-        scratch_shapes=[pad, wide],
+        grid=(WORK,),
+        in_specs=[tile, edge, edge, flat, whole(8, chans), whole(8, chans)],
+        out_specs=whole(*small.shape),
+        out_shape=small,
+        scratch_shapes=[pad, wide, pltpu.VMEM((chips * small.shape[1], chans), f32)],
         compiler_params=params,
         cost_estimate=brief,
         name="taps",
-    )(tiles, above, below, d_filt)
-
-    scale_row = jnp.sum(scale_grad, axis=0)
-    gain_row = jnp.sum(gain_grad, axis=0)
-    small = jnp.concatenate([tap_grad, gain_row[None], scale_row[None]]).astype(bf16)
-    lines = -(-small.shape[0] // chips)
-    small = jnp.pad(small, ((0, chips * lines - small.shape[0]), (0, 0)))
-    small = jnp.pad(small.reshape(chips, lines, chans), ((0, 0), (0, -lines % 8), (0, 0)))
+    )(tiles, above, below, d_filt, gain_grad, scale_grad)
+
     small, d_above, d_below, mine1, got1, mine2, got2 = after(
         small, d_above, d_below, mine1, got1, mine2, got2
     )
@@ -487,24 +511,28 @@
     parts = quarters(mine2, got2) + quarters(mine1, got1)
     ring2, ring1 = ring_sent(parts[:SIDE]), ring_sent(parts[SIDE:])
     share, _, _ = after(share, parts[SIDE - 1], parts[-1])
-    share, d_filt, d_above, d_below = after(share, d_filt, d_above, d_below)
+    block_back = to_partner(block_out[1])
+    share, d_filt, d_above, d_below, block_back = after(share, d_filt, d_above, d_below, block_back)
     small = everywhere(share)
 
-    grad_input = pl.pallas_call(
+    grad_input, grad_sent = pl.pallas_call(
         input_kernel,
-        grid=(slots,),
-        in_specs=[smem, flat_live, edge_live, edge_live, tile_live, whole(TAPS * TAPS, chans)],
-        out_specs=tile,
-        out_shape=shape(tiles.shape, f32),
+        grid=(WORK,),
+        in_specs=[flat, edge, edge, tile, whole(TAPS * TAPS, chans)],
+        out_specs=[tile, whole(1, rows, cols, chans)],
+        out_shape=[shape(tiles.shape, f32), shape((1, rows, cols, chans), bf16)],
         scratch_shapes=[pad, wide],
         compiler_params=params,
         cost_estimate=brief,
         name="inputs",
-    )(tile_counts, d_filt, d_above, d_below, cotangent, taps)
+    )(d_filt, d_above, d_below, cotangent, taps)
 
     grad_kernel = small[: TAPS * TAPS].reshape(dw_kernel.shape)
     blocks = jnp.concatenate([total_of(parts[0], ring2), total_of(parts[SIDE], ring1)], axis=1)
-    blocks, small, grad_input = after(blocks, small, grad_input)
+    blocks, small, grad_input, grad_sent = after(blocks, small, grad_input, grad_sent)
+    grad_back = to_partner(grad_sent[0])
+    block_out = all_slots(block_out, block_back, count, slots)
+    grad_input = all_slots(grad_input, grad_back, count, slots)
     sums = plane_exchanged(blocks)
     own = hidden // (8 * chips)
     grad_fc2 = sums[:own].reshape(-1, hidden)

time: 177 us -> 178 us (level)
  Pallas kernels: 78 us -> 59.6 us
  starting transfers between devices: 47.8 us -> 58 us
  other arithmetic: 18.3 us -> 22.9 us
  waiting for transfers between devices: 19.4 us -> 21.8 us
  local copies, waits for them, and re-layouts: 10.7 us -> 13 us
    ppermute x0 -> x4, waiting for transfers between devices: none -> 18.5 us  [to_partner(): lax.ppermute(cells, 'slide', [(i, (i + slides // 2) % slides) for i in ra...]
    pallas_call x4 -> x5, Pallas kernels: 78 us -> 59.6 us  [the longest x1 28.5 us: body(): pl.pallas_call(mlp_kernel, grid=(hidden // BLOCK,), in_specs=[smem, once(...]
    all_to_all x2, waiting for transfers between devices: 17.9 us -> 1.48 us  [plane_exchanged(): lax.all_to_all(blocks.reshape(-1, blocks.shape[-1]), ('slide', 'row'), 0,...]
    ppermute x0 -> x4, starting transfers between devices: none -> 9.66 us  [to_partner(): lax.ppermute(cells, 'slide', [(i, (i + slides // 2) % slides) for i in ra...]
    concatenate x1 -> x4, other arithmetic: 0.02 us -> 5.14 us  [the longest x1 1.57 us: body(): jnp.concatenate([below0, below1])]
    broadcast_in_dim x0 -> x4, other arithmetic: none -> 4.44 us  [the longest x2 3.31 us: all_slots(): return jnp.stack(kept + [none] * (slots - len(kept)))[None]]
    ppermute x2 -> x3, starting transfers between devices: 9.76 us -> 12.6 us  [edges(): above = lax.ppermute(tail, 'row', [(i, i + 1) for i in range(ends)])]
    all_to_all x2, starting transfers between devices: 14.6 us -> 11.9 us  [plane_exchanged(): lax.all_to_all(blocks.reshape(-1, blocks.shape[-1]), ('slide', 'row'), 0,...]
  transfers between devices with their start and end apart: 15 -> 21, of which waited for: 4 -> 3; matrix products, arithmetic and copies ran while one was open for 10% -> 15% of each run, Pallas kernels for 14% -> 14%
where the time goes in v4:
time: 178 us; the launch traced here: 177 us
  Pallas kernels  59.6 us (33%)
  starting transfers between devices  58 us (33%)
  other arithmetic  22.9 us (13%)
  waiting for transfers between devices  21.8 us (12%)
  local copies, waits for them, and re-layouts  13 us (7%)
    pallas_call x1, Pallas kernels, body(): pl.pallas_call(mlp_kernel, grid=(hidden // BLOCK,), in_specs=[smem, once(...  28.5 us
    ppermute x4, waiting for transfers between devices, to_partner(): lax.ppermute(cells, 'slide', [(i, (i + slides // 2) % slides) for i in ra...  18.5 us
    pallas_call x2, Pallas kernels, forward(): pl.pallas_call(forward_kernel, grid=(1,), in_specs=[one, line, line, one,...  13.6 us
    ppermute x3, starting transfers between devices, edges(): above = lax.ppermute(tail, 'row', [(i, i + 1) for i in range(ends)])  12.6 us
    all_to_all x2, starting transfers between devices, plane_exchanged(): lax.all_to_all(blocks.reshape(-1, blocks.shape[-1]), ('slide', 'row'), 0,...  11.9 us
    all_to_all x1, starting transfers between devices, everywhere(): got = lax.all_to_all(sent, ('slide', 'row'), 0, 0, tiled=True)  9.87 us
    ppermute x4, starting transfers between devices, to_partner(): lax.ppermute(cells, 'slide', [(i, (i + slides // 2) % slides) for i in ra...  9.66 us
    pallas_call x1, Pallas kernels, body(): pl.pallas_call(input_kernel, grid=(WORK,), in_specs=[flat, edge, edge, ti...  9.53 us
  transfers between devices with their start and end apart: 21, of which 3 were waited for; matrix products, arithmetic and copies ran while one was open for 15% of the time, Pallas kernels for 14%

profile of v4, /device:TPU:1, one launch (start us, length us, event | category | flops | bytes accessed | tf_op | source)
XLA Modules:
  0.0 177.1 jit_solution(7908230450562525246)
XLA Ops:
  2.0 3.8 %collective-permute-start = (bf16[16,16,768]{2,1,0:T(8,128)(2,1)S(1)}, bf16[16,16,768]{2,1,0:T(8,128)(2,1)S(1)}, u32[]{:S(2)}, u32[]{:S(2)}) collective-permute-start(bf16[16,16,768]{2,1,0:T(8,128)(2,1)S(1)} %get-tuple-element.96), channel_id=1, source_target_pairs={{0,64},{4,68},{8,72},{12,76},{16,80},{20,84},{24,88},{28,92},{32,9... | collective-permute-start | bytes 1179656 | tf_op jit(solution)/shard_map/ppermute | solution.py:353
  7.7 4.8 %collective-permute-start.4 = (bf16[1,3,16,768]{3,2,1,0:T(8,128)(2,1)}, bf16[1,3,16,768]{3,2,1,0:T(8,128)(2,1)}, u32[]{:S(2)}, u32[]{:S(2)}) collective-permute-start(bf16[1,3,16,768]{3,2,1,0:T(8,128)(2,1)} %get-tuple-element.101), channel_id=1, source_target_pairs={{0,1},{1,2},{2,3},{4,5},{5,6},{6,7},{8,9},{9,10},{10,11},{12,13},{... | collective-permute-start | bytes 221192 | tf_op jit(solution)/shard_map/ppermute | solution.py:97
  15.3 1.6 reshape.93.kernel
  16.9 6.7 %forward.2 = (bf16[512,768]{1,0:T(8,128)(2,1)}, f32[512,768]{1,0:T(8,128)}, f32[512,128]{1,0:T(8,128)}, bf16[512,768]{1,0:T(8,128)(2,1)}) custom-call(bf16[1,16,16,768]{3,2,1,0:T(8,128)(2,1)} %copy-done.1, bf16[1,3,16,768]{3,2,1,0:T(8,128)(2,1)} %collective-permute-done.4.above, bf16[1,3,16,768]{3,2,1,0:T(8,128)(2,1)} %collective-permute-done.5.below, ...), custom_call_target="tpu_custom_call" | custom-call | flops 1 | bytes 1 | tf_op jit(solution)/shard_map/forward/pallas_call | solution.py:401
  26.2 4.0 %collective-permute-start.1 = (bf16[1,3,16,768]{3,2,1,0:T(8,128)(2,1)S(1)}, bf16[1,3,16,768]{3,2,1,0:T(8,128)(2,1)S(1)}, u32[]{:S(2)}, u32[]{:S(2)}) collective-permute-start(bf16[1,3,16,768]{3,2,1,0:T(8,128)(2,1)S(1)} %get-tuple-element.103), channel_id=1, source_target_pairs={{0,1},{1,2},{2,3},{4,5},{5,6},{6,7},{8,9},{9,10},{10,11},{12,13},{... | collective-permute-start | bytes 221192 | tf_op jit(solution)/shard_map/ppermute | solution.py:97
  33.0 6.9 %forward.3 = (bf16[512,768]{1,0:T(8,128)(2,1)}, f32[512,768]{1,0:T(8,128)}, f32[512,128]{1,0:T(8,128)}, bf16[512,768]{1,0:T(8,128)(2,1)}) custom-call(bf16[1,16,16,768]{3,2,1,0:T(8,128)(2,1)} %copy-done, bf16[1,3,16,768]{3,2,1,0:T(8,128)(2,1)} %copy-done.14, ...), custom_call_target="tpu_custom_call", output_to_operand_aliasing={{0}: (7, {}), {1}: (8, {}), {2}: (9, {}), {3}: (10, {})} | custom-call | flops 1 | bytes 1 | tf_op jit(solution)/shard_map/forward/pallas_call | solution.py:401
  39.8 28.5 %mlp.1 = (bf16[4,4,4,24,768]{4,3,2,1,0:T(8,128)(2,1)}, bf16[4,4,4,24,768]{4,3,2,1,0:T(8,128)(2,1)}, bf16[4,4,4,24,768]{4,3,2,1,0:T(8,128)(2,1)}, bf16[4,4,4,24,7...) custom-call(s32[1]{0:T(128)} %bitcast.core, ...), custom_call_target="tpu_custom_call" | custom-call | flops 1 | bytes 1 | tf_op jit(solution)/shard_map/mlp/pallas_call | solution.py:436
  68.3 2.2 %collective-permute-start.8 = (bf16[4,4,4,24,768]{4,3,2,1,0:T(8,128)(2,1)}, bf16[4,4,4,24,768]{4,3,2,1,0:T(8,128)(2,1)S(1)}, u32[]{:S(2)}, u32[]{:S(2)}) collective-permute-start(bf16[4,4,4,24,768]{4,3,2,1,0:T(8,128)(2,1)} %get-tuple-element.59), channel_id=1, source_target_pairs={{0,4},{4,0},{8,12},{12,8},{16,20},{20,16},{24,28},{28,24},{32,36},... | collective-permute-start | bytes 7077896 | tf_op jit(solution)/shard_map/ppermute | solution.py:34
  70.6 3.8 %collective-permute-start.6 = (bf16[2,3,16,768]{3,2,1,0:T(8,128)(2,1)}, bf16[2,3,16,768]{3,2,1,0:T(8,128)(2,1)S(1)}, u32[]{:S(2)}, u32[]{:S(2)}) collective-permute-start(bf16[2,3,16,768]{3,2,1,0:T(8,128)(2,1)} %get-tuple-element.56), channel_id=1, source_target_pairs={{0,1},{1,2},{2,3},{4,5},{5,6},{6,7},{8,9},{9,10},{10,11},{12,13},{... | collective-permute-start | bytes 442376 | tf_op jit(solution)/shard_map/ppermute | solution.py:97
  78.8 8.0 %taps.1 = bf16[16,8,768]{2,1,0:T(8,128)(2,1)} custom-call(bf16[2,16,16,768]{3,2,1,0:T(8,128)(2,1)} %pad_maximum_fusion.1.tiles, bf16[2,3,16,768]{3,2,1,0:T(8,128)(2,1)} %pad_maximum_fusion.3.above, bf16[2,3,16,768]{3,2,1,0:T(8,128)(2,1)} %pad_maximum_fusion.4.below, f32[512,768]{1,0:T(8,128)} %get-tuple-element.72.d_filt, f32[8,768]{1,0:T(8,128)} %get-tuple-element.54.gains, ...), custom_call_target="tpu_custom_call" | custom-call | flops 1 | bytes 1 | tf_op jit(solution)/shard_map/taps/pallas_call | solution.py:495
  88.4 3.5 %fusion.9 = (bf16[4,4,24,768]{3,2,1,0:T(8,128)(2,1)S(1)}, bf16[4,4,24,768]{3,2,1,0:T(8,128)(2,1)}, bf16[4,4,24,768]{3,2,1,0:T(8,128)(2,1)}) fusion(bf16[4,4,4,24,768]{4,3,2,1,0:T(8,128)(2,1)} %collective-permute-done.9, s32[]{:T(128)S(6)} %select_n.143, bf16[4,4,4,24,768]{4,3,2,1,0:T(8,128)(2,1)} %get-tuple-element.63, s32[]{:T(128)S(6)} %select_n.145, ...), kind=kLoop, calls=%fused_computation.29 | loop fusion | flops 3538944 | bytes 5308428 | tf_op jit(solution)/shard_map/convert_element_type | solution.py:44
  94.2 2.9 %collective-permute-start.10 = (bf16[16,16,768]{2,1,0:T(8,128)(2,1)}, bf16[16,16,768]{2,1,0:T(8,128)(2,1)}, u32[]{:S(2)}, u32[]{:S(2)}) collective-permute-start(bf16[16,16,768]{2,1,0:T(8,128)(2,1)} %get-tuple-element.98), channel_id=1, source_target_pairs={{0,64},{4,68},{8,72},{12,76},{16,80},{20,84},{24,88},{28,92},{32,9... | collective-permute-start | bytes 1179656 | tf_op jit(solution)/shard_map/ppermute | solution.py:353
  97.1 2.4 %collective-permute-start.12 = (bf16[4,4,24,768]{3,2,1,0:T(8,128)(2,1)}, bf16[4,4,24,768]{3,2,1,0:T(8,128)(2,1)}, u32[]{:S(2)}, u32[]{:S(2)}) collective-permute-start(bf16[4,4,24,768]{3,2,1,0:T(8,128)(2,1)} %get-tuple-element.86), channel_id=1, source_target_pairs={{0,2},{4,20},{1,3},{5,21},{2,0},{6,22},{3,1},{7,23},{8,10},{12,28}... | collective-permute-start | bytes 1769480 | tf_op jit(solution)/shard_map/ppermute | solution.py:60
  100.7 6.4 %all-to-all-start = ((bf16[16,8,768]{2,1,0:T(8,128)(2,1)}), bf16[16,8,768]{2,1,0:T(8,128)(2,1)S(1)}, u32[]{:S(2)}, u32[]{:S(2)}) async-start(bf16[16,8,768]{2,1,0:T(8,128)(2,1)} %taps.1), calls=%async_computation | async-start | bytes 393216 | tf_op jit(solution)/shard_map/all_to_all | solution.py:74
  107.0 2.9 %fusion.12 = (bf16[4,4,24,768]{3,2,1,0:T(8,128)(2,1)}, bf16[4,4,24,768]{3,2,1,0:T(8,128)(2,1)}, bf16[4,4,24,768]{3,2,1,0:T(8,128)(2,1)}) fusion(bf16[4,4,4,24,768]{4,3,2,1,0:T(8,128)(2,1)} %copy-done.6, s32[]{:T(128)S(6)} %select_n.143, bf16[4,4,4,24,768]{4,3,2,1,0:T(8,128)(2,1)S(1)} %copy-done.5, s32[]{:T(128)S(6)} %select_n.145, s32[]{:T(128)S(6)} %select_n.138), kind=kLoop, calls=%fused_computation.32 | loop fusion | flops 3538944 | bytes 5308428 | tf_op jit(solution)/shard_map/convert_element_type | solution.py:44
  115.3 9.9 %all-to-all-start.1 = ((bf16[128,24,128]{2,1,0:T(8,128)(2,1)}), bf16[128,24,128]{2,1,0:T(8,128)(2,1)S(1)}, u32[]{:S(2)}, u32[]{:S(2)}) async-start(bf16[128,24,128]{2,1,0:T(8,128)(2,1)} %broadcast_in_dim.43), calls=%async_computation.1 | async-start | bytes 1572864 | tf_op jit(solution)/shard_map/all_to_all | solution.py:89
  125.2 9.5 %inputs.1 = (f32[2,16,16,768]{3,2,1,0:T(8,128)}, bf16[1,16,16,768]{3,2,1,0:T(8,128)(2,1)}) custom-call(f32[512,768]{1,0:T(8,128)} %get-tuple-element.72.d_filt, bf16[2,3,16,768]{3,2,1,0:T(8,128)(2,1)} %copy-done.16, bf16[2,3,16,768]{3,2,1,0:T(8,128)(2,1)} %copy-done.17, bf16[2,16,16,768]{3,2,1,0:T(8,128)(2,1)} %pad_maximum_fusion.2.cotan, ...), custom_call_target="tpu_custom_call" | custom-call | flops 1 | bytes 1 | tf_op jit(solution)/shard_map/inputs/pallas_call | solution.py:518
  134.7 2.1 %fusion.5 = bf16[4,4,24,768]{3,2,1,0:T(8,128)(2,1)S(1)} fusion(bf16[4,4,24,768]{3,2,1,0:T(8,128)(2,1)} %collective-permute-done.13, bf16[4,4,24,768]{3,2,1,0:T(8,128)(2,1)} %collective-permute-done.12, bf16[4,4,24,768]{3,2,1,0:T(8,128)(2,1)} %collective-permute-done.11, bf16[4,4,4,24,768]{4,3,2,1,0:T(8,128)(2,1)} %collective-permute-done.9, ...), kind=kLoop, calls=%fused_computation.11 | loop fusion | flops 3538944 | bytes 3538948 | tf_op jit(solution)/shard_map/convert_element_type | solution.py:67
  136.9 2.0 %fusion.2 = bf16[4,4,24,768]{3,2,1,0:T(8,128)(2,1)S(1)} fusion(bf16[4,4,24,768]{3,2,1,0:T(8,128)(2,1)} %collective-permute-done.16, bf16[4,4,24,768]{3,2,1,0:T(8,128)(2,1)} %collective-permute-done.15, bf16[4,4,24,768]{3,2,1,0:T(8,128)(2,1)} %collective-permute-done.14, bf16[4,4,4,24,768]{4,3,2,1,0:T(8,128)(2,1)} %copy-done.6, s32[]{:T(128)S(6)} %select_n.141, ...), kind=kLoop, calls=%fused_computation.7 | loop fusion | flops 3538944 | bytes 3538948 | tf_op jit(solution)/shard_map/convert_element_type | solution.py:67
  140.0 1.8 %all-to-all-done.1 = bf16[128,24,128]{2,1,0:T(8,128)(2,1)S(1)} async-done(((bf16[128,24,128]{2,1,0:T(8,128)(2,1)}), bf16[128,24,128]{2,1,0:T(8,128)(2,1)S(1)}, u32[]{:S(2)}, u32[]{:S(2)}) %all-to-all-start.1) | async-done | bytes 786464 | tf_op jit(solution)/shard_map/all_to_all | solution.py:89
  142.8 5.5 %all-to-all-start.2 = ((bf16[16,48,768]{2,1,0:T(8,128)(2,1)}), bf16[16,48,768]{2,1,0:T(8,128)(2,1)S(1)}, u32[]{:S(2)}, u32[]{:S(2)}) async-start(bf16[16,48,768]{2,1,0:T(8,128)(2,1)} %pad_maximum_fusion), calls=%async_computation.2 | async-start | bytes 2359296 | tf_op jit(solution)/shard_map/all_to_all | solution.py:74
  150.6 2.9 %collective-permute-start.17 = (bf16[16,16,768]{2,1,0:T(8,128)(2,1)}, bf16[16,16,768]{2,1,0:T(8,128)(2,1)S(1)}, u32[]{:S(2)}, u32[]{:S(2)}) collective-permute-start(bf16[16,16,768]{2,1,0:T(8,128)(2,1)} %bitcast.65), channel_id=1, source_target_pairs={{0,64},{4,68},{8,72},{12,76},{16,80},{20,84},{24,88},{28,92},{32,9... | collective-permute-start | bytes 1179656 | tf_op jit(solution)/shard_map/ppermute | solution.py:353
  155.0 18.5 %collective-permute-done.17 = bf16[16,16,768]{2,1,0:T(8,128)(2,1)S(1)} collective-permute-done((bf16[16,16,768]{2,1,0:T(8,128)(2,1)}, bf16[16,16,768]{2,1,0:T(8,128)(2,1)S(1)}, u32[]{:S(2)}, u32[]{:S(2)}) %collective-permute-start.17) | collective-permute-done | bytes 393248 | tf_op jit(solution)/shard_map/ppermute | solution.py:353
  173.6 2.0 %maximum_bitcast_fusion = f32[1,4,16,16,768]{4,3,2,1,0:T(8,128)} fusion(f32[1,16,16,768]{3,2,1,0:T(8,128)S(1)} %broadcast_in_dim.44, f32[1,16,16,768]{3,2,1,0:T(8,128)S(1)} %select_bitcast_fusion, f32[1,16,16,768]{3,2,1,0:T(8,128)S(1)} %get-tuple-element.92, f32[1,16,16,768]{3,2,1,0:T(8,128)S(1)} %get-tuple-element.91), kind=kLoop, calls=%fused_computation | loop fusion | flops 2359296 | bytes 6291456 | tf_op jit(solution)/shard_map/broadcast_in_dim | solution.py:361
  (103 shorter events, 32.7 us)
Async XLA Ops:
  2.0 21.7 %collective-permute-start = (bf16[16,16,768]{2,1,0:T(8,128)(2,1)S(1)}, bf16[16,16,768]{2,1,0:T(8,128)(2,1)S(1)}, u32[]{:S(2)}, u32[]{:S(2)}) collective-permute-start(bf16[16,16,768]{2,1,0:T(8,128)(2,1)S(1)} %get-tuple-element.96), channel_id=1, source_target_pairs={{0,64},{4,68},{8,72},{12,76},{16,80},{20,84},{24,88},{28,92},{32,9... | collective-permute-start | bytes 1179656 | tf_op jit(solution)/shard_map/ppermute | solution.py:353
  6.4 10.4 %collective-permute-start.5 = (bf16[1,3,16,768]{3,2,1,0:T(8,128)(2,1)}, bf16[1,3,16,768]{3,2,1,0:T(8,128)(2,1)}, u32[]{:S(2)}, u32[]{:S(2)}) collective-permute-start(bf16[1,3,16,768]{3,2,1,0:T(8,128)(2,1)} %get-tuple-element.100), channel_id=1, source_target_pairs={{1,0},{2,1},{3,2},{5,4},{6,5},{7,6},{9,8},{10,9},{11,10},{13,12},{... | collective-permute-start | bytes 221192 | tf_op jit(solution)/shard_map/ppermute | solution.py:98
  7.7 9.1 %collective-permute-start.4 = (bf16[1,3,16,768]{3,2,1,0:T(8,128)(2,1)}, bf16[1,3,16,768]{3,2,1,0:T(8,128)(2,1)}, u32[]{:S(2)}, u32[]{:S(2)}) collective-permute-start(bf16[1,3,16,768]{3,2,1,0:T(8,128)(2,1)} %get-tuple-element.101), channel_id=1, source_target_pairs={{0,1},{1,2},{2,3},{4,5},{5,6},{6,7},{8,9},{9,10},{10,11},{12,13},{... | collective-permute-start | bytes 221192 | tf_op jit(solution)/shard_map/ppermute | solution.py:97
  13.4 17.8 %collective-permute-start.3 = (bf16[16,16,768]{2,1,0:T(8,128)(2,1)S(1)}, bf16[16,16,768]{2,1,0:T(8,128)(2,1)S(1)}, u32[]{:S(2)}, u32[]{:S(2)}) collective-permute-start(bf16[16,16,768]{2,1,0:T(8,128)(2,1)S(1)} %get-tuple-element.94), channel_id=1, source_target_pairs={{0,64},{4,68},{8,72},{12,76},{16,80},{20,84},{24,88},{28,92},{32,9... | collective-permute-start | bytes 1179656 | tf_op jit(solution)/shard_map/ppermute | solution.py:353
  24.8 7.5 %collective-permute-start.2 = (bf16[1,3,16,768]{3,2,1,0:T(8,128)(2,1)S(1)}, bf16[1,3,16,768]{3,2,1,0:T(8,128)(2,1)S(1)}, u32[]{:S(2)}, u32[]{:S(2)}) collective-permute-start(bf16[1,3,16,768]{3,2,1,0:T(8,128)(2,1)S(1)} %get-tuple-element.102), channel_id=1, source_target_pairs={{1,0},{2,1},{3,2},{5,4},{6,5},{7,6},{9,8},{10,9},{11,10},{13,12},{... | collective-permute-start | bytes 221192 | tf_op jit(solution)/shard_map/ppermute | solution.py:98
  26.2 6.1 %collective-permute-start.1 = (bf16[1,3,16,768]{3,2,1,0:T(8,128)(2,1)S(1)}, bf16[1,3,16,768]{3,2,1,0:T(8,128)(2,1)S(1)}, u32[]{:S(2)}, u32[]{:S(2)}) collective-permute-start(bf16[1,3,16,768]{3,2,1,0:T(8,128)(2,1)S(1)} %get-tuple-element.103), channel_id=1, source_target_pairs={{0,1},{1,2},{2,3},{4,5},{5,6},{6,7},{8,9},{9,10},{10,11},{12,13},{... | collective-permute-start | bytes 221192 | tf_op jit(solution)/shard_map/ppermute | solution.py:97
  39.8 35.9 %copy-start.15 = (bf16[1,3,16,768]{3,2,1,0:T(8,128)(2,1)S(1)}, bf16[1,3,16,768]{3,2,1,0:T(8,128)(2,1)}, u32[]{:S(2)}) copy-start(bf16[1,3,16,768]{3,2,1,0:T(8,128)(2,1)} %copy-done.14) | copy-start | bytes 221188
  39.8 37.5 %copy-start.13 = (bf16[1,3,16,768]{3,2,1,0:T(8,128)(2,1)S(1)}, bf16[1,3,16,768]{3,2,1,0:T(8,128)(2,1)}, u32[]{:S(2)}) copy-start(bf16[1,3,16,768]{3,2,1,0:T(8,128)(2,1)} %copy-done.12) | copy-start | bytes 221188
  68.3 18.6 %collective-permute-start.8 = (bf16[4,4,4,24,768]{4,3,2,1,0:T(8,128)(2,1)}, bf16[4,4,4,24,768]{4,3,2,1,0:T(8,128)(2,1)S(1)}, u32[]{:S(2)}, u32[]{:S(2)}) collective-permute-start(bf16[4,4,4,24,768]{4,3,2,1,0:T(8,128)(2,1)} %get-tuple-element.59), channel_id=1, source_target_pairs={{0,4},{4,0},{8,12},{12,8},{16,20},{20,16},{24,28},{28,24},{32,36},... | collective-permute-start | bytes 7077896 | tf_op jit(solution)/shard_map/ppermute | solution.py:34
  70.5 16.4 %collective-permute-start.9 = (bf16[4,4,4,24,768]{4,3,2,1,0:T(8,128)(2,1)}, bf16[4,4,4,24,768]{4,3,2,1,0:T(8,128)(2,1)}, u32[]{:S(2)}, u32[]{:S(2)}) collective-permute-start(bf16[4,4,4,24,768]{4,3,2,1,0:T(8,128)(2,1)} %get-tuple-element.61), channel_id=1, source_target_pairs={{0,4},{4,0},{8,12},{12,8},{16,20},{20,16},{24,28},{28,24},{32,36},... | collective-permute-start | bytes 7077896 | tf_op jit(solution)/shard_map/ppermute | solution.py:34
  70.6 16.3 %collective-permute-start.6 = (bf16[2,3,16,768]{3,2,1,0:T(8,128)(2,1)}, bf16[2,3,16,768]{3,2,1,0:T(8,128)(2,1)S(1)}, u32[]{:S(2)}, u32[]{:S(2)}) collective-permute-start(bf16[2,3,16,768]{3,2,1,0:T(8,128)(2,1)} %get-tuple-element.56), channel_id=1, source_target_pairs={{0,1},{1,2},{2,3},{4,5},{5,6},{6,7},{8,9},{9,10},{10,11},{12,13},{... | collective-permute-start | bytes 442376 | tf_op jit(solution)/shard_map/ppermute | solution.py:97
  74.4 12.5 %collective-permute-start.7 = (bf16[2,3,16,768]{3,2,1,0:T(8,128)(2,1)}, bf16[2,3,16,768]{3,2,1,0:T(8,128)(2,1)S(1)}, u32[]{:S(2)}, u32[]{:S(2)}) collective-permute-start(bf16[2,3,16,768]{3,2,1,0:T(8,128)(2,1)} %get-tuple-element.57), channel_id=1, source_target_pairs={{1,0},{2,1},{3,2},{5,4},{6,5},{7,6},{9,8},{10,9},{11,10},{13,12},{... | collective-permute-start | bytes 442376 | tf_op jit(solution)/shard_map/ppermute | solution.py:98
  91.9 15.1 %copy-start.5 = (bf16[4,4,4,24,768]{4,3,2,1,0:T(8,128)(2,1)S(1)}, bf16[4,4,4,24,768]{4,3,2,1,0:T(8,128)(2,1)}, u32[]{:S(2)}) copy-start(bf16[4,4,4,24,768]{4,3,2,1,0:T(8,128)(2,1)} %get-tuple-element.65) | copy-start | bytes 7077892
  91.9 19.3 %collective-permute-start.11 = (bf16[4,4,24,768]{3,2,1,0:T(8,128)(2,1)S(1)}, bf16[4,4,24,768]{3,2,1,0:T(8,128)(2,1)}, u32[]{:S(2)}, u32[]{:S(2)}) collective-permute-start(bf16[4,4,24,768]{3,2,1,0:T(8,128)(2,1)S(1)} %get-tuple-element.85), channel_id=1, source_target_pairs={{0,1},{4,12},{1,2},{5,13},{2,3},{6,14},{3,0},{7,15},{8,9},{12,20},... | collective-permute-start | bytes 1769480 | tf_op jit(solution)/shard_map/ppermute | solution.py:60
  94.2 16.1 %collective-permute-start.10 = (bf16[16,16,768]{2,1,0:T(8,128)(2,1)}, bf16[16,16,768]{2,1,0:T(8,128)(2,1)}, u32[]{:S(2)}, u32[]{:S(2)}) collective-permute-start(bf16[16,16,768]{2,1,0:T(8,128)(2,1)} %get-tuple-element.98), channel_id=1, source_target_pairs={{0,64},{4,68},{8,72},{12,76},{16,80},{20,84},{24,88},{28,92},{32,9... | collective-permute-start | bytes 1179656 | tf_op jit(solution)/shard_map/ppermute | solution.py:353
  97.1 37.7 %collective-permute-start.12 = (bf16[4,4,24,768]{3,2,1,0:T(8,128)(2,1)}, bf16[4,4,24,768]{3,2,1,0:T(8,128)(2,1)}, u32[]{:S(2)}, u32[]{:S(2)}) collective-permute-start(bf16[4,4,24,768]{3,2,1,0:T(8,128)(2,1)} %get-tuple-element.86), channel_id=1, source_target_pairs={{0,2},{4,20},{1,3},{5,21},{2,0},{6,22},{3,1},{7,23},{8,10},{12,28}... | collective-permute-start | bytes 1769480 | tf_op jit(solution)/shard_map/ppermute | solution.py:60
  99.5 35.2 %collective-permute-start.13 = (bf16[4,4,24,768]{3,2,1,0:T(8,128)(2,1)}, bf16[4,4,24,768]{3,2,1,0:T(8,128)(2,1)}, u32[]{:S(2)}, u32[]{:S(2)}) collective-permute-start(bf16[4,4,24,768]{3,2,1,0:T(8,128)(2,1)} %get-tuple-element.87), channel_id=1, source_target_pairs={{0,3},{4,28},{1,0},{5,29},{2,1},{6,30},{3,2},{7,31},{8,11},{12,4},... | collective-permute-start | bytes 1769480 | tf_op jit(solution)/shard_map/ppermute | solution.py:60
  100.7 13.6 %all-to-all-start = ((bf16[16,8,768]{2,1,0:T(8,128)(2,1)}), bf16[16,8,768]{2,1,0:T(8,128)(2,1)S(1)}, u32[]{:S(2)}, u32[]{:S(2)}) async-start(bf16[16,8,768]{2,1,0:T(8,128)(2,1)} %taps.1), calls=%async_computation | async-start | bytes 393216 | tf_op jit(solution)/shard_map/all_to_all | solution.py:74
  110.0 26.9 %collective-permute-start.14 = (bf16[4,4,24,768]{3,2,1,0:T(8,128)(2,1)}, bf16[4,4,24,768]{3,2,1,0:T(8,128)(2,1)}, u32[]{:S(2)}, u32[]{:S(2)}) collective-permute-start(bf16[4,4,24,768]{3,2,1,0:T(8,128)(2,1)} %get-tuple-element.88), channel_id=1, source_target_pairs={{0,1},{4,12},{1,2},{5,13},{2,3},{6,14},{3,0},{7,15},{8,9},{12,20},... | collective-permute-start | bytes 1769480 | tf_op jit(solution)/shard_map/ppermute | solution.py:60
  110.3 26.6 %collective-permute-start.15 = (bf16[4,4,24,768]{3,2,1,0:T(8,128)(2,1)}, bf16[4,4,24,768]{3,2,1,0:T(8,128)(2,1)}, u32[]{:S(2)}, u32[]{:S(2)}) collective-permute-start(bf16[4,4,24,768]{3,2,1,0:T(8,128)(2,1)} %get-tuple-element.89), channel_id=1, source_target_pairs={{0,2},{4,20},{1,3},{5,21},{2,0},{6,22},{3,1},{7,23},{8,10},{12,28}... | collective-permute-start | bytes 1769480 | tf_op jit(solution)/shard_map/ppermute | solution.py:60
  111.2 25.7 %collective-permute-start.16 = (bf16[4,4,24,768]{3,2,1,0:T(8,128)(2,1)}, bf16[4,4,24,768]{3,2,1,0:T(8,128)(2,1)}, u32[]{:S(2)}, u32[]{:S(2)}) collective-permute-start(bf16[4,4,24,768]{3,2,1,0:T(8,128)(2,1)} %get-tuple-element.90), channel_id=1, source_target_pairs={{0,3},{4,28},{1,0},{5,29},{2,1},{6,30},{3,2},{7,31},{8,11},{12,4},... | collective-permute-start | bytes 1769480 | tf_op jit(solution)/shard_map/ppermute | solution.py:60
  115.3 26.5 %all-to-all-start.1 = ((bf16[128,24,128]{2,1,0:T(8,128)(2,1)}), bf16[128,24,128]{2,1,0:T(8,128)(2,1)S(1)}, u32[]{:S(2)}, u32[]{:S(2)}) async-start(bf16[128,24,128]{2,1,0:T(8,128)(2,1)} %broadcast_in_dim.43), calls=%async_computation.1 | async-start | bytes 1572864 | tf_op jit(solution)/shard_map/all_to_all | solution.py:89
  142.8 32.8 %all-to-all-start.2 = ((bf16[16,48,768]{2,1,0:T(8,128)(2,1)}), bf16[16,48,768]{2,1,0:T(8,128)(2,1)S(1)}, u32[]{:S(2)}, u32[]{:S(2)}) async-start(bf16[16,48,768]{2,1,0:T(8,128)(2,1)} %pad_maximum_fusion), calls=%async_computation.2 | async-start | bytes 2359296 | tf_op jit(solution)/shard_map/all_to_all | solution.py:74
  150.6 22.9 %collective-permute-start.17 = (bf16[16,16,768]{2,1,0:T(8,128)(2,1)}, bf16[16,16,768]{2,1,0:T(8,128)(2,1)S(1)}, u32[]{:S(2)}, u32[]{:S(2)}) collective-permute-start(bf16[16,16,768]{2,1,0:T(8,128)(2,1)} %bitcast.65), channel_id=1, source_target_pairs={{0,64},{4,68},{8,72},{12,76},{16,80},{20,84},{24,88},{28,92},{32,9... | collective-permute-start | bytes 1179656 | tf_op jit(solution)/shard_map/ppermute | solution.py:353
  (17 other events, 111.5 us)

commit v5 on v3

--- a/solution.py
+++ b/solution.py
@@ -1,3 +1,4 @@
+import functools
 import itertools
 import math
 
@@ -39,11 +40,7 @@
     own = jnp.where(core == 0, lax.axis_index("row"), lax.axis_index("slide") // 2 % SIDE)
 
     def cut(half, by):
-        cells = half.reshape(SIDE, SIDE, SIDE, -1, half.shape[-1])
-        at = (own + by) % SIDE
-        along_z = lax.dynamic_index_in_dim(cells, at, 2, keepdims=False)
-        along_x = lax.dynamic_index_in_dim(cells, at, 1, keepdims=False)
-        return jnp.where(core == 0, along_z, along_x).astype(f32)
+        return lax.dynamic_index_in_dim(half, (own + by) % SIDE, 0, keepdims=False).astype(f32)
 
     return [(cut(mine, by) + cut(got, by)).astype(bf16) for by in range(SIDE)]
 
@@ -96,10 +93,8 @@
     return whole.reshape(-1, share.shape[-1])
 
 
-def edges(cells):
+def edges(head, tail):
     ends = lax.axis_size("row") - 1
-    head = cells[:, :REACH]
-    tail = cells[:, cells.shape[1] - REACH :]
     above = lax.ppermute(tail, "row", [(i, i + 1) for i in range(ends)])
     below = lax.ppermute(head, "row", [(i + 1, i) for i in range(ends)])
     return above, below
@@ -156,7 +151,8 @@
 
 def spread_kernel(wide, kernel_ref):
     for tap in range(TAPS * TAPS):
-        wide[tap] = jnp.broadcast_to(kernel_ref[tap : tap + 1, :], wide.shape[1:])
+        a, b = divmod(tap, TAPS)
+        wide[tap] = jnp.broadcast_to(kernel_ref[a, b : b + 1, :], wide.shape[1:])
 
 
 def forward_kernel(
@@ -209,16 +205,18 @@
     return jnp.where(pre < 0.0, tail, 1.0 - tail), bell * density
 
 
-def split_rows(core, mine, other, rows_at):
-    count = mine.shape[1]
-    for chip in range(mine.shape[0]):
-        for half, which in ((mine, core[0]), (other, 1 - core[0])):
-            rows_at(half, chip, pl.ds(pl.multiple_of((2 * chip + which) * count, 32), count))
+def split_rows(core, mine, other, y, first, rows_at):
+    count = mine.shape[3]
+    for x, z in itertools.product(range(SIDE), repeat=2):
+        flipped = [jnp.where(core[0] == 0, *pair) for pair in ((z, x), (x, z))]
+        for half, which, at in ((mine, core[0], flipped), (other, 1 - core[0], flipped[::-1])):
+            begin = pl.multiple_of(first + ((2 * x + which) * SIDE + z) * count, 8)
+            rows_at(half, (at[0], y, at[1]), pl.ds(begin, count))
 
 
 def mlp_kernel(
     core, count, normed, spread, first, second, unit, inv, gain, scale, tiles, cotan,
-    mine1, other1, mine2, other2, d_filt, out, gain_grad, scale_grad,
+    mine1, other1, mine2, other2, d_filt, d_head, d_tail, out, gain_grad, scale_grad,
     turned, total2, term, back, branch,
 ):
     step = pl.program_id(0)
@@ -246,21 +244,26 @@
     )
     term[...] = lax.dot_general(
         d_pre, normed[...], (((0,), (0,)), ((), ())), preferred_element_type=f32
-    ).astype(bf16)
+    )
 
     def copy1(half, chip, at):
-        half[chip] = term[at, :]
-
-    split_rows(core, mine1, other1, copy1)
+        half[chip] = term[at, :].astype(bf16)
+
+    split_rows(core, mine1, other1, 0, 0, copy1)
     back[...] += jnp.dot(d_pre, first[...], preferred_element_type=f32)
 
     @pl.when(step == pl.num_programs(0) - 1)
     def _():
         def copy2(half, chip, at):
             for i in range(BLOCK // LANES):
-                half[chip, :, i * LANES : (i + 1) * LANES] = total2[i, at, :].astype(bf16)
-
-        split_rows(core, mine2, other2, copy2)
+                lanes = slice(i * LANES, (i + 1) * LANES)
+                half[(*chip, slice(None), lanes)] = total2[i, at, :].astype(bf16)
+
+        def over(y, carry):
+            split_rows(core, mine2, other2, y, y * (total2.shape[1] // SIDE), copy2)
+            return carry
+
+        lax.fori_loop(0, SIDE, over, 0)
         lines = 64 // cols
 
         def finish(i, kept):
@@ -285,12 +288,18 @@
 
         start = jnp.zeros((8, chans), f32)
         gain_grad[...], scale_grad[...] = lax.fori_loop(0, pixels // 64, finish, (start, start))
+        for slot in range(MOST):
+            begin, end = slot * rows * cols, (slot + 1) * rows * cols
+            ends = (REACH, cols, chans)
+            d_head[slot] = d_filt[begin : begin + REACH * cols, :].reshape(ends).astype(bf16)
+            d_tail[slot] = d_filt[end - REACH * cols : end, :].reshape(ends).astype(bf16)
         out[0, MOST:] = jnp.zeros((out.shape[1] - MOST, rows, cols, chans), bf16)
 
 
-def tap_kernel(tiles, above, below, d_filt, grad, pad, total):
+def tap_kernel(tiles, above, below, d_filt, gains, scales, small, pad, total, lines):
     slot = pl.program_id(0)
     rows, cols, chans = tiles.shape[2:]
+    share = -(-(TAPS * TAPS + 2) // small.shape[0])
 
     @pl.when(slot == 0)
     def _():
@@ -317,15 +326,21 @@
 
     @pl.when(slot == pl.num_programs(0) - 1)
     def _():
-        for tap in range(TAPS * TAPS):
-            grad[tap : tap + 1, :] = jnp.sum(total[tap], axis=0, keepdims=True)
-
-
-def input_kernel(count, d_filt, above, below, cotan, kernel, out, pad, wide):
-    slot = pl.program_id(0)
+        lines[...] = jnp.zeros_like(lines)
+        for i in range(TAPS * TAPS + 2):
+            value = total[i] if i < TAPS * TAPS else (gains, scales)[i - TAPS * TAPS][...]
+            at = i // share * small.shape[1] + i % share
+            lines[at : at + 1, :] = jnp.sum(value, axis=0, keepdims=True)
+        for i in range(small.shape[0]):
+            small[i] = lines[i * small.shape[1] : (i + 1) * small.shape[1], :].astype(bf16)
+
+
+def input_kernel(first, count, d_filt, above, below, cotan, kernel, *refs):
+    out, pad, wide = refs[-3:]
+    slot = pl.program_id(0) + first
     rows, cols, chans = out.shape[2:]
 
-    @pl.when(slot == 0)
+    @pl.when(slot == first)
     def _():
         spread_kernel(wide, kernel)
         clear_padded(pad)
@@ -354,9 +369,8 @@
     hidden = fc1_weight.shape[0]
     pixels = rows * cols
     every = MOST * pixels
-    taps = dw_kernel.reshape(TAPS * TAPS, chans)
     gain, scale = ln_gain[None], layer_scale[None]
-    above, below = edges(tiles[0, :MOST])
+    above, below = edges(tiles[0, :MOST, :REACH], tiles[0, :MOST, rows - REACH :])
 
     params = pltpu.CompilerParams(
         vmem_limit_bytes=60 * 1024 * 1024, dimension_semantics=("arbitrary",)
@@ -365,15 +379,8 @@
     brief = pl.CostEstimate(flops=1, bytes_accessed=1, transcendentals=0)
     smem = pl.BlockSpec(memory_space=pltpu.SMEM)
     tile = pl.BlockSpec((1, 1, rows, cols, chans), lambda s: (0, s, 0, 0, 0))
-    tile_live = pl.BlockSpec(
-        (1, 1, rows, cols, chans), lambda s: (0, jnp.minimum(s, MOST - 1), 0, 0, 0)
-    )
     edge = pl.BlockSpec((1, REACH, cols, chans), lambda s: (s, 0, 0, 0))
-    edge_live = pl.BlockSpec(
-        (1, REACH, cols, chans), lambda s: (jnp.minimum(s, MOST - 1), 0, 0, 0)
-    )
     flat = pl.BlockSpec((pixels, chans), lambda s: (s, 0))
-    flat_live = pl.BlockSpec((pixels, chans), lambda s: (jnp.minimum(s, MOST - 1), 0))
 
     def whole(*dims):
         return pl.BlockSpec(dims, lambda s: (0,) * len(dims))
@@ -384,7 +391,7 @@
     normed, unit, inv, spread = pl.pallas_call(
         forward_kernel,
         grid=(MOST,),
-        in_specs=[smem, tile, edge, edge, tile, whole(TAPS * TAPS, chans), whole(1, chans), whole(1, chans)],
+        in_specs=[smem, tile, edge, edge, tile, whole(TAPS, TAPS, chans), whole(1, chans), whole(1, chans)],
         out_specs=[flat, flat, pl.BlockSpec((pixels, LANES), lambda s: (s, 0)), flat],
         out_shape=[
             shape((every, chans), bf16),
@@ -396,18 +403,19 @@
         compiler_params=params,
         cost_estimate=brief,
         name="forward",
-    )(tile_counts, tiles, above, below, cotangent, taps, gain, scale)
+    )(tile_counts, tiles, above, below, cotangent, dw_kernel, gain, scale)
 
     chips = SIDE * SIDE
-    halves = shape((chips, hidden // (2 * chips), chans), bf16)
+    halves = shape((SIDE, SIDE, SIDE, hidden // (8 * chips), chans), bf16)
+    d_edge = shape((MOST, REACH, cols, chans), bf16)
     core = (lax.axis_index("slide") % 2).reshape(1)
 
     def once(*dims):
         return pl.BlockSpec(dims, lambda s: (0,) * len(dims), pipeline_mode=pl.Buffered(1))
 
-    quarter_of = pl.BlockSpec((SIDE, *halves.shape[1:]), lambda j: (j, 0, 0))
+    quarter_of = pl.BlockSpec((SIDE, 1, *halves.shape[2:]), lambda j: (0, j, 0, 0, 0))
     live = once(1, MOST, rows, cols, chans)
-    mine1, other1, mine2, other2, d_filt, block_out, gain_grad, scale_grad = pl.pallas_call(
+    mine1, other1, mine2, other2, d_filt, d_head, d_tail, block_out, gain_grad, scale_grad = pl.pallas_call(
         mlp_kernel,
         grid=(hidden // BLOCK,),
         in_specs=[
@@ -430,6 +438,8 @@
             once(*halves.shape),
             once(*halves.shape),
             once(every, chans),
+            once(*d_edge.shape),
+            once(*d_edge.shape),
             once(*tiles.shape),
             once(8, chans),
             once(8, chans),
@@ -440,6 +450,8 @@
             halves,
             halves,
             shape((every, chans), f32),
+            d_edge,
+            d_edge,
             shape(tiles.shape, bf16),
             shape((8, chans), f32),
             shape((8, chans), f32),
@@ -447,7 +459,7 @@
         scratch_shapes=[
             pltpu.VMEM((chans, every), bf16),
             pltpu.VMEM((chans // LANES, hidden, LANES), f32),
-            pltpu.VMEM((BLOCK, chans), bf16),
+            pltpu.VMEM((BLOCK, chans), f32),
             pltpu.VMEM((every, chans), f32),
             pltpu.VMEM((every, chans), f32),
         ],
@@ -459,52 +471,65 @@
     )
 
     got2, got1 = from_other_core(other2), from_other_core(other1)
-    d_cells = d_filt.reshape(MOST, rows, cols, chans)
-    d_above, d_below = edges(d_cells.astype(bf16))
-
-    tap_grad = pl.pallas_call(
+    d_above, d_below = edges(d_head, d_tail)
+
+    lines = -(-(TAPS * TAPS + 2) // chips)
+    small = shape((chips, -(-lines // 8) * 8, chans), bf16)
+    small = pl.pallas_call(
         tap_kernel,
         grid=(MOST,),
-        in_specs=[tile, edge, edge, flat],
-        out_specs=whole(TAPS * TAPS, chans),
-        out_shape=shape((TAPS * TAPS, chans), f32),
-        scratch_shapes=[pad, wide],
+        in_specs=[tile, edge, edge, flat, whole(8, chans), whole(8, chans)],
+        out_specs=whole(*small.shape),
+        out_shape=small,
+        scratch_shapes=[pad, wide, pltpu.VMEM((chips * small.shape[1], chans), f32)],
         compiler_params=params,
         cost_estimate=brief,
         name="taps",
-    )(tiles, above, below, d_filt)
-
-    scale_row = jnp.sum(scale_grad, axis=0)
-    gain_row = jnp.sum(gain_grad, axis=0)
-    small = jnp.concatenate([tap_grad, gain_row[None], scale_row[None]]).astype(bf16)
-    lines = -(-small.shape[0] // chips)
-    small = jnp.pad(small, ((0, chips * lines - small.shape[0]), (0, 0)))
-    small = jnp.pad(small.reshape(chips, lines, chans), ((0, 0), (0, -lines % 8), (0, 0)))
+    )(tiles, above, below, d_filt, gain_grad, scale_grad)
+
     small, d_above, d_below, mine1, got1, mine2, got2 = after(
         small, d_above, d_below, mine1, got1, mine2, got2
     )
     share = plane_exchanged(small)[:lines]
-    parts = quarters(mine2, got2) + quarters(mine1, got1)
-    ring2, ring1 = ring_sent(parts[:SIDE]), ring_sent(parts[SIDE:])
-    share, _, _ = after(share, parts[SIDE - 1], parts[-1])
+    parts2, parts1 = quarters(mine2, got2), quarters(mine1, got1)
+    ring2, ring1 = ring_sent(parts2), ring_sent(parts1)
+    share, _, _ = after(share, parts2[-1], parts1[-1])
     share, d_filt, d_above, d_below = after(share, d_filt, d_above, d_below)
     small = everywhere(share)
 
-    grad_input = pl.pallas_call(
-        input_kernel,
-        grid=(slots,),
-        in_specs=[smem, flat_live, edge_live, edge_live, tile_live, whole(TAPS * TAPS, chans)],
-        out_specs=tile,
-        out_shape=shape(tiles.shape, f32),
-        scratch_shapes=[pad, wide],
-        compiler_params=params,
-        cost_estimate=brief,
-        name="inputs",
-    )(tile_counts, d_filt, d_above, d_below, cotangent, taps)
+    def input_grads(first, some, earlier, d_filt, d_above, d_below):
+        def at(s):
+            return jnp.minimum(s + first, MOST - 1)
+
+        tile_at = (1, 1, rows, cols, chans)
+        edge_at = pl.BlockSpec((1, REACH, cols, chans), lambda s: (at(s), 0, 0, 0))
+        return pl.pallas_call(
+            functools.partial(input_kernel, first),
+            grid=(some,),
+            in_specs=[
+                smem,
+                pl.BlockSpec((pixels, chans), lambda s: (at(s), 0)),
+                edge_at,
+                edge_at,
+                pl.BlockSpec(tile_at, lambda s: (0, at(s), 0, 0, 0)),
+                whole(TAPS, TAPS, chans),
+            ]
+            + [pl.BlockSpec(memory_space=pl.ANY)] * len(earlier),
+            out_specs=pl.BlockSpec(tile_at, lambda s: (0, s + first, 0, 0, 0)),
+            out_shape=shape(tiles.shape, f32),
+            scratch_shapes=[pad, wide],
+            input_output_aliases={6: 0} if earlier else {},
+            compiler_params=params,
+            cost_estimate=brief,
+            name="inputs",
+        )(tile_counts, d_filt, d_above, d_below, cotangent, dw_kernel, *earlier)
+
+    grad_input = input_grads(0, 2, [], d_filt, d_above, d_below)
 
     grad_kernel = small[: TAPS * TAPS].reshape(dw_kernel.shape)
-    blocks = jnp.concatenate([total_of(parts[0], ring2), total_of(parts[SIDE], ring1)], axis=1)
-    blocks, small, grad_input = after(blocks, small, grad_input)
+    blocks = jnp.concatenate([total_of(parts2[0], ring2), total_of(parts1[0], ring1)], axis=1)
+    blocks, small, grad_input, d_filt = after(blocks, small, grad_input, d_filt)
+    grad_input = input_grads(2, slots - 2, [grad_input], d_filt, d_above, d_below)
     sums = plane_exchanged(blocks)
     own = hidden // (8 * chips)
     grad_fc2 = sums[:own].reshape(-1, hidden)

time: 177 us -> 165 us (0.932)
  other arithmetic: 18.3 us -> 12.2 us
  waiting for transfers between devices: 19.4 us -> 15.5 us
  Pallas kernels: 78 us -> 81.2 us
  starting transfers between devices: 47.8 us -> 44.6 us
    all_to_all x2, waiting for transfers between devices: 17.9 us -> 12.7 us  [plane_exchanged(): lax.all_to_all(blocks.reshape(-1, blocks.shape[-1]), ('slide', 'row'), 0,...]
    convert_element_type x2, other arithmetic: 9.11 us -> 6.41 us  [quarters(): return [(cut(mine, by) + cut(got, by)).astype(bf16) for by in range(SIDE)]]
    pallas_call x1 -> x2, Pallas kernels: 13.3 us -> 15.7 us  [input_grads(): pl.pallas_call(functools.partial(input_kernel, first), grid=(some,), in_s...]
    all_to_all x1, waiting for transfers between devices: 0.01 us -> 1.88 us  [everywhere(): got = lax.all_to_all(sent, ('slide', 'row'), 0, 0, tiled=True)]
    convert_element_type x1 -> x0, other arithmetic: 1.78 us -> none  [body(): d_above, d_below = edges(d_cells.astype(bf16))]
  transfers between devices with their start and end apart: 15 -> 15, of which waited for: 4 -> 4; matrix products, arithmetic and copies ran while one was open for 10% -> 8% of each run, Pallas kernels for 14% -> 16%
where the time goes in v5:
time: 165 us
  Pallas kernels  81.2 us (49%)
  starting transfers between devices  44.6 us (27%)
  waiting for transfers between devices  15.5 us (9%)
  other arithmetic  12.2 us (7%)
  local copies, waits for them, and re-layouts  9.52 us (6%)
    pallas_call x1, Pallas kernels, body(): pl.pallas_call(mlp_kernel, grid=(hidden // BLOCK,), in_specs=[smem, smem,...  39.1 us
    pallas_call x2, Pallas kernels, input_grads(): pl.pallas_call(functools.partial(input_kernel, first), grid=(some,), in_s...  15.7 us
    pallas_call x1, Pallas kernels, body(): pl.pallas_call(forward_kernel, grid=(MOST,), in_specs=[smem, tile, edge,...  15.6 us
    all_to_all x2, starting transfers between devices, plane_exchanged(): lax.all_to_all(blocks.reshape(-1, blocks.shape[-1]), ('slide', 'row'), 0,...  13.7 us
    all_to_all x2, waiting for transfers between devices, plane_exchanged(): lax.all_to_all(blocks.reshape(-1, blocks.shape[-1]), ('slide', 'row'), 0,...  12.7 us
    pallas_call x1, Pallas kernels, body(): pl.pallas_call(tap_kernel, grid=(MOST,), in_specs=[tile, edge, edge, flat...  10.8 us
    all_to_all x1, starting transfers between devices, everywhere(): got = lax.all_to_all(sent, ('slide', 'row'), 0, 0, tiled=True)  9.92 us
    ppermute x2, starting transfers between devices, edges(): above = lax.ppermute(tail, 'row', [(i, i + 1) for i in range(ends)])  9.12 us
  transfers between devices with their start and end apart: 15, of which 4 were waited for; matrix products, arithmetic and copies ran while one was open for 8% of the time, Pallas kernels for 16%

profile of v5, /device:TPU:1, one launch (start us, length us, event | category | flops | bytes accessed | tf_op | source)
XLA Modules:
  0.0 164.6 jit_solution(4816165945319298006)
XLA Ops:
  1.7 1.3 collective-permute-start.1
  3.0 5.0 %collective-permute-start = (bf16[3,3,16,768]{3,2,1,0:T(8,128)(2,1)S(1)}, bf16[3,3,16,768]{3,2,1,0:T(8,128)(2,1)S(1)}, u32[]{:S(2)}, u32[]{:S(2)}) collective-permute-start(bf16[3,3,16,768]{3,2,1,0:T(8,128)(2,1)S(1)} %get-tuple-element.78), channel_id=1, source_target_pairs={{0,1},{1,2},{2,3},{4,5},{5,6},{6,7},{8,9},{9,10},{10,11},{12,13},{... | collective-permute-start | bytes 663560 | tf_op jit(solution)/shard_map/ppermute | solution.py:98
  8.7 1.3 broadcast_in_dim.13.gain
  12.8 15.6 %forward.1 = (bf16[768,768]{1,0:T(8,128)(2,1)}, f32[768,768]{1,0:T(8,128)}, f32[768,128]{1,0:T(8,128)}, bf16[768,768]{1,0:T(8,128)(2,1)}) custom-call(s32[1]{0:T(128)S(6)} %copy.17.count, bf16[1,4,16,16,768]{4,3,2,1,0:T(8,128)(2,1)} %tiles.5, bf16[3,3,16,768]{3,2,1,0:T(8,128)(2,1)} %copy-done.5, bf16[3,3,16,768]{3,2,1,0:T(8,128)(2,1)} %copy-done.4, ...), custom_call_target="tpu_custom_call" | custom-call | flops 1 | bytes 1 | tf_op jit(solution)/shard_map/forward/pallas_call | solution.py:391
  28.4 39.1 %mlp.1 = (bf16[4,4,4,24,768]{4,3,2,1,0:T(8,128)(2,1)}, bf16[4,4,4,24,768]{4,3,2,1,0:T(8,128)(2,1)}, bf16[4,4,4,24,768]{4,3,2,1,0:T(8,128)(2,1)}, bf16[4,4,4,24,7...) custom-call(s32[1]{0:T(128)} %bitcast.core, ...), custom_call_target="tpu_custom_call" | custom-call | flops 1 | bytes 1 | tf_op jit(solution)/shard_map/mlp/pallas_call | solution.py:418
  67.5 1.6 collective-permute-start.4
  69.3 4.1 %collective-permute-start.2 = (bf16[3,3,16,768]{3,2,1,0:T(8,128)(2,1)}, bf16[3,3,16,768]{3,2,1,0:T(8,128)(2,1)S(1)}, u32[]{:S(2)}, u32[]{:S(2)}) collective-permute-start(bf16[3,3,16,768]{3,2,1,0:T(8,128)(2,1)} %get-tuple-element.45), channel_id=1, source_target_pairs={{0,1},{1,2},{2,3},{4,5},{5,6},{6,7},{8,9},{9,10},{10,11},{12,13},{... | collective-permute-start | bytes 663560 | tf_op jit(solution)/shard_map/ppermute | solution.py:98
  73.4 1.3 collective-permute-start.3
  74.8 10.8 %taps.1 = bf16[16,8,768]{2,1,0:T(8,128)(2,1)} custom-call(bf16[1,4,16,16,768]{4,3,2,1,0:T(8,128)(2,1)} %tiles.5, bf16[3,3,16,768]{3,2,1,0:T(8,128)(2,1)} %copy-done.5, bf16[3,3,16,768]{3,2,1,0:T(8,128)(2,1)} %copy-done.4, f32[768,768]{1,0:T(8,128)} %get-tuple-element.63.d_filt, f32[8,768]{1,0:T(8,128)} %get-tuple-element.43.gains, ...), custom_call_target="tpu_custom_call" | custom-call | flops 1 | bytes 1 | tf_op jit(solution)/shard_map/taps/pallas_call | solution.py:478
  85.6 1.5 copy-done.1
  87.2 3.5 %fusion.7 = (bf16[4,4,24,768]{3,2,1,0:T(8,128)(2,1)}, bf16[4,4,24,768]{3,2,1,0:T(8,128)(2,1)}, bf16[4,4,24,768]{3,2,1,0:T(8,128)(2,1)}) fusion(bf16[4,4,4,24,768]{4,3,2,1,0:T(8,128)(2,1)} %collective-permute-done.5, s32[]{:T(128)S(6)} %select_n.98, bf16[4,4,4,24,768]{4,3,2,1,0:T(8,128)(2,1)} %get-tuple-element.51, s32[]{:T(128)S(6)} %select_n.102, ...), kind=kLoop, calls=%fused_computation.21 | loop fusion | flops 3538944 | bytes 5308428 | tf_op jit(solution)/shard_map/convert_element_type | solution.py:45
  91.9 2.4 %collective-permute-start.7 = (bf16[4,4,24,768]{3,2,1,0:T(8,128)(2,1)}, bf16[4,4,24,768]{3,2,1,0:T(8,128)(2,1)}, u32[]{:S(2)}, u32[]{:S(2)}) collective-permute-start(bf16[4,4,24,768]{3,2,1,0:T(8,128)(2,1)} %get-tuple-element.73), channel_id=1, source_target_pairs={{0,2},{4,20},{1,3},{5,21},{2,0},{6,22},{3,1},{7,23},{8,10},{12,28}... | collective-permute-start | bytes 1769480 | tf_op jit(solution)/shard_map/ppermute | solution.py:61
  95.5 8.3 %all-to-all-start = ((bf16[16,8,768]{2,1,0:T(8,128)(2,1)}), bf16[16,8,768]{2,1,0:T(8,128)(2,1)S(1)}, u32[]{:S(2)}, u32[]{:S(2)}) async-start(bf16[16,8,768]{2,1,0:T(8,128)(2,1)} %taps.1), calls=%async_computation | async-start | bytes 393216 | tf_op jit(solution)/shard_map/all_to_all | solution.py:75
  103.9 2.9 %fusion.11 = (bf16[4,4,24,768]{3,2,1,0:T(8,128)(2,1)}, bf16[4,4,24,768]{3,2,1,0:T(8,128)(2,1)}, bf16[4,4,24,768]{3,2,1,0:T(8,128)(2,1)}) fusion(bf16[4,4,4,24,768]{4,3,2,1,0:T(8,128)(2,1)} %copy-done.1, s32[]{:T(128)S(6)} %select_n.98, bf16[4,4,4,24,768]{4,3,2,1,0:T(8,128)(2,1)S(1)} %copy-done, s32[]{:T(128)S(6)} %select_n.102, s32[]{:T(128)S(6)} %select_n.100), kind=kLoop, calls=%fused_computation.25 | loop fusion | flops 3538944 | bytes 5308428 | tf_op jit(solution)/shard_map/convert_element_type | solution.py:45
  107.9 1.6 collective-permute-start.11
  109.5 1.4 all-to-all-done
  112.0 9.9 %all-to-all-start.1 = ((bf16[128,24,128]{2,1,0:T(8,128)(2,1)}), bf16[128,24,128]{2,1,0:T(8,128)(2,1)S(1)}, u32[]{:S(2)}, u32[]{:S(2)}) async-start(bf16[128,24,128]{2,1,0:T(8,128)(2,1)} %broadcast_in_dim.16), calls=%async_computation.1 | async-start | bytes 1572864 | tf_op jit(solution)/shard_map/all_to_all | solution.py:90
  121.9 9.5 %inputs.2.refs_0_ = f32[1,4,16,16,768]{4,3,2,1,0:T(8,128)} custom-call(s32[1]{0:T(128)S(6)} %copy.17.count, f32[768,768]{1,0:T(8,128)} %get-tuple-element.63.d_filt, bf16[3,3,16,768]{3,2,1,0:T(8,128)(2,1)} %copy-done.2, bf16[3,3,16,768]{3,2,1,0:T(8,128)(2,1)} %copy-done.3, bf16[1,4,16,16,768]{4,3,2,1,0:T(8,128)(2,1)} %cotan.7, f32[7,7,768]{2,1,0:T(8,128)} %kernel.5), custom_call_target="tpu_custom_call" | custom-call | flops 1 | bytes 1 | tf_op jit(solution)/shard_map/inputs/pallas_call | solution.py:506
  131.4 2.1 %fusion.5 = bf16[4,4,24,768]{3,2,1,0:T(8,128)(2,1)S(1)} fusion(bf16[4,4,24,768]{3,2,1,0:T(8,128)(2,1)} %collective-permute-done.8, bf16[4,4,24,768]{3,2,1,0:T(8,128)(2,1)} %collective-permute-done.7, bf16[4,4,24,768]{3,2,1,0:T(8,128)(2,1)} %collective-permute-done.6, bf16[4,4,4,24,768]{4,3,2,1,0:T(8,128)(2,1)} %collective-permute-done.5, s32[]{:T(128)S(6)} %select_n.96, ...), kind=kLoop, calls=%fused_computation.9 | loop fusion | flops 3538944 | bytes 3538948 | tf_op jit(solution)/shard_map/convert_element_type | solution.py:68
  133.6 2.0 %fusion.2 = bf16[4,4,24,768]{3,2,1,0:T(8,128)(2,1)S(1)} fusion(bf16[4,4,24,768]{3,2,1,0:T(8,128)(2,1)} %collective-permute-done.11, bf16[4,4,24,768]{3,2,1,0:T(8,128)(2,1)} %collective-permute-done.10, bf16[4,4,24,768]{3,2,1,0:T(8,128)(2,1)} %collective-permute-done.9, bf16[4,4,4,24,768]{4,3,2,1,0:T(8,128)(2,1)} %copy-done.1, s32[]{:T(128)S(6)} %select_n.96, ...), kind=kLoop, calls=%fused_computation.5 | loop fusion | flops 3538944 | bytes 3538948 | tf_op jit(solution)/shard_map/convert_element_type | solution.py:68
  136.7 1.9 %all-to-all-done.1 = bf16[128,24,128]{2,1,0:T(8,128)(2,1)S(1)} async-done(((bf16[128,24,128]{2,1,0:T(8,128)(2,1)}), bf16[128,24,128]{2,1,0:T(8,128)(2,1)S(1)}, u32[]{:S(2)}, u32[]{:S(2)}) %all-to-all-start.1) | async-done | bytes 786464 | tf_op jit(solution)/shard_map/all_to_all | solution.py:90
  139.0 5.3 %all-to-all-start.2 = ((bf16[16,48,768]{2,1,0:T(8,128)(2,1)}), bf16[16,48,768]{2,1,0:T(8,128)(2,1)S(1)}, u32[]{:S(2)}, u32[]{:S(2)}) async-start(bf16[16,48,768]{2,1,0:T(8,128)(2,1)} %pad_maximum_fusion), calls=%async_computation.2 | async-start | bytes 2359296 | tf_op jit(solution)/shard_map/all_to_all | solution.py:75
  144.3 6.2 %inputs.3 = f32[1,4,16,16,768]{4,3,2,1,0:T(8,128)} custom-call(s32[1]{0:T(128)S(6)} %copy.17.count, f32[768,768]{1,0:T(8,128)} %get-tuple-element.63.d_filt, bf16[3,3,16,768]{3,2,1,0:T(8,128)(2,1)} %copy-done.2, bf16[3,3,16,768]{3,2,1,0:T(8,128)(2,1)} %copy-done.3, bf16[1,4,16,16,768]{4,3,2,1,0:T(8,128)(2,1)} %cotan.7, ...), custom_call_target="tpu_custom_call", output_to_operand_aliasing={{}: (6, {})} | custom-call | flops 1 | bytes 1 | tf_op jit(solution)/shard_map/inputs/pallas_call | solution.py:506
  151.8 11.3 %all-to-all-done.2 = bf16[16,48,768]{2,1,0:T(8,128)(2,1)S(1)} async-done(((bf16[16,48,768]{2,1,0:T(8,128)(2,1)}), bf16[16,48,768]{2,1,0:T(8,128)(2,1)S(1)}, u32[]{:S(2)}, u32[]{:S(2)}) %all-to-all-start.2) | async-done | bytes 1179680 | tf_op jit(solution)/shard_map/all_to_all | solution.py:75
  (45 shorter events, 12.9 us)
Async XLA Ops:
  1.7 9.5 %collective-permute-start.1 = (bf16[3,3,16,768]{3,2,1,0:T(8,128)(2,1)S(1)}, bf16[3,3,16,768]{3,2,1,0:T(8,128)(2,1)S(1)}, u32[]{:S(2)}, u32[]{:S(2)}) collective-permute-start(bf16[3,3,16,768]{3,2,1,0:T(8,128)(2,1)S(1)} %get-tuple-element.77), channel_id=1, source_target_pairs={{1,0},{2,1},{3,2},{5,4},{6,5},{7,6},{9,8},{10,9},{11,10},{13,12},{... | collective-permute-start | bytes 663560 | tf_op jit(solution)/shard_map/ppermute | solution.py:99
  3.0 9.1 %collective-permute-start = (bf16[3,3,16,768]{3,2,1,0:T(8,128)(2,1)S(1)}, bf16[3,3,16,768]{3,2,1,0:T(8,128)(2,1)S(1)}, u32[]{:S(2)}, u32[]{:S(2)}) collective-permute-start(bf16[3,3,16,768]{3,2,1,0:T(8,128)(2,1)S(1)} %get-tuple-element.78), channel_id=1, source_target_pairs={{0,1},{1,2},{2,3},{4,5},{5,6},{6,7},{8,9},{9,10},{10,11},{12,13},{... | collective-permute-start | bytes 663560 | tf_op jit(solution)/shard_map/ppermute | solution.py:98
  11.2 0.9 copy-start.4
  12.1 0.7 copy-start.5
  67.5 18.1 %collective-permute-start.4 = (bf16[4,4,4,24,768]{4,3,2,1,0:T(8,128)(2,1)}, bf16[4,4,4,24,768]{4,3,2,1,0:T(8,128)(2,1)S(1)}, u32[]{:S(2)}, u32[]{:S(2)}) collective-permute-start(bf16[4,4,4,24,768]{4,3,2,1,0:T(8,128)(2,1)} %get-tuple-element.48), channel_id=1, source_target_pairs={{0,4},{4,0},{8,12},{12,8},{16,20},{20,16},{24,28},{28,24},{32,36},... | collective-permute-start | bytes 7077896 | tf_op jit(solution)/shard_map/ppermute | solution.py:35
  69.2 16.4 %collective-permute-start.5 = (bf16[4,4,4,24,768]{4,3,2,1,0:T(8,128)(2,1)}, bf16[4,4,4,24,768]{4,3,2,1,0:T(8,128)(2,1)}, u32[]{:S(2)}, u32[]{:S(2)}) collective-permute-start(bf16[4,4,4,24,768]{4,3,2,1,0:T(8,128)(2,1)} %get-tuple-element.50), channel_id=1, source_target_pairs={{0,4},{4,0},{8,12},{12,8},{16,20},{20,16},{24,28},{28,24},{32,36},... | collective-permute-start | bytes 7077896 | tf_op jit(solution)/shard_map/ppermute | solution.py:35
  69.3 16.3 %collective-permute-start.2 = (bf16[3,3,16,768]{3,2,1,0:T(8,128)(2,1)}, bf16[3,3,16,768]{3,2,1,0:T(8,128)(2,1)S(1)}, u32[]{:S(2)}, u32[]{:S(2)}) collective-permute-start(bf16[3,3,16,768]{3,2,1,0:T(8,128)(2,1)} %get-tuple-element.45), channel_id=1, source_target_pairs={{0,1},{1,2},{2,3},{4,5},{5,6},{6,7},{8,9},{9,10},{10,11},{12,13},{... | collective-permute-start | bytes 663560 | tf_op jit(solution)/shard_map/ppermute | solution.py:98
  73.4 12.2 %collective-permute-start.3 = (bf16[3,3,16,768]{3,2,1,0:T(8,128)(2,1)}, bf16[3,3,16,768]{3,2,1,0:T(8,128)(2,1)S(1)}, u32[]{:S(2)}, u32[]{:S(2)}) collective-permute-start(bf16[3,3,16,768]{3,2,1,0:T(8,128)(2,1)} %get-tuple-element.46), channel_id=1, source_target_pairs={{1,0},{2,1},{3,2},{5,4},{6,5},{7,6},{9,8},{10,9},{11,10},{13,12},{... | collective-permute-start | bytes 663560 | tf_op jit(solution)/shard_map/ppermute | solution.py:99
  85.6 21.2 %copy-start.2 = (bf16[3,3,16,768]{3,2,1,0:T(8,128)(2,1)}, bf16[3,3,16,768]{3,2,1,0:T(8,128)(2,1)S(1)}, u32[]{:S(2)}) copy-start(bf16[3,3,16,768]{3,2,1,0:T(8,128)(2,1)S(1)} %collective-permute-done.2.above) | copy-start | bytes 663556
  85.6 21.1 %copy-start.3 = (bf16[3,3,16,768]{3,2,1,0:T(8,128)(2,1)}, bf16[3,3,16,768]{3,2,1,0:T(8,128)(2,1)S(1)}, u32[]{:S(2)}) copy-start(bf16[3,3,16,768]{3,2,1,0:T(8,128)(2,1)S(1)} %collective-permute-done.3.below) | copy-start | bytes 663556
  85.6 1.5 copy-start.1
  87.2 16.7 %copy-start = (bf16[4,4,4,24,768]{4,3,2,1,0:T(8,128)(2,1)S(1)}, bf16[4,4,4,24,768]{4,3,2,1,0:T(8,128)(2,1)}, u32[]{:S(2)}) copy-start(bf16[4,4,4,24,768]{4,3,2,1,0:T(8,128)(2,1)} %get-tuple-element.53) | copy-start | bytes 7077892
  90.7 17.2 %collective-permute-start.6 = (bf16[4,4,24,768]{3,2,1,0:T(8,128)(2,1)}, bf16[4,4,24,768]{3,2,1,0:T(8,128)(2,1)}, u32[]{:S(2)}, u32[]{:S(2)}) collective-permute-start(bf16[4,4,24,768]{3,2,1,0:T(8,128)(2,1)} %get-tuple-element.71), channel_id=1, source_target_pairs={{0,1},{4,12},{1,2},{5,13},{2,3},{6,14},{3,0},{7,15},{8,9},{12,20},... | collective-permute-start | bytes 1769480 | tf_op jit(solution)/shard_map/ppermute | solution.py:61
  91.9 39.5 %collective-permute-start.7 = (bf16[4,4,24,768]{3,2,1,0:T(8,128)(2,1)}, bf16[4,4,24,768]{3,2,1,0:T(8,128)(2,1)}, u32[]{:S(2)}, u32[]{:S(2)}) collective-permute-start(bf16[4,4,24,768]{3,2,1,0:T(8,128)(2,1)} %get-tuple-element.73), channel_id=1, source_target_pairs={{0,2},{4,20},{1,3},{5,21},{2,0},{6,22},{3,1},{7,23},{8,10},{12,28}... | collective-permute-start | bytes 1769480 | tf_op jit(solution)/shard_map/ppermute | solution.py:61
  94.3 37.1 %collective-permute-start.8 = (bf16[4,4,24,768]{3,2,1,0:T(8,128)(2,1)}, bf16[4,4,24,768]{3,2,1,0:T(8,128)(2,1)}, u32[]{:S(2)}, u32[]{:S(2)}) collective-permute-start(bf16[4,4,24,768]{3,2,1,0:T(8,128)(2,1)} %get-tuple-element.72), channel_id=1, source_target_pairs={{0,3},{4,28},{1,0},{5,29},{2,1},{6,30},{3,2},{7,31},{8,11},{12,4},... | collective-permute-start | bytes 1769480 | tf_op jit(solution)/shard_map/ppermute | solution.py:61
  95.5 15.4 %all-to-all-start = ((bf16[16,8,768]{2,1,0:T(8,128)(2,1)}), bf16[16,8,768]{2,1,0:T(8,128)(2,1)S(1)}, u32[]{:S(2)}, u32[]{:S(2)}) async-start(bf16[16,8,768]{2,1,0:T(8,128)(2,1)} %taps.1), calls=%async_computation | async-start | bytes 393216 | tf_op jit(solution)/shard_map/all_to_all | solution.py:75
  106.7 26.8 %collective-permute-start.9 = (bf16[4,4,24,768]{3,2,1,0:T(8,128)(2,1)}, bf16[4,4,24,768]{3,2,1,0:T(8,128)(2,1)}, u32[]{:S(2)}, u32[]{:S(2)}) collective-permute-start(bf16[4,4,24,768]{3,2,1,0:T(8,128)(2,1)} %get-tuple-element.74), channel_id=1, source_target_pairs={{0,1},{4,12},{1,2},{5,13},{2,3},{6,14},{3,0},{7,15},{8,9},{12,20},... | collective-permute-start | bytes 1769480 | tf_op jit(solution)/shard_map/ppermute | solution.py:61
  107.1 26.5 %collective-permute-start.10 = (bf16[4,4,24,768]{3,2,1,0:T(8,128)(2,1)}, bf16[4,4,24,768]{3,2,1,0:T(8,128)(2,1)}, u32[]{:S(2)}, u32[]{:S(2)}) collective-permute-start(bf16[4,4,24,768]{3,2,1,0:T(8,128)(2,1)} %get-tuple-element.76), channel_id=1, source_target_pairs={{0,2},{4,20},{1,3},{5,21},{2,0},{6,22},{3,1},{7,23},{8,10},{12,28}... | collective-permute-start | bytes 1769480 | tf_op jit(solution)/shard_map/ppermute | solution.py:61
  107.9 25.7 %collective-permute-start.11 = (bf16[4,4,24,768]{3,2,1,0:T(8,128)(2,1)}, bf16[4,4,24,768]{3,2,1,0:T(8,128)(2,1)}, u32[]{:S(2)}, u32[]{:S(2)}) collective-permute-start(bf16[4,4,24,768]{3,2,1,0:T(8,128)(2,1)} %get-tuple-element.75), channel_id=1, source_target_pairs={{0,3},{4,28},{1,0},{5,29},{2,1},{6,30},{3,2},{7,31},{8,11},{12,4},... | collective-permute-start | bytes 1769480 | tf_op jit(solution)/shard_map/ppermute | solution.py:61
  112.0 26.6 %all-to-all-start.1 = ((bf16[128,24,128]{2,1,0:T(8,128)(2,1)}), bf16[128,24,128]{2,1,0:T(8,128)(2,1)S(1)}, u32[]{:S(2)}, u32[]{:S(2)}) async-start(bf16[128,24,128]{2,1,0:T(8,128)(2,1)} %broadcast_in_dim.16), calls=%async_computation.1 | async-start | bytes 1572864 | tf_op jit(solution)/shard_map/all_to_all | solution.py:90
  139.0 24.2 %all-to-all-start.2 = ((bf16[16,48,768]{2,1,0:T(8,128)(2,1)}), bf16[16,48,768]{2,1,0:T(8,128)(2,1)S(1)}, u32[]{:S(2)}, u32[]{:S(2)}) async-start(bf16[16,48,768]{2,1,0:T(8,128)(2,1)} %pad_maximum_fusion), calls=%async_computation.2 | async-start | bytes 2359296 | tf_op jit(solution)/shard_map/all_to_all | solution.py:75

commit v6 on v5

--- a/solution.py
+++ b/solution.py
@@ -155,11 +155,11 @@
         wide[tap] = jnp.broadcast_to(kernel_ref[a, b : b + 1, :], wide.shape[1:])
 
 
-def forward_kernel(
-    count, tiles, above, below, cotan, kernel, gain, scale, normed, unit, spread, held_out, pad, wide, filt
+def forward_step(
+    slot, count, tiles, above, below, cotan, kernel, gain, scale, normed, unit, inv, spread, pad, wide, filt
 ):
-    slot = pl.program_id(0)
     rows, cols, chans = tiles.shape[2:]
+    base = slot * rows * cols
 
     @pl.when(slot == 0)
     def _():
@@ -167,17 +167,18 @@
         clear_padded(pad)
 
     def line_of(r, lanes):
-        return tiles[0, 0, r, :, lanes]
-
-    fill_padded(pad, above, line_of, below, rows, cols, chans)
+        return tiles[0, slot, r, :, lanes]
+
+    here = pl.ds(slot, 1)
+    fill_padded(pad, above.at[here], line_of, below.at[here], rows, cols, chans)
 
     def emit(p, half, lanes, value):
         filt[pl.ds(p * cols + 8 * half, 8), lanes] = value
 
     stencil(pad, wide, rows, cols, chans, False, emit)
     weight = (slot < count[0]).astype(f32)
-    held = cotan[...].reshape(rows * cols, chans).astype(f32) * weight
-    held_out[...] = (held * scale[...]).astype(bf16)
+    held = cotan[0, slot].reshape(rows * cols, chans).astype(f32) * weight
+    spread[pl.ds(pl.multiple_of(base, 256), rows * cols), :] = (held * scale[...]).astype(bf16)
 
     def norm(i, carry):
         at = pl.ds(pl.multiple_of(i * 64, 64), 64)
@@ -185,9 +186,10 @@
         center = value - jnp.mean(value, axis=-1, keepdims=True)
         inv_std = lax.rsqrt(jnp.mean(center * center, axis=-1, keepdims=True) + epsilon)
         one = center * inv_std
-        unit[at, :] = one
-        normed[at, :] = (one * gain[...]).astype(bf16)
-        spread[at, :] = jnp.broadcast_to(inv_std, (64, LANES))
+        to = pl.ds(pl.multiple_of(base + i * 64, 64), 64)
+        unit[to, :] = one
+        normed[to, :] = (one * gain[...]).astype(bf16)
+        inv[to, :] = jnp.broadcast_to(inv_std, (64, LANES))
         return carry
 
     lax.fori_loop(0, rows * cols // 64, norm, 0)
@@ -214,12 +216,33 @@
             rows_at(half, (at[0], y, at[1]), pl.ds(begin, count))
 
 
-def mlp_kernel(
-    core, count, normed, spread, first, second, unit, inv, gain, scale, tiles, cotan,
+def main_kernel(
+    core, count, above, below, kernel, first, second, gain, scale, tiles, cotan,
+    mine1, other1, mine2, other2, d_filt, d_head, d_tail, out, gain_grad, scale_grad,
+    normed, spread, unit, inv, pad, wide, filt, *scratch,
+):
+    at = pl.program_id(0)
+
+    @pl.when(at < MOST)
+    def _():
+        forward_step(
+            at, count, tiles, above, below, cotan, kernel, gain, scale,
+            normed, unit, inv, spread, pad, wide, filt,
+        )
+
+    @pl.when(at >= MOST)
+    def _():
+        mlp_step(
+            at - MOST, core, count, normed, spread, first, second, unit, inv, gain, scale, tiles, cotan,
+            mine1, other1, mine2, other2, d_filt, d_head, d_tail, out, gain_grad, scale_grad, *scratch,
+        )
+
+
+def mlp_step(
+    step, core, count, normed, spread, first, second, unit, inv, gain, scale, tiles, cotan,
     mine1, other1, mine2, other2, d_filt, d_head, d_tail, out, gain_grad, scale_grad,
     turned, total2, term, back, branch,
 ):
-    step = pl.program_id(0)
     pixels, chans = normed.shape
     rows, cols = tiles.shape[2:4]
 
@@ -252,7 +275,7 @@
     split_rows(core, mine1, other1, 0, 0, copy1)
     back[...] += jnp.dot(d_pre, first[...], preferred_element_type=f32)
 
-    @pl.when(step == pl.num_programs(0) - 1)
+    @pl.when(step == total2.shape[1] // BLOCK - 1)
     def _():
         def copy2(half, chip, at):
             for i in range(BLOCK // LANES):
@@ -388,23 +411,6 @@
     pad = pltpu.VMEM((chans // LANES, (rows + 2 * REACH) * PITCH + 8, LANES), f32)
     wide = pltpu.VMEM((TAPS * TAPS, 8, chans), f32)
 
-    normed, unit, inv, spread = pl.pallas_call(
-        forward_kernel,
-        grid=(MOST,),
-        in_specs=[smem, tile, edge, edge, tile, whole(TAPS, TAPS, chans), whole(1, chans), whole(1, chans)],
-        out_specs=[flat, flat, pl.BlockSpec((pixels, LANES), lambda s: (s, 0)), flat],
-        out_shape=[
-            shape((every, chans), bf16),
-            shape((every, chans), f32),
-            shape((every, LANES), f32),
-            shape((every, chans), bf16),
-        ],
-        scratch_shapes=[pad, wide, pltpu.VMEM((pixels, chans), f32)],
-        compiler_params=params,
-        cost_estimate=brief,
-        name="forward",
-    )(tile_counts, tiles, above, below, cotangent, dw_kernel, gain, scale)
-
     chips = SIDE * SIDE
     halves = shape((SIDE, SIDE, SIDE, hidden // (8 * chips), chans), bf16)
     d_edge = shape((MOST, REACH, cols, chans), bf16)
@@ -413,20 +419,22 @@
     def once(*dims):
         return pl.BlockSpec(dims, lambda s: (0,) * len(dims), pipeline_mode=pl.Buffered(1))
 
-    quarter_of = pl.BlockSpec((SIDE, 1, *halves.shape[2:]), lambda j: (0, j, 0, 0, 0))
+    def block(j):
+        return jnp.maximum(j - MOST, 0)
+
+    quarter_of = pl.BlockSpec((SIDE, 1, *halves.shape[2:]), lambda j: (0, block(j), 0, 0, 0))
     live = once(1, MOST, rows, cols, chans)
     mine1, other1, mine2, other2, d_filt, d_head, d_tail, block_out, gain_grad, scale_grad = pl.pallas_call(
-        mlp_kernel,
-        grid=(hidden // BLOCK,),
+        main_kernel,
+        grid=(MOST + hidden // BLOCK,),
         in_specs=[
             smem,
             smem,
-            once(every, chans),
-            once(every, chans),
-            pl.BlockSpec((BLOCK, chans), lambda j: (j, 0)),
-            pl.BlockSpec((chans, BLOCK), lambda j: (0, j)),
-            once(every, chans),
-            once(every, LANES),
+            once(*above.shape),
+            once(*below.shape),
+            once(*dw_kernel.shape),
+            pl.BlockSpec((BLOCK, chans), lambda j: (block(j), 0)),
+            pl.BlockSpec((chans, BLOCK), lambda j: (0, block(j))),
             once(1, chans),
             once(1, chans),
             live,
@@ -457,6 +465,13 @@
             shape((8, chans), f32),
         ],
         scratch_shapes=[
+            pltpu.VMEM((every, chans), bf16),
+            pltpu.VMEM((every, chans), bf16),
+            pltpu.VMEM((every, chans), f32),
+            pltpu.VMEM((every, LANES), f32),
+            pad,
+            wide,
+            pltpu.VMEM((pixels, chans), f32),
             pltpu.VMEM((chans, every), bf16),
             pltpu.VMEM((chans // LANES, hidden, LANES), f32),
             pltpu.VMEM((BLOCK, chans), f32),
@@ -465,9 +480,9 @@
         ],
         compiler_params=params,
         cost_estimate=brief,
-        name="mlp",
+        name="main",
     )(
-        core, tile_counts, normed, spread, fc1_weight, fc2_weight, unit, inv, gain, scale, tiles, cotangent
+        core, tile_counts, above, below, dw_kernel, fc1_weight, fc2_weight, gain, scale, tiles, cotangent
     )
 
     got2, got1 = from_other_core(other2), from_other_core(other1)

time: 165 us -> 162 us (0.982)
  Pallas kernels: 81.2 us -> 77.6 us
    pallas_call x2 -> x1, Pallas kernels: 54.8 us -> 51.2 us  [body(): pl.pallas_call(main_kernel, grid=(MOST + hidden // BLOCK,), in_specs=[sme...]
where the time goes in v6:
time: 162 us; the launch traced here: 161 us
  Pallas kernels  77.6 us (48%)
  starting transfers between devices  44.7 us (28%)
  waiting for transfers between devices  15.4 us (10%)
  other arithmetic  12.2 us (8%)
  local copies, waits for them, and re-layouts  9.49 us (6%)
  between operations  1.62 us (1%)
    pallas_call x1, Pallas kernels, body(): pl.pallas_call(main_kernel, grid=(MOST + hidden // BLOCK,), in_specs=[sme...  51.2 us
    pallas_call x2, Pallas kernels, input_grads(): pl.pallas_call(functools.partial(input_kernel, first), grid=(some,), in_s...  15.7 us
    all_to_all x2, starting transfers between devices, plane_exchanged(): lax.all_to_all(blocks.reshape(-1, blocks.shape[-1]), ('slide', 'row'), 0,...  13.7 us
    all_to_all x2, waiting for transfers between devices, plane_exchanged(): lax.all_to_all(blocks.reshape(-1, blocks.shape[-1]), ('slide', 'row'), 0,...  12.7 us
    pallas_call x1, Pallas kernels, body(): pl.pallas_call(tap_kernel, grid=(MOST,), in_specs=[tile, edge, edge, flat...  10.8 us
    all_to_all x1, starting transfers between devices, everywhere(): got = lax.all_to_all(sent, ('slide', 'row'), 0, 0, tiled=True)  9.93 us
    ppermute x2, starting transfers between devices, edges(): above = lax.ppermute(tail, 'row', [(i, i + 1) for i in range(ends)])  9.12 us
    ppermute x6, starting transfers between devices, ring_sent(): lax.ppermute(parts[by], ('slide', 'row'), pairs[by])  7.62 us
  transfers between devices with their start and end apart: 15, of which 4 were waited for; matrix products, arithmetic and copies ran while one was open for 8% of the time, Pallas kernels for 16%

profile of v6, /device:TPU:1, one launch (start us, length us, event | category | flops | bytes accessed | tf_op | source)
XLA Modules:
  0.0 161.0 jit_solution(2439695698652356047)
XLA Ops:
  1.7 1.3 collective-permute-start.1
  3.0 5.0 %collective-permute-start = (bf16[3,3,16,768]{3,2,1,0:T(8,128)(2,1)S(1)}, bf16[3,3,16,768]{3,2,1,0:T(8,128)(2,1)S(1)}, u32[]{:S(2)}, u32[]{:S(2)}) collective-permute-start(bf16[3,3,16,768]{3,2,1,0:T(8,128)(2,1)S(1)} %get-tuple-element.70), channel_id=1, source_target_pairs={{0,1},{1,2},{2,3},{4,5},{5,6},{6,7},{8,9},{9,10},{10,11},{12,13},{... | collective-permute-start | bytes 663560 | tf_op jit(solution)/shard_map/ppermute | solution.py:98
  8.7 1.3 broadcast_in_dim.13.gain
  10.0 1.3 broadcast_in_dim.14.scale
  12.8 51.2 %main.1 = (bf16[4,4,4,24,768]{4,3,2,1,0:T(8,128)(2,1)}, bf16[4,4,4,24,768]{4,3,2,1,0:T(8,128)(2,1)}, bf16[4,4,4,24,768]{4,3,2,1,0:T(8,128)(2,1)}, bf16[4,4,4,24,...) custom-call(s32[1]{0:T(128)} %bitcast.core, ...), custom_call_target="tpu_custom_call" | custom-call | flops 1 | bytes 1 | tf_op jit(solution)/shard_map/main/pallas_call | solution.py:427
  63.9 1.6 %collective-permute-start.4 = (bf16[4,4,4,24,768]{4,3,2,1,0:T(8,128)(2,1)}, bf16[4,4,4,24,768]{4,3,2,1,0:T(8,128)(2,1)S(1)}, u32[]{:S(2)}, u32[]{:S(2)}) collective-permute-start(bf16[4,4,4,24,768]{4,3,2,1,0:T(8,128)(2,1)} %get-tuple-element.40), channel_id=1, source_target_pairs={{0,4},{4,0},{8,12},{12,8},{16,20},{20,16},{24,28},{28,24},{32,36},... | collective-permute-start | bytes 7077896 | tf_op jit(solution)/shard_map/ppermute | solution.py:35
  65.7 4.1 %collective-permute-start.2 = (bf16[3,3,16,768]{3,2,1,0:T(8,128)(2,1)}, bf16[3,3,16,768]{3,2,1,0:T(8,128)(2,1)S(1)}, u32[]{:S(2)}, u32[]{:S(2)}) collective-permute-start(bf16[3,3,16,768]{3,2,1,0:T(8,128)(2,1)} %get-tuple-element.37), channel_id=1, source_target_pairs={{0,1},{1,2},{2,3},{4,5},{5,6},{6,7},{8,9},{9,10},{10,11},{12,13},{... | collective-permute-start | bytes 663560 | tf_op jit(solution)/shard_map/ppermute | solution.py:98
  69.8 1.3 collective-permute-start.3
  71.2 10.8 %taps.1 = bf16[16,8,768]{2,1,0:T(8,128)(2,1)} custom-call(bf16[1,4,16,16,768]{4,3,2,1,0:T(8,128)(2,1)} %tiles.3, bf16[3,3,16,768]{3,2,1,0:T(8,128)(2,1)} %copy-done.5, bf16[3,3,16,768]{3,2,1,0:T(8,128)(2,1)} %copy-done.4, f32[768,768]{1,0:T(8,128)} %get-tuple-element.55.d_filt, f32[8,768]{1,0:T(8,128)} %get-tuple-element.35.gains, ...), custom_call_target="tpu_custom_call" | custom-call | flops 1 | bytes 1 | tf_op jit(solution)/shard_map/taps/pallas_call | solution.py:493
  82.0 1.5 copy-done.1
  83.5 3.6 %fusion.7 = (bf16[4,4,24,768]{3,2,1,0:T(8,128)(2,1)}, bf16[4,4,24,768]{3,2,1,0:T(8,128)(2,1)}, bf16[4,4,24,768]{3,2,1,0:T(8,128)(2,1)}) fusion(bf16[4,4,4,24,768]{4,3,2,1,0:T(8,128)(2,1)} %collective-permute-done.5, s32[]{:T(128)S(6)} %select_n.98, bf16[4,4,4,24,768]{4,3,2,1,0:T(8,128)(2,1)} %get-tuple-element.43, s32[]{:T(128)S(6)} %select_n.102, ...), kind=kLoop, calls=%fused_computation.21 | loop fusion | flops 3538944 | bytes 5308428 | tf_op jit(solution)/shard_map/convert_element_type | solution.py:45
  88.3 2.4 %collective-permute-start.7 = (bf16[4,4,24,768]{3,2,1,0:T(8,128)(2,1)}, bf16[4,4,24,768]{3,2,1,0:T(8,128)(2,1)}, u32[]{:S(2)}, u32[]{:S(2)}) collective-permute-start(bf16[4,4,24,768]{3,2,1,0:T(8,128)(2,1)} %get-tuple-element.65), channel_id=1, source_target_pairs={{0,2},{4,20},{1,3},{5,21},{2,0},{6,22},{3,1},{7,23},{8,10},{12,28}... | collective-permute-start | bytes 1769480 | tf_op jit(solution)/shard_map/ppermute | solution.py:61
  91.9 8.3 %all-to-all-start = ((bf16[16,8,768]{2,1,0:T(8,128)(2,1)}), bf16[16,8,768]{2,1,0:T(8,128)(2,1)S(1)}, u32[]{:S(2)}, u32[]{:S(2)}) async-start(bf16[16,8,768]{2,1,0:T(8,128)(2,1)} %taps.1), calls=%async_computation | async-start | bytes 393216 | tf_op jit(solution)/shard_map/all_to_all | solution.py:75
  100.3 2.9 %fusion.11 = (bf16[4,4,24,768]{3,2,1,0:T(8,128)(2,1)}, bf16[4,4,24,768]{3,2,1,0:T(8,128)(2,1)}, bf16[4,4,24,768]{3,2,1,0:T(8,128)(2,1)}) fusion(bf16[4,4,4,24,768]{4,3,2,1,0:T(8,128)(2,1)} %copy-done.1, s32[]{:T(128)S(6)} %select_n.98, bf16[4,4,4,24,768]{4,3,2,1,0:T(8,128)(2,1)S(1)} %copy-done, s32[]{:T(128)S(6)} %select_n.102, s32[]{:T(128)S(6)} %select_n.100), kind=kLoop, calls=%fused_computation.25 | loop fusion | flops 3538944 | bytes 5308428 | tf_op jit(solution)/shard_map/convert_element_type | solution.py:45
  104.4 1.6 collective-permute-start.11
  106.0 1.4 all-to-all-done
  108.4 9.9 %all-to-all-start.1 = ((bf16[128,24,128]{2,1,0:T(8,128)(2,1)}), bf16[128,24,128]{2,1,0:T(8,128)(2,1)S(1)}, u32[]{:S(2)}, u32[]{:S(2)}) async-start(bf16[128,24,128]{2,1,0:T(8,128)(2,1)} %broadcast_in_dim.16), calls=%async_computation.1 | async-start | bytes 1572864 | tf_op jit(solution)/shard_map/all_to_all | solution.py:90
  118.4 9.5 %inputs.2.refs_0_ = f32[1,4,16,16,768]{4,3,2,1,0:T(8,128)} custom-call(s32[1]{0:T(128)S(6)} %copy.17.count, f32[768,768]{1,0:T(8,128)} %get-tuple-element.55.d_filt, bf16[3,3,16,768]{3,2,1,0:T(8,128)(2,1)} %copy-done.2, bf16[3,3,16,768]{3,2,1,0:T(8,128)(2,1)} %copy-done.3, bf16[1,4,16,16,768]{4,3,2,1,0:T(8,128)(2,1)} %cotan.5, f32[7,7,768]{2,1,0:T(8,128)} %kernel.5), custom_call_target="tpu_custom_call" | custom-call | flops 1 | bytes 1 | tf_op jit(solution)/shard_map/inputs/pallas_call | solution.py:521
  127.9 2.1 %fusion.5 = bf16[4,4,24,768]{3,2,1,0:T(8,128)(2,1)S(1)} fusion(bf16[4,4,24,768]{3,2,1,0:T(8,128)(2,1)} %collective-permute-done.8, bf16[4,4,24,768]{3,2,1,0:T(8,128)(2,1)} %collective-permute-done.7, bf16[4,4,24,768]{3,2,1,0:T(8,128)(2,1)} %collective-permute-done.6, bf16[4,4,4,24,768]{4,3,2,1,0:T(8,128)(2,1)} %collective-permute-done.5, s32[]{:T(128)S(6)} %select_n.96, ...), kind=kLoop, calls=%fused_computation.9 | loop fusion | flops 3538944 | bytes 3538948 | tf_op jit(solution)/shard_map/convert_element_type | solution.py:68
  130.0 2.0 %fusion.2 = bf16[4,4,24,768]{3,2,1,0:T(8,128)(2,1)S(1)} fusion(bf16[4,4,24,768]{3,2,1,0:T(8,128)(2,1)} %collective-permute-done.11, bf16[4,4,24,768]{3,2,1,0:T(8,128)(2,1)} %collective-permute-done.10, bf16[4,4,24,768]{3,2,1,0:T(8,128)(2,1)} %collective-permute-done.9, bf16[4,4,4,24,768]{4,3,2,1,0:T(8,128)(2,1)} %copy-done.1, s32[]{:T(128)S(6)} %select_n.96, ...), kind=kLoop, calls=%fused_computation.5 | loop fusion | flops 3538944 | bytes 3538948 | tf_op jit(solution)/shard_map/convert_element_type | solution.py:68
  133.1 1.9 %all-to-all-done.1 = bf16[128,24,128]{2,1,0:T(8,128)(2,1)S(1)} async-done(((bf16[128,24,128]{2,1,0:T(8,128)(2,1)}), bf16[128,24,128]{2,1,0:T(8,128)(2,1)S(1)}, u32[]{:S(2)}, u32[]{:S(2)}) %all-to-all-start.1) | async-done | bytes 786464 | tf_op jit(solution)/shard_map/all_to_all | solution.py:90
  135.4 5.3 %all-to-all-start.2 = ((bf16[16,48,768]{2,1,0:T(8,128)(2,1)}), bf16[16,48,768]{2,1,0:T(8,128)(2,1)S(1)}, u32[]{:S(2)}, u32[]{:S(2)}) async-start(bf16[16,48,768]{2,1,0:T(8,128)(2,1)} %pad_maximum_fusion), calls=%async_computation.2 | async-start | bytes 2359296 | tf_op jit(solution)/shard_map/all_to_all | solution.py:75
  140.7 6.2 %inputs.3 = f32[1,4,16,16,768]{4,3,2,1,0:T(8,128)} custom-call(s32[1]{0:T(128)S(6)} %copy.17.count, f32[768,768]{1,0:T(8,128)} %get-tuple-element.55.d_filt, bf16[3,3,16,768]{3,2,1,0:T(8,128)(2,1)} %copy-done.2, bf16[3,3,16,768]{3,2,1,0:T(8,128)(2,1)} %copy-done.3, bf16[1,4,16,16,768]{4,3,2,1,0:T(8,128)(2,1)} %cotan.5, ...), custom_call_target="tpu_custom_call", output_to_operand_aliasing={{}: (6, {})} | custom-call | flops 1 | bytes 1 | tf_op jit(solution)/shard_map/inputs/pallas_call | solution.py:521
  148.3 11.3 %all-to-all-done.2 = bf16[16,48,768]{2,1,0:T(8,128)(2,1)S(1)} async-done(((bf16[16,48,768]{2,1,0:T(8,128)(2,1)}), bf16[16,48,768]{2,1,0:T(8,128)(2,1)S(1)}, u32[]{:S(2)}, u32[]{:S(2)}) %all-to-all-start.2) | async-done | bytes 1179680 | tf_op jit(solution)/shard_map/all_to_all | solution.py:75
  (44 shorter events, 11.6 us)
Async XLA Ops:
  1.7 9.5 %collective-permute-start.1 = (bf16[3,3,16,768]{3,2,1,0:T(8,128)(2,1)S(1)}, bf16[3,3,16,768]{3,2,1,0:T(8,128)(2,1)S(1)}, u32[]{:S(2)}, u32[]{:S(2)}) collective-permute-start(bf16[3,3,16,768]{3,2,1,0:T(8,128)(2,1)S(1)} %get-tuple-element.69), channel_id=1, source_target_pairs={{1,0},{2,1},{3,2},{5,4},{6,5},{7,6},{9,8},{10,9},{11,10},{13,12},{... | collective-permute-start | bytes 663560 | tf_op jit(solution)/shard_map/ppermute | solution.py:99
  3.0 9.1 %collective-permute-start = (bf16[3,3,16,768]{3,2,1,0:T(8,128)(2,1)S(1)}, bf16[3,3,16,768]{3,2,1,0:T(8,128)(2,1)S(1)}, u32[]{:S(2)}, u32[]{:S(2)}) collective-permute-start(bf16[3,3,16,768]{3,2,1,0:T(8,128)(2,1)S(1)} %get-tuple-element.70), channel_id=1, source_target_pairs={{0,1},{1,2},{2,3},{4,5},{5,6},{6,7},{8,9},{9,10},{10,11},{12,13},{... | collective-permute-start | bytes 663560 | tf_op jit(solution)/shard_map/ppermute | solution.py:98
  11.2 0.9 copy-start.4
  12.1 0.7 copy-start.5
  63.9 18.1 %collective-permute-start.4 = (bf16[4,4,4,24,768]{4,3,2,1,0:T(8,128)(2,1)}, bf16[4,4,4,24,768]{4,3,2,1,0:T(8,128)(2,1)S(1)}, u32[]{:S(2)}, u32[]{:S(2)}) collective-permute-start(bf16[4,4,4,24,768]{4,3,2,1,0:T(8,128)(2,1)} %get-tuple-element.40), channel_id=1, source_target_pairs={{0,4},{4,0},{8,12},{12,8},{16,20},{20,16},{24,28},{28,24},{32,36},... | collective-permute-start | bytes 7077896 | tf_op jit(solution)/shard_map/ppermute | solution.py:35
  65.6 16.4 %collective-permute-start.5 = (bf16[4,4,4,24,768]{4,3,2,1,0:T(8,128)(2,1)}, bf16[4,4,4,24,768]{4,3,2,1,0:T(8,128)(2,1)}, u32[]{:S(2)}, u32[]{:S(2)}) collective-permute-start(bf16[4,4,4,24,768]{4,3,2,1,0:T(8,128)(2,1)} %get-tuple-element.42), channel_id=1, source_target_pairs={{0,4},{4,0},{8,12},{12,8},{16,20},{20,16},{24,28},{28,24},{32,36},... | collective-permute-start | bytes 7077896 | tf_op jit(solution)/shard_map/ppermute | solution.py:35
  65.7 16.3 %collective-permute-start.2 = (bf16[3,3,16,768]{3,2,1,0:T(8,128)(2,1)}, bf16[3,3,16,768]{3,2,1,0:T(8,128)(2,1)S(1)}, u32[]{:S(2)}, u32[]{:S(2)}) collective-permute-start(bf16[3,3,16,768]{3,2,1,0:T(8,128)(2,1)} %get-tuple-element.37), channel_id=1, source_target_pairs={{0,1},{1,2},{2,3},{4,5},{5,6},{6,7},{8,9},{9,10},{10,11},{12,13},{... | collective-permute-start | bytes 663560 | tf_op jit(solution)/shard_map/ppermute | solution.py:98
  69.8 12.2 %collective-permute-start.3 = (bf16[3,3,16,768]{3,2,1,0:T(8,128)(2,1)}, bf16[3,3,16,768]{3,2,1,0:T(8,128)(2,1)S(1)}, u32[]{:S(2)}, u32[]{:S(2)}) collective-permute-start(bf16[3,3,16,768]{3,2,1,0:T(8,128)(2,1)} %get-tuple-element.38), channel_id=1, source_target_pairs={{1,0},{2,1},{3,2},{5,4},{6,5},{7,6},{9,8},{10,9},{11,10},{13,12},{... | collective-permute-start | bytes 663560 | tf_op jit(solution)/shard_map/ppermute | solution.py:99
  82.0 21.2 %copy-start.2 = (bf16[3,3,16,768]{3,2,1,0:T(8,128)(2,1)}, bf16[3,3,16,768]{3,2,1,0:T(8,128)(2,1)S(1)}, u32[]{:S(2)}) copy-start(bf16[3,3,16,768]{3,2,1,0:T(8,128)(2,1)S(1)} %collective-permute-done.2.above) | copy-start | bytes 663556
  82.0 21.2 %copy-start.3 = (bf16[3,3,16,768]{3,2,1,0:T(8,128)(2,1)}, bf16[3,3,16,768]{3,2,1,0:T(8,128)(2,1)S(1)}, u32[]{:S(2)}) copy-start(bf16[3,3,16,768]{3,2,1,0:T(8,128)(2,1)S(1)} %collective-permute-done.3.below) | copy-start | bytes 663556
  82.0 1.5 copy-start.1
  83.5 16.7 %copy-start = (bf16[4,4,4,24,768]{4,3,2,1,0:T(8,128)(2,1)S(1)}, bf16[4,4,4,24,768]{4,3,2,1,0:T(8,128)(2,1)}, u32[]{:S(2)}) copy-start(bf16[4,4,4,24,768]{4,3,2,1,0:T(8,128)(2,1)} %get-tuple-element.45) | copy-start | bytes 7077892
  87.1 17.3 %collective-permute-start.6 = (bf16[4,4,24,768]{3,2,1,0:T(8,128)(2,1)}, bf16[4,4,24,768]{3,2,1,0:T(8,128)(2,1)}, u32[]{:S(2)}, u32[]{:S(2)}) collective-permute-start(bf16[4,4,24,768]{3,2,1,0:T(8,128)(2,1)} %get-tuple-element.63), channel_id=1, source_target_pairs={{0,1},{4,12},{1,2},{5,13},{2,3},{6,14},{3,0},{7,15},{8,9},{12,20},... | collective-permute-start | bytes 1769480 | tf_op jit(solution)/shard_map/ppermute | solution.py:61
  88.3 39.5 %collective-permute-start.7 = (bf16[4,4,24,768]{3,2,1,0:T(8,128)(2,1)}, bf16[4,4,24,768]{3,2,1,0:T(8,128)(2,1)}, u32[]{:S(2)}, u32[]{:S(2)}) collective-permute-start(bf16[4,4,24,768]{3,2,1,0:T(8,128)(2,1)} %get-tuple-element.65), channel_id=1, source_target_pairs={{0,2},{4,20},{1,3},{5,21},{2,0},{6,22},{3,1},{7,23},{8,10},{12,28}... | collective-permute-start | bytes 1769480 | tf_op jit(solution)/shard_map/ppermute | solution.py:61
  90.8 37.1 %collective-permute-start.8 = (bf16[4,4,24,768]{3,2,1,0:T(8,128)(2,1)}, bf16[4,4,24,768]{3,2,1,0:T(8,128)(2,1)}, u32[]{:S(2)}, u32[]{:S(2)}) collective-permute-start(bf16[4,4,24,768]{3,2,1,0:T(8,128)(2,1)} %get-tuple-element.64), channel_id=1, source_target_pairs={{0,3},{4,28},{1,0},{5,29},{2,1},{6,30},{3,2},{7,31},{8,11},{12,4},... | collective-permute-start | bytes 1769480 | tf_op jit(solution)/shard_map/ppermute | solution.py:61
  91.9 15.4 %all-to-all-start = ((bf16[16,8,768]{2,1,0:T(8,128)(2,1)}), bf16[16,8,768]{2,1,0:T(8,128)(2,1)S(1)}, u32[]{:S(2)}, u32[]{:S(2)}) async-start(bf16[16,8,768]{2,1,0:T(8,128)(2,1)} %taps.1), calls=%async_computation | async-start | bytes 393216 | tf_op jit(solution)/shard_map/all_to_all | solution.py:75
  103.2 26.8 %collective-permute-start.9 = (bf16[4,4,24,768]{3,2,1,0:T(8,128)(2,1)}, bf16[4,4,24,768]{3,2,1,0:T(8,128)(2,1)}, u32[]{:S(2)}, u32[]{:S(2)}) collective-permute-start(bf16[4,4,24,768]{3,2,1,0:T(8,128)(2,1)} %get-tuple-element.66), channel_id=1, source_target_pairs={{0,1},{4,12},{1,2},{5,13},{2,3},{6,14},{3,0},{7,15},{8,9},{12,20},... | collective-permute-start | bytes 1769480 | tf_op jit(solution)/shard_map/ppermute | solution.py:61
  103.5 26.5 %collective-permute-start.10 = (bf16[4,4,24,768]{3,2,1,0:T(8,128)(2,1)}, bf16[4,4,24,768]{3,2,1,0:T(8,128)(2,1)}, u32[]{:S(2)}, u32[]{:S(2)}) collective-permute-start(bf16[4,4,24,768]{3,2,1,0:T(8,128)(2,1)} %get-tuple-element.68), channel_id=1, source_target_pairs={{0,2},{4,20},{1,3},{5,21},{2,0},{6,22},{3,1},{7,23},{8,10},{12,28}... | collective-permute-start | bytes 1769480 | tf_op jit(solution)/shard_map/ppermute | solution.py:61
  104.4 25.6 %collective-permute-start.11 = (bf16[4,4,24,768]{3,2,1,0:T(8,128)(2,1)}, bf16[4,4,24,768]{3,2,1,0:T(8,128)(2,1)}, u32[]{:S(2)}, u32[]{:S(2)}) collective-permute-start(bf16[4,4,24,768]{3,2,1,0:T(8,128)(2,1)} %get-tuple-element.67), channel_id=1, source_target_pairs={{0,3},{4,28},{1,0},{5,29},{2,1},{6,30},{3,2},{7,31},{8,11},{12,4},... | collective-permute-start | bytes 1769480 | tf_op jit(solution)/shard_map/ppermute | solution.py:61
  108.4 26.6 %all-to-all-start.1 = ((bf16[128,24,128]{2,1,0:T(8,128)(2,1)}), bf16[128,24,128]{2,1,0:T(8,128)(2,1)S(1)}, u32[]{:S(2)}, u32[]{:S(2)}) async-start(bf16[128,24,128]{2,1,0:T(8,128)(2,1)} %broadcast_in_dim.16), calls=%async_computation.1 | async-start | bytes 1572864 | tf_op jit(solution)/shard_map/all_to_all | solution.py:90
  135.4 24.2 %all-to-all-start.2 = ((bf16[16,48,768]{2,1,0:T(8,128)(2,1)}), bf16[16,48,768]{2,1,0:T(8,128)(2,1)S(1)}, u32[]{:S(2)}, u32[]{:S(2)}) async-start(bf16[16,48,768]{2,1,0:T(8,128)(2,1)} %pad_maximum_fusion), calls=%async_computation.2 | async-start | bytes 2359296 | tf_op jit(solution)/shard_map/all_to_all | solution.py:75
